TPU v7x, 32 devices: a whole 2x2x4 slice. The times are simulated.
32 devices in a mesh: irrep: 4 (over y, x), edge: 8 (over z, core).
Axes of the slice: x: 2, y: 2, z: 4, core: 2. Of those that a mesh axis runs over, the one named last changes fastest.
Arguments:
- edge_vec: float32 [3, 16384], P(None, ('irrep', 'edge')), may hold values from -4.8 to 4.8, as said below
- edge_live: int32 [16384], P(('irrep', 'edge')), may hold values from 0 to 1, as said below
- source: int32 [16384], P(('irrep', 'edge')), may hold values from 0 to 511
- target: int32 [16384], P(('irrep', 'edge')), may hold values from 0 to 511
- species: int32 [512], replicated, may hold values from 0 to 3
- force_label: float32 [3, 512], P(None, ('irrep', 'edge')), may hold values from -6 to 6
- force_mask: int32 [512], P(('irrep', 'edge')), may hold values 0 or 1
- block_owner: int32 [256], replicated, may hold values from 0 to 255, each once
- pair_in_weight: float32 [16, 1024], replicated, may hold values from -1.5 to 1.5
- pair_in_first: float32 [16, 1024], replicated, may hold values from -0.00061035156 to 0.00061035156
- pair_in_second: float32 [16, 1024], replicated, may hold values from 1e-08 to 4e-08
- pair_out_weight: float32 [1024, 1024], replicated, may hold values from -0.1875 to 0.1875
- pair_out_first: float32 [1024, 1024], replicated, may hold values from -0.00061035156 to 0.00061035156
- pair_out_second: float32 [1024, 1024], replicated, may hold values from 1e-08 to 4e-08
- env_weight: float32 [2, 64, 1024], replicated, may hold values from -0.1875 to 0.1875
- env_first: float32 [2, 64, 1024], replicated, may hold values from -0.00061035156 to 0.00061035156
- env_second: float32 [2, 64, 1024], replicated, may hold values from 1e-08 to 4e-08
- scalar_weight: float32 [2, 64, 1024], replicated, may hold values from -0.75 to 0.75
- scalar_first: float32 [2, 64, 1024], replicated, may hold values from -0.00061035156 to 0.00061035156
- scalar_second: float32 [2, 64, 1024], replicated, may hold values from 1e-08 to 4e-08
- mix_weight: float32 [1, 3, 64, 64], replicated, may hold values from -0.75 to 0.75
- mix_first: float32 [1, 3, 64, 64], replicated, may hold values from -0.00061035156 to 0.00061035156
- mix_second: float32 [1, 3, 64, 64], replicated, may hold values from 1e-08 to 4e-08
- energy_head: float32 [1028], replicated, may hold values from -1 to 2, as said below
- head_first: float32 [1028], replicated, may hold values from -0.00061035156 to 0.00061035156
- head_second: float32 [1028], replicated, may hold values from 1e-08 to 4e-08
- soap_weight: float32 [256, 128, 128], P(('irrep', 'edge')), may hold values from -0.1875 to 0.1875
- soap_first: float32 [256, 128, 128], P(('irrep', 'edge')), may hold values from -0.00061035156 to 0.00061035156
- soap_second: float32 [256, 128, 128], P(('irrep', 'edge')), may hold values from 1e-08 to 4e-08
- soap_left: float32 [256, 128, 128], P(('irrep', 'edge')), may hold values from -1 to 1, as said below
- soap_right: float32 [256, 128, 128], P(('irrep', 'edge')), may hold values from -1 to 1, as said below
- soap_lstat: float32 [256, 128, 128], P(('irrep', 'edge')), may hold values from -1 to 1, as said below
- soap_rstat: float32 [256, 128, 128], P(('irrep', 'edge')), may hold values from -1 to 1, as said below
- soap_average: float32 [256, 128, 128], P(('irrep', 'edge')), may hold values from -0.1875 to 0.1875
Outputs:
- loss_sum: float32 [], replicated
- label_count: float32 [], replicated
- new_pair_in_weight: float32 [16, 1024], replicated
- new_pair_in_first: float32 [16, 1024], replicated
- new_pair_in_second: float32 [16, 1024], replicated
- new_pair_out_weight: float32 [1024, 1024], replicated
- new_pair_out_first: float32 [1024, 1024], replicated
- new_pair_out_second: float32 [1024, 1024], replicated
- new_env_weight: float32 [2, 64, 1024], replicated
- new_env_first: float32 [2, 64, 1024], replicated
- new_env_second: float32 [2, 64, 1024], replicated
- new_scalar_weight: float32 [2, 64, 1024], replicated
- new_scalar_first: float32 [2, 64, 1024], replicated
- new_scalar_second: float32 [2, 64, 1024], replicated
- new_mix_weight: float32 [1, 3, 64, 64], replicated
- new_mix_first: float32 [1, 3, 64, 64], replicated
- new_mix_second: float32 [1, 3, 64, 64], replicated
- new_energy_head: float32 [1028], replicated
- new_head_first: float32 [1028], replicated
- new_head_second: float32 [1028], replicated
- new_soap_weight: float32 [256, 128, 128], P(('irrep', 'edge'))
- new_soap_first: float32 [256, 128, 128], P(('irrep', 'edge'))
- new_soap_second: float32 [256, 128, 128], P(('irrep', 'edge'))
- new_soap_left: float32 [256, 128, 128], P(('irrep', 'edge'))
- new_soap_right: float32 [256, 128, 128], P(('irrep', 'edge'))
- new_soap_lstat: float32 [256, 128, 128], P(('irrep', 'edge'))
- new_soap_rstat: float32 [256, 128, 128], P(('irrep', 'edge'))
- new_soap_average: float32 [256, 128, 128], P(('irrep', 'edge'))
Inputs may be any that keep to these rules, and one draw needn't show every extreme that they name: `edge_vec`: every edge vector has length between 1 and 4.8. `edge_live`: in the 512 slots of each device the used ones come first, at least half are used, and some device uses all. `energy_head`: the first 1024 entries are readout weights, the last 4 are positive species scales. `soap_left`: each block is an orthogonal matrix. `soap_right`: each block is an orthogonal matrix. `soap_lstat`: each block is symmetric with a positive dominant diagonal. `soap_rstat`: each block is symmetric with a positive dominant diagonal.
All inputs are finite; a program needn't handle non-finite values. No bound on the sum of `force_mask` on one device may be relied on, other than what follows from the above.
Results may differ from a plain program's by a relative error of at most 0.0003.
Values sent between devices are 32-bit elements; how exact they have to be, the bound alone decides.
No kernel may reach another device: no remote copies, remote signals or barrier semaphores. Data moves between devices by JAX's collectives and lax.ppermute only.
A program may use at most 448 MiB of HBM per device.

v0:
```python
from functools import partial
import math

import jax
import jax.numpy as jnp
import numpy as np
from jax import lax
from jax.sharding import PartitionSpec as P

D = 1024
NB = 8
SPECIES = 4
LAYERS = 2
BS = 128
NS_STEPS = 4
ADAM_STEP = 10


HIGH = lax.Precision.HIGHEST
CUTOFF = 5.0
ROOT_TWO = math.sqrt(2.0)
ROOT_THREE = math.sqrt(3.0)
ROOT_SIX = math.sqrt(6.0)
HARMONIC = math.sqrt(7.5)
RESIDUAL = 1.0 / math.sqrt(2.0)


def shape_basis():
    return [
        np.array([[0.0, 1, 0], [1, 0, 0], [0, 0, 0]]) / ROOT_TWO,
        np.array([[0.0, 0, 0], [0, 0, 1], [0, 1, 0]]) / ROOT_TWO,
        np.array([[0.0, 0, 1], [0, 0, 0], [1, 0, 0]]) / ROOT_TWO,
        np.array([[1.0, 0, 0], [0, -1, 0], [0, 0, 0]]) / ROOT_TWO,
        np.array([[-1.0, 0, 0], [0, -1, 0], [0, 0, 2]]) / ROOT_SIX,
    ]


def cross_three(left_vec, right_vec):
    return np.array(
        [
            left_vec[1] * right_vec[2] - left_vec[2] * right_vec[1],
            left_vec[2] * right_vec[0] - left_vec[0] * right_vec[2],
            left_vec[0] * right_vec[1] - left_vec[1] * right_vec[0],
        ]
    )


def product_table():
    tensors = shape_basis()
    table = np.zeros((9, 9, 9))
    unit_rows = np.eye(9)
    for first in range(9):
        for second in range(9):
            left = unit_rows[first]
            right = unit_rows[second]
            left_mat = sum((left[4 + slot] * tensors[slot] for slot in range(5)))
            right_mat = sum((right[4 + slot] * tensors[slot] for slot in range(5)))
            left_vec = left[1:4]
            right_vec = right[1:4]
            scalar = left[0] * right[0] + left_vec @ right_vec + np.sum(left_mat * right_mat.T)
            vector = (
                left[0] * right_vec
                + right[0] * left_vec
                + cross_three(left_vec, right_vec)
                + left_mat @ right_vec
                + right_mat @ left_vec
            )
            matrix = (
                left[0] * right_mat
                + right[0] * left_mat
                + (np.outer(left_vec, right_vec) + np.outer(right_vec, left_vec)) / 2
                + (left_mat @ right_mat + right_mat @ left_mat) / 2
            )
            table[first, second, 0] = scalar
            table[first, second, 1:4] = vector
            for slot in range(5):
                table[first, second, 4 + slot] = np.sum(tensors[slot] * matrix)
    return (table / 3.0).astype(np.float32)


def contract_last(left, right):
    return lax.dot_general(left, right, (((1,), (1,)), ((), ())), precision=HIGH)


def contract_first(left, right):
    return lax.dot_general(left, right, (((0,), (0,)), ((), ())), precision=HIGH)


def geometry_piece(params, inputs, live_edges, onehot_source, onehot_target):
    pair_in, pair_out = params
    vectors = inputs[0]
    distance = jnp.sqrt(jnp.sum(vectors * vectors, axis=0))
    unit_x = vectors[0] / distance
    unit_y = vectors[1] / distance
    unit_z = vectors[2] / distance
    ratio = distance / CUTOFF
    envelope = (1.0 - 28.0 * ratio**6 + 48.0 * ratio**7 - 21.0 * ratio**8) * live_edges
    orders = jnp.arange(1, NB + 1).astype(jnp.float32)[:, None]
    bessel = (
        math.sqrt(2.0 / CUTOFF)
        * jnp.sin(orders * (math.pi / CUTOFF) * distance[None])
        / distance[None]
    )
    features = jnp.concatenate([bessel, onehot_source, onehot_target], axis=0)
    hidden = jax.nn.silu(contract_first(features, pair_in))
    latent = envelope[:, None] * jnp.dot(hidden, pair_out, precision=HIGH)
    harmonics = jnp.stack(
        [
            jnp.ones_like(unit_x),
            ROOT_THREE * unit_x,
            ROOT_THREE * unit_y,
            ROOT_THREE * unit_z,
            HARMONIC * ROOT_TWO * unit_x * unit_y,
            HARMONIC * ROOT_TWO * unit_y * unit_z,
            HARMONIC * ROOT_TWO * unit_x * unit_z,
            HARMONIC * (unit_x * unit_x - unit_y * unit_y) / ROOT_TWO,
            HARMONIC * (2.0 * unit_z * unit_z - unit_x * unit_x - unit_y * unit_y) / ROOT_SIX,
        ]
    )
    return (harmonics, envelope, latent)


def mix_blocks(mixing, tensor):
    return jnp.concatenate(
        [
            jnp.einsum("cd,kde->kce", mixing[0], tensor[0:1], precision=HIGH),
            jnp.einsum("cd,kde->kce", mixing[1], tensor[1:4], precision=HIGH),
            jnp.einsum("cd,kde->kce", mixing[2], tensor[4:9], precision=HIGH),
        ],
        axis=0,
    )


def embed_piece(params, inputs):
    embedded = inputs[1][:, None, :] * contract_last(params[0], inputs[0])[None]
    if len(inputs) == 2:
        return (embedded,)
    return (jnp.concatenate([embedded, mix_blocks(params[1], inputs[2])], axis=0),)


def product_piece(params, inputs, width):
    environ, feature = inputs
    table = jnp.asarray(product_table()[:, :, :width])
    summed = feature[0][None] * jnp.einsum("bk,bce->kce", table[0], environ, precision=HIGH)
    for first in range(1, 9):
        summed = summed + feature[first][None] * jnp.einsum(
            "bk,bce->kce", table[first], environ, precision=HIGH
        )
    return (summed,)


def update_piece(params, inputs):
    x_in, scal_in, second_w = params
    latent, previous, envelope = inputs
    preact = jnp.dot(latent, x_in, precision=HIGH) + contract_first(previous[0], scal_in)
    return (
        (latent + envelope[:, None] * jnp.dot(jax.nn.silu(preact), second_w, precision=HIGH))
        * RESIDUAL,
    )


def energy_piece(params, inputs, onehot_source):
    head = params[0]
    latent, envelope = inputs
    per_edge = jnp.dot(latent, head[:D], precision=HIGH)
    factor = jnp.dot(head[D:], onehot_source, precision=HIGH)
    return (jnp.sum(envelope * factor * per_edge),)


def pullback(function, params, inputs, cotangents):
    outputs, backward = jax.vjp(function, params, inputs)
    return backward(cotangents)


def second_pullback(function, params, inputs, cotangents, tangents):

    def backward_of(weights, values, cots):
        return pullback(function, weights, values, cots)[1]

    outputs, backward = jax.vjp(backward_of, params, inputs, cotangents)
    return backward(tangents)


def add_trees(first, second):
    return jax.tree.map(jnp.add, first, second)


def to_group(tensor):
    return lax.all_to_all(tensor, "irrep", split_axis=1, concat_axis=2, tiled=True)


def to_rows(tensor):
    return lax.all_to_all(tensor, "irrep", split_axis=2, concat_axis=1, tiled=True)


def environ_op(tensor, row_source, atoms, scale):
    partial_sum = (
        jnp.zeros(tensor.shape[:2] + (atoms,), jnp.float32).at[:, :, row_source].add(tensor)
    )
    summed = lax.psum(partial_sum, "edge")
    return summed[:, :, row_source] * scale


def spread(stacked, layer_no, row_source, atoms, scale):
    environ = environ_op(stacked[:9], row_source, atoms, scale)
    feature = stacked[9:] if layer_no else stacked
    return (environ, feature)


def spread_back(environ_cot, feature_cot, layer_no, row_source, atoms, scale):
    embed_cot = environ_op(environ_cot, row_source, atoms, scale)
    if layer_no:
        return jnp.concatenate([embed_cot, feature_cot], axis=0)
    return embed_cot + feature_cot


def to_matrices(blocks):
    side = D // BS
    return (
        blocks.reshape(2 * LAYERS, side, side, BS, BS)
        .transpose(0, 1, 3, 2, 4)
        .reshape(2 * LAYERS, D, D)
    )


def to_blocks(matrices):
    side = D // BS
    return (
        matrices.reshape(2 * LAYERS, side, BS, side, BS)
        .transpose(0, 1, 3, 2, 4)
        .reshape(2 * LAYERS * side * side, BS, BS)
    )


def adamw(weight, first, second, grad):
    first_new = 0.9 * first + 0.1 * grad
    second_new = 0.99 * second + 0.01 * grad * grad
    normal = (
        first_new
        / (1.0 - 0.9**ADAM_STEP)
        / (jnp.sqrt(second_new / (1.0 - 0.99**ADAM_STEP)) + 1e-08)
    )
    return (weight - 0.01 * (normal + 0.01 * weight), first_new, second_new)


def orthogonalize(matrix):
    current = matrix / jnp.sqrt(jnp.sum(matrix * matrix))
    for step_no in range(NS_STEPS):
        current = 1.5 * current - 0.5 * jnp.dot(
            jnp.dot(current, current.T, precision=HIGH), current, precision=HIGH
        )
    return current


def soap_slot(grad, weight, first, second, left, right, lstat, rstat, average):
    rotated = jnp.dot(jnp.dot(left.T, grad, precision=HIGH), right, precision=HIGH)
    first_new = 0.9 * first + 0.1 * rotated
    second_new = 0.99 * second + 0.01 * rotated * rotated
    normal = (
        first_new
        / (1.0 - 0.9**ADAM_STEP)
        / (jnp.sqrt(second_new / (1.0 - 0.99**ADAM_STEP)) + 1e-08)
    )
    weight_new = weight - 0.01 * (
        jnp.dot(jnp.dot(left, normal, precision=HIGH), right.T, precision=HIGH) + 0.01 * weight
    )
    lstat_new = 0.95 * lstat + 0.05 * jnp.dot(grad, grad.T, precision=HIGH)
    rstat_new = 0.95 * rstat + 0.05 * jnp.dot(grad.T, grad, precision=HIGH)
    left_new = orthogonalize(jnp.dot(lstat_new, left, precision=HIGH))
    right_new = orthogonalize(jnp.dot(rstat_new, right, precision=HIGH))
    plain = jnp.dot(jnp.dot(left, first_new, precision=HIGH), right.T, precision=HIGH)
    first_out = jnp.dot(jnp.dot(left_new.T, plain, precision=HIGH), right_new, precision=HIGH)
    average_new = 0.99 * average + 0.01 * weight_new
    return (
        weight_new,
        first_out,
        second_new,
        left_new,
        right_new,
        lstat_new,
        rstat_new,
        average_new,
    )


def local(
    edge_vec,
    edge_live,
    source,
    target,
    species,
    force_label,
    force_mask,
    block_owner,
    pair_in_weight,
    pair_in_first,
    pair_in_second,
    pair_out_weight,
    pair_out_first,
    pair_out_second,
    env_weight,
    env_first,
    env_second,
    scalar_weight,
    scalar_first,
    scalar_second,
    mix_weight,
    mix_first,
    mix_second,
    energy_head,
    head_first,
    head_second,
    soap_weight,
    soap_first,
    soap_second,
    soap_left,
    soap_right,
    soap_lstat,
    soap_rstat,
    soap_average,
):
    slots = lax.all_gather(soap_weight, ("irrep", "edge"), axis=0, tiled=True)
    matrices = to_matrices(jnp.zeros_like(slots).at[block_owner].set(slots))
    row_source = lax.all_gather(source, "irrep", axis=0, tiled=True)
    atoms = force_label.shape[1] * lax.axis_size("irrep") * lax.axis_size("edge")
    scale = math.sqrt(force_label.shape[1] / edge_vec.shape[1])
    live_edges = edge_live.astype(jnp.float32)
    kinds = jnp.arange(SPECIES, dtype=jnp.int32)[:, None]
    onehot_source = (species[source][None, :] == kinds).astype(jnp.float32)
    onehot_target = (species[target][None, :] == kinds).astype(jnp.float32)
    geometry_fn = partial(
        geometry_piece,
        live_edges=live_edges,
        onehot_source=onehot_source,
        onehot_target=onehot_target,
    )
    energy_fn = partial(energy_piece, onehot_source=onehot_source)
    product_fns = [
        partial(product_piece, width=1 if layer_no == LAYERS - 1 else 9)
        for layer_no in range(LAYERS)
    ]
    geo_params = (pair_in_weight, pair_out_weight)
    head_params = (energy_head,)
    embed_params = [(env_weight[0],)] + [(env_weight[1], mix_weight[0])]
    update_params = [
        (matrices[2 * layer_no], scalar_weight[layer_no], matrices[2 * layer_no + 1])
        for layer_no in range(LAYERS)
    ]
    harmonics, envelope, latent = geometry_fn(geo_params, (edge_vec,))
    embed_inputs, product_inputs, update_inputs = ([], [], [])
    previous = None
    for layer_no in range(LAYERS):
        inputs = (latent, harmonics) if layer_no == 0 else (latent, harmonics, previous)
        embed_inputs.append(inputs)
        stacked = embed_piece(embed_params[layer_no], inputs)[0]
        environ, feature = spread(to_group(stacked), layer_no, row_source, atoms, scale)
        product_inputs.append((environ, feature))
        previous = to_rows(product_fns[layer_no]((), (environ, feature))[0])
        update_inputs.append((latent, previous, envelope))
        latent = update_piece(update_params[layer_no], update_inputs[layer_no])[0]
    unit_cot = jnp.ones((), jnp.float32)
    latent_cot, envelope_cot = pullback(energy_fn, head_params, (latent, envelope), (unit_cot,))[1]
    harmonics_cot = jnp.zeros_like(harmonics)
    update_cots, product_cots, embed_cots = ([None] * LAYERS, [None] * LAYERS, [None] * LAYERS)
    carried = None
    for layer_no in reversed(range(LAYERS)):
        update_cots[layer_no] = (latent_cot,)
        latent_part, previous_cot, envelope_part = pullback(
            update_piece, update_params[layer_no], update_inputs[layer_no], (latent_cot,)
        )[1]
        envelope_cot = envelope_cot + envelope_part
        if carried is not None:
            previous_cot = previous_cot + carried
        product_cots[layer_no] = (to_group(previous_cot),)
        environ_cot, feature_cot = pullback(
            product_fns[layer_no], (), product_inputs[layer_no], product_cots[layer_no]
        )[1]
        embed_cots[layer_no] = (
            to_rows(spread_back(environ_cot, feature_cot, layer_no, row_source, atoms, scale)),
        )
        inputs_cot = pullback(
            embed_piece, embed_params[layer_no], embed_inputs[layer_no], embed_cots[layer_no]
        )[1]
        latent_cot = latent_part + inputs_cot[0]
        harmonics_cot = harmonics_cot + inputs_cot[1]
        carried = inputs_cot[2] if layer_no else None
    geo_cot = (harmonics_cot, envelope_cot, latent_cot)
    vec_grad = pullback(geometry_fn, geo_params, (edge_vec,), geo_cot)[1][0]
    partial_force = (
        jnp.zeros((3, atoms), jnp.float32).at[:, source].add(vec_grad).at[:, target].add(-vec_grad)
    )
    force = lax.psum_scatter(partial_force, ("irrep", "edge"), scatter_dimension=1, tiled=True)
    label_mask = force_mask.astype(jnp.float32)
    label_total = lax.psum(jnp.sum(label_mask), ("irrep", "edge"))
    residual = force - force_label
    loss_local = jnp.sum(label_mask[None] * residual * residual)
    force_cot = 2.0 * label_mask[None] * residual / label_total
    every_cot = lax.all_gather(force_cot, ("irrep", "edge"), axis=1, tiled=True)
    vec_tangent = every_cot[:, source] - every_cot[:, target]
    geo_grad, unused_hat, tangents = second_pullback(
        geometry_fn, geo_params, (edge_vec,), geo_cot, (vec_tangent,)
    )
    harmonics_dot, envelope_dot, latent_dot = tangents
    embed_grads, update_grads = ([None] * LAYERS, [None] * LAYERS)
    embed_hats, product_hats, update_hats = ([None] * LAYERS, [None] * LAYERS, [None] * LAYERS)
    previous_dot = None
    for layer_no in range(LAYERS):
        tangent_in = (
            (latent_dot, harmonics_dot)
            if layer_no == 0
            else (latent_dot, harmonics_dot, previous_dot)
        )
        embed_grads[layer_no], embed_hats[layer_no], stacked_dot = second_pullback(
            embed_piece,
            embed_params[layer_no],
            embed_inputs[layer_no],
            embed_cots[layer_no],
            tangent_in,
        )
        environ_dot, feature_dot = spread(
            to_group(stacked_dot[0]), layer_no, row_source, atoms, scale
        )
        unused_grad, product_hats[layer_no], result_dot = second_pullback(
            product_fns[layer_no],
            (),
            product_inputs[layer_no],
            product_cots[layer_no],
            (environ_dot, feature_dot),
        )
        previous_dot = to_rows(result_dot[0])
        update_grads[layer_no], update_hats[layer_no], latent_next = second_pullback(
            update_piece,
            update_params[layer_no],
            update_inputs[layer_no],
            update_cots[layer_no],
            (latent_dot, previous_dot, envelope_dot),
        )
        latent_dot = latent_next[0]
    head_grad, final_hats, unused_dot = second_pullback(
        energy_fn, head_params, (latent, envelope), (unit_cot,), (latent_dot, envelope_dot)
    )
    latent_hat, envelope_hat = final_hats
    harmonics_hat = jnp.zeros_like(harmonics)
    carried = None
    for layer_no in reversed(range(LAYERS)):
        param_cot, inputs_cot = pullback(
            update_piece, update_params[layer_no], update_inputs[layer_no], (latent_hat,)
        )
        update_grads[layer_no] = add_trees(update_grads[layer_no], param_cot)
        latent_part, previous_hat, envelope_part = add_trees(inputs_cot, update_hats[layer_no])
        envelope_hat = envelope_hat + envelope_part
        if carried is not None:
            previous_hat = previous_hat + carried
        environ_hat, feature_hat = pullback(
            product_fns[layer_no], (), product_inputs[layer_no], (to_group(previous_hat),)
        )[1]
        environ_hat = environ_hat + product_hats[layer_no][0]
        feature_hat = feature_hat + product_hats[layer_no][1]
        stacked_hat = to_rows(
            spread_back(environ_hat, feature_hat, layer_no, row_source, atoms, scale)
        )
        param_cot, inputs_cot = pullback(
            embed_piece, embed_params[layer_no], embed_inputs[layer_no], (stacked_hat,)
        )
        embed_grads[layer_no] = add_trees(embed_grads[layer_no], param_cot)
        inputs_cot = add_trees(inputs_cot, embed_hats[layer_no])
        latent_hat = latent_part + inputs_cot[0]
        harmonics_hat = harmonics_hat + inputs_cot[1]
        carried = inputs_cot[2] if layer_no else None
    geo_grad = add_trees(
        geo_grad,
        pullback(geometry_fn, geo_params, (edge_vec,), (harmonics_hat, envelope_hat, latent_hat))[
            0
        ],
    )
    env_grad = jnp.stack([embed_grads[layer_no][0] for layer_no in range(LAYERS)])
    mix_grad = jnp.stack([embed_grads[1][1]])
    scalar_grad = jnp.stack([update_grads[layer_no][1] for layer_no in range(LAYERS)])
    matrix_grad = jnp.stack(
        [
            update_grads[layer_no // 2][0 if layer_no % 2 == 0 else 2]
            for layer_no in range(2 * LAYERS)
        ]
    )
    pair_in_grad, pair_out_grad, env_grad, scalar_grad, mix_grad, head_total, loss_sum = lax.psum(
        (geo_grad[0], geo_grad[1], env_grad, scalar_grad, mix_grad, head_grad[0], loss_local),
        ("irrep", "edge"),
    )
    slot_grads = to_blocks(matrix_grad)[block_owner]
    own_grads = lax.psum_scatter(slot_grads, ("irrep", "edge"), scatter_dimension=0, tiled=True)
    new_pair_in = adamw(pair_in_weight, pair_in_first, pair_in_second, pair_in_grad)
    new_pair_out = adamw(pair_out_weight, pair_out_first, pair_out_second, pair_out_grad)
    new_env = adamw(env_weight, env_first, env_second, env_grad)
    new_scalar = adamw(scalar_weight, scalar_first, scalar_second, scalar_grad)
    new_mix = adamw(mix_weight, mix_first, mix_second, mix_grad)
    new_head = adamw(energy_head, head_first, head_second, head_total)
    soap = jax.vmap(soap_slot)(
        own_grads,
        soap_weight,
        soap_first,
        soap_second,
        soap_left,
        soap_right,
        soap_lstat,
        soap_rstat,
        soap_average,
    )
    return (
        loss_sum,
        label_total,
        new_pair_in[0],
        new_pair_in[1],
        new_pair_in[2],
        new_pair_out[0],
        new_pair_out[1],
        new_pair_out[2],
        new_env[0],
        new_env[1],
        new_env[2],
        new_scalar[0],
        new_scalar[1],
        new_scalar[2],
        new_mix[0],
        new_mix[1],
        new_mix[2],
        new_head[0],
        new_head[1],
        new_head[2],
        soap[0],
        soap[1],
        soap[2],
        soap[3],
        soap[4],
        soap[5],
        soap[6],
        soap[7],
    )


def solution(mesh):
    placed = (
        P(None, ("irrep", "edge")),
        P(("irrep", "edge")),
        P(("irrep", "edge")),
        P(("irrep", "edge")),
        P(),
        P(None, ("irrep", "edge")),
        P(("irrep", "edge")),
        P(),
        P(),
        P(),
        P(),
        P(),
        P(),
        P(),
        P(),
        P(),
        P(),
        P(),
        P(),
        P(),
        P(),
        P(),
        P(),
        P(),
        P(),
        P(),
        P(("irrep", "edge"), None, None),
        P(("irrep", "edge"), None, None),
        P(("irrep", "edge"), None, None),
        P(("irrep", "edge"), None, None),
        P(("irrep", "edge"), None, None),
        P(("irrep", "edge"), None, None),
        P(("irrep", "edge"), None, None),
        P(("irrep", "edge"), None, None),
    )
    return jax.shard_map(
        local,
        mesh=mesh,
        in_specs=placed,
        out_specs=(
            P(),
            P(),
            P(),
            P(),
            P(),
            P(),
            P(),
            P(),
            P(),
            P(),
            P(),
            P(),
            P(),
            P(),
            P(),
            P(),
            P(),
            P(),
            P(),
            P(),
            P(("irrep", "edge"), None, None),
            P(("irrep", "edge"), None, None),
            P(("irrep", "edge"), None, None),
            P(("irrep", "edge"), None, None),
            P(("irrep", "edge"), None, None),
            P(("irrep", "edge"), None, None),
            P(("irrep", "edge"), None, None),
            P(("irrep", "edge"), None, None),
        ),
        check_vma=False,
    )
```

profile of v0, /device:TPU:0, one launch (start us, length us, event | category | flops | bytes accessed | tf_op | source)
XLA Modules:
  0.0 5365.4 jit_solution(8455498700464869848)
XLA Ops:
  42.0 28.9 all-gather
  91.5 248.0 %scatter_fusion.1 = f32[9,16,512]{1,0,2:T(8,128)} fusion(f32[9,16,512]{1,0,2:T(8,128)} %broadcast.567.clone, s32[2048]{0:T(1024)S(1)} %get-tuple-element.272, f32[2048,9,16]{2,1,0:T(8,128)} %copy.2123), kind=kCustom, calls=%fused_computation.14 | custom fusion | flops 294912 | bytes 3547136 | tf_op jit(solution)/shard_map/scatter-add | solution.py:198
  346.7 159.6 %all-reduce.87.cloned.1.call-done = f32[9,16,512]{1,0,2:T(8,128)} async-done(((f32[9,16,512]{1,0,2:T(8,128)}), f32[9,16,512]{1,0,2:T(8,128)}) %all-reduce.87.cloned.1.call-update) | async-done | bytes 294928 | tf_op jit(solution)/shard_map/psum | solution.py:200
  506.3 21.1 gather_fusion.2
  638.5 25.7 reshape.1673
  691.6 45.7 scatter_fusion
  795.4 34.4 all-to-all-done.2
  847.7 248.0 %scatter_fusion.2 = f32[9,16,512]{1,0,2:T(8,128)} fusion(f32[9,16,512]{1,0,2:T(8,128)} %broadcast.567.clone.1, s32[2048]{0:T(1024)S(1)} %get-tuple-element.272, f32[2048,9,16]{2,1,0:T(8,128)} %bitcast.1468), kind=kCustom, calls=%fused_computation.15 | custom fusion | flops 294912 | bytes 3547136 | tf_op jit(solution)/shard_map/scatter-add | solution.py:198
  1103.6 88.3 %all-reduce.89.cloned.1.call-done = f32[9,16,512]{1,0,2:T(8,128)} async-done(((f32[9,16,512]{1,0,2:T(8,128)}), f32[9,16,512]{1,0,2:T(8,128)}) %all-reduce.89.cloned.1.call-update) | async-done | bytes 294928 | tf_op jit(solution)/shard_map/psum | solution.py:200
  1333.1 248.0 %scatter_fusion.3 = f32[9,16,512]{1,0,2:T(8,128)} fusion(f32[9,16,512]{1,0,2:T(8,128)} %broadcast.567.clone.2, s32[2048]{0:T(1024)S(1)} %get-tuple-element.272, f32[2048,9,16]{2,1,0:T(8,128)} %copy.2158), kind=kCustom, calls=%fused_computation.16 | custom fusion | flops 294912 | bytes 3547136 | tf_op jit(solution)/shard_map/scatter-add | solution.py:198
  1584.4 92.0 %all-reduce.91.cloned.1.call-done = f32[9,16,512]{1,0,2:T(8,128)} async-done(((f32[9,16,512]{1,0,2:T(8,128)}), f32[9,16,512]{1,0,2:T(8,128)}) %all-reduce.91.cloned.1.call-update) | async-done | bytes 294928 | tf_op jit(solution)/shard_map/psum | solution.py:200
  1786.5 27.1 reshape.1677
  1953.5 248.0 %scatter_fusion.4 = f32[9,16,512]{1,0,2:T(8,128)} fusion(f32[9,16,512]{1,0,2:T(8,128)} %broadcast.567.clone.3, s32[2048]{0:T(1024)S(1)} %get-tuple-element.272, f32[2048,9,16]{2,1,0:T(8,128)} %copy.2193), kind=kCustom, calls=%fused_computation.17 | custom fusion | flops 294912 | bytes 3547136 | tf_op jit(solution)/shard_map/scatter-add | solution.py:198
  2213.0 84.5 %all-reduce.93.cloned.1.call-done = f32[9,16,512]{1,0,2:T(8,128)} async-done(((f32[9,16,512]{1,0,2:T(8,128)}), f32[9,16,512]{1,0,2:T(8,128)}) %all-reduce.93.cloned.1.call-update) | async-done | bytes 294928 | tf_op jit(solution)/shard_map/psum | solution.py:200
  2297.5 21.1 gather_fusion.5
  2437.2 41.0 psum.117
  2481.6 88.7 %reduce-scatter.3.cloned.1.call-done = f32[3,16]{0,1:T(8,128)} async-done(((f32[3,512]{0,1:T(8,128)}), f32[3,16]{0,1:T(8,128)}) %reduce-scatter.3.cloned.1.call-update) | async-done | bytes 208 | tf_op jit(solution)/shard_map/reduce_scatter | solution.py:392
  2574.3 39.5 all-gather.1
  2730.1 248.0 %scatter_fusion.6 = f32[9,16,512]{1,0,2:T(8,128)} fusion(f32[9,16,512]{1,0,2:T(8,128)} %broadcast.567.clone.5, s32[2048]{0:T(1024)S(1)} %get-tuple-element.272, f32[2048,9,16]{2,1,0:T(8,128)} %copy.2216), kind=kCustom, calls=%fused_computation.20 | custom fusion | flops 294912 | bytes 3547136 | tf_op jit(solution)/shard_map/scatter-add | solution.py:198
  3037.6 35.8 all-reduce.95.cloned.1.call-done
  3073.4 21.1 gather_fusion.8
  3204.7 24.4 reshape.1681
  3356.6 248.0 %scatter_fusion.7 = f32[9,16,512]{1,0,2:T(8,128)} fusion(f32[9,16,512]{1,0,2:T(8,128)} %broadcast.567.clone.4, s32[2048]{0:T(1024)S(1)} %get-tuple-element.272, f32[2048,9,16]{2,1,0:T(8,128)} %bitcast.1469), kind=kCustom, calls=%fused_computation.21 | custom fusion | flops 294912 | bytes 3547136 | tf_op jit(solution)/shard_map/scatter-add | solution.py:198
  3619.8 82.1 %all-reduce.97.cloned.1.call-done = f32[9,16,512]{1,0,2:T(8,128)} async-done(((f32[9,16,512]{1,0,2:T(8,128)}), f32[9,16,512]{1,0,2:T(8,128)}) %all-reduce.97.cloned.1.call-update) | async-done | bytes 294928 | tf_op jit(solution)/shard_map/psum | solution.py:200
  3880.8 248.0 %scatter_fusion.8 = f32[9,16,512]{1,0,2:T(8,128)} fusion(f32[9,16,512]{1,0,2:T(8,128)} %broadcast.567.clone.6, s32[2048]{0:T(1024)S(1)} %get-tuple-element.272, f32[2048,9,16]{2,1,0:T(8,128)} %copy.2252), kind=kCustom, calls=%fused_computation.22 | custom fusion | flops 294912 | bytes 3547136 | tf_op jit(solution)/shard_map/scatter-add | solution.py:198
  4131.4 93.2 %all-reduce.99.cloned.1.call-done = f32[9,16,512]{1,0,2:T(8,128)} async-done(((f32[9,16,512]{1,0,2:T(8,128)}), f32[9,16,512]{1,0,2:T(8,128)}) %all-reduce.99.cloned.1.call-update) | async-done | bytes 294928 | tf_op jit(solution)/shard_map/psum | solution.py:200
  4338.4 27.1 reshape.1685
  4505.6 248.0 %scatter_fusion.9 = f32[9,16,512]{1,0,2:T(8,128)} fusion(f32[9,16,512]{1,0,2:T(8,128)} %broadcast.567, s32[2048]{0:T(1024)S(1)} %get-tuple-element.272, f32[2048,9,16]{2,1,0:T(8,128)} %copy.2306), kind=kCustom, calls=%fused_computation.23 | custom fusion | flops 294912 | bytes 3547136 | tf_op jit(solution)/shard_map/scatter-add | solution.py:198
  4765.3 84.4 %all-reduce.101.cloned.1.call-done = f32[9,16,512]{1,0,2:T(8,128)} async-done(((f32[9,16,512]{1,0,2:T(8,128)}), f32[9,16,512]{1,0,2:T(8,128)}) %all-reduce.101.cloned.1.call-update) | async-done | bytes 294928 | tf_op jit(solution)/shard_map/psum | solution.py:200
  5063.9 42.6 all-reduce.75
  5108.0 31.4 all-reduce.103.cloned.1.call-done
  5155.0 172.4 %reduce-scatter.5.cloned.1.call-done = f32[8,128,128]{2,1,0:T(8,128)} async-done(((f32[256,128,128]{2,1,0:T(8,128)}), f32[8,128,128]{2,1,0:T(8,128)}) %reduce-scatter.5.cloned.1.call-update) | async-done | bytes 524304 | tf_op jit(solution)/shard_map/reduce_scatter | solution.py:490
  (1668 shorter events, 1945.1 us)
Async XLA Ops:
  8.0 5321.3 %copy-start = (f32[8,128,128]{2,1,0:T(8,128)S(1)}, f32[8,128,128]{2,1,0:T(8,128)}, u32[]{:S(2)}) copy-start(f32[8,128,128]{2,1,0:T(8,128)} %param.72) | copy-start | bytes 1572868
  19.5 775.4 %copy-start.369 = (f32[512]{0:T(512)}, f32[512]{0:T(512)S(1)}, u32[]{:S(2)}) copy-start(f32[512]{0:T(512)S(1)} %get-tuple-element.107) | copy-start | bytes 6148
  32.6 733.4 %copy-start.13 = (f32[512,1024]{1,0:T(8,128)}, f32[512,1024]{1,0:T(8,128)S(1)}, u32[]{:S(2)}) copy-start(f32[512,1024]{1,0:T(8,128)S(1)} %fusion.582) | copy-start | bytes 6291460
  35.1 751.7 %copy-start.191 = (f32[9,512]{1,0:T(8,128)}, f32[9,512]{1,0:T(8,128)S(1)}, u32[]{:S(2)}) copy-start(f32[9,512]{1,0:T(8,128)S(1)} %stack.28) | copy-start | bytes 55300
  36.7 34.2 all-to-all-start
  42.0 464.4 %all-reduce.87.cloned.1.call-start = ((), (), s32[]{:S(2)}) async-start(), calls=%async_computation.19 | async-start | bytes 8388608 | tf_op jit(solution)/shard_map/psum | solution.py:200
  339.5 344.2 %all-gather.4.cloned.1.call-start = ((), (), s32[]{:S(2)}) async-start(), calls=%async_computation.18 | async-start | bytes 17301504 | tf_op jit(solution)/shard_map/all_gather | solution.py:322
  612.2 19.7 all-to-all-start.1
  789.5 40.3 all-to-all-start.2
  794.2 397.8 %all-reduce.89.cloned.1.call-start = ((), (), s32[]{:S(2)}) async-start(), calls=%async_computation.20 | async-start | bytes 8388608 | tf_op jit(solution)/shard_map/psum | solution.py:200
  1265.8 15.0 all-to-all-start.3
  1269.8 406.6 %all-reduce.91.cloned.1.call-start = ((), (), s32[]{:S(2)}) async-start(), calls=%async_computation.21 | async-start | bytes 8388608 | tf_op jit(solution)/shard_map/psum | solution.py:200
  1744.3 32.9 all-to-all-start.5
  1850.0 28.1 all-to-all-start.6
  1853.7 443.7 %all-reduce.93.cloned.1.call-start = ((), (), s32[]{:S(2)}) async-start(), calls=%async_computation.22 | async-start | bytes 8388608 | tf_op jit(solution)/shard_map/psum | solution.py:200
  2349.3 27.2 all-to-all-start.7
  2353.6 216.7 %reduce-scatter.3.cloned.1.call-start = ((), (), s32[]{:S(2)}) async-start(), calls=%async_computation.23 | async-start | bytes 270336 | tf_op jit(solution)/shard_map/reduce_scatter | solution.py:392
  2681.8 29.4 all-to-all-start.8
  2685.5 387.9 %all-reduce.95.cloned.1.call-start = ((), (), s32[]{:S(2)}) async-start(), calls=%async_computation.24 | async-start | bytes 8388608 | tf_op jit(solution)/shard_map/psum | solution.py:200
  2699.4 607.3 %copy-start.254 = (f32[4,16,512]{2,1,0:T(8,128)}, f32[4,16,512]{2,1,0:T(8,128)S(1)}, u32[]{:S(2)}) copy-start(f32[4,16,512]{2,1,0:T(8,128)S(1)} %get-tuple-element.62) | copy-start | bytes 393220
  3180.0 19.7 all-to-all-start.9
  3277.2 61.6 %all-to-all-start.10 = ((f32[18,64,512]{2,0,1:T(8,128)}), f32[18,64,512]{2,0,1:T(8,128)}, u32[]{:S(2)}, u32[]{:S(2)}) async-start(f32[18,64,512]{2,0,1:T(8,128)} %pad_maximum_fusion.2), calls=%async_computation.11 | async-start | bytes 6291456 | tf_op jit(solution)/shard_map/all_to_all | solution.py:189
  3281.8 420.1 %all-reduce.97.cloned.1.call-start = ((), (), s32[]{:S(2)}) async-start(), calls=%async_computation.25 | async-start | bytes 8388608 | tf_op jit(solution)/shard_map/psum | solution.py:200
  3777.1 9.0 all-to-all-start.11
  3852.0 9.0 all-to-all-start.12
  3856.0 368.6 %all-reduce.99.cloned.1.call-start = ((), (), s32[]{:S(2)}) async-start(), calls=%async_computation.26 | async-start | bytes 8388608 | tf_op jit(solution)/shard_map/psum | solution.py:200
  4291.2 37.5 all-to-all-start.13
  4399.6 29.7 all-to-all-start.14
  4404.2 445.4 %all-reduce.101.cloned.1.call-start = ((), (), s32[]{:S(2)}) async-start(), calls=%async_computation.27 | async-start | bytes 8388608 | tf_op jit(solution)/shard_map/psum | solution.py:200
  4902.0 21.1 all-to-all-start.15
  4906.5 232.9 %all-reduce.103.cloned.1.call-start = ((), (), s32[]{:S(2)}) async-start(), calls=%async_computation.29 | async-start | bytes 10616832 | tf_op jit(solution)/shard_map/psum | solution.py:485
  4989.7 337.6 %reduce-scatter.5.cloned.1.call-start = ((), (), s32[]{:S(2)}) async-start(), calls=%async_computation.28 | async-start | bytes 17301504 | tf_op jit(solution)/shard_map/reduce_scatter | solution.py:490
  (524 other events, 6923.3 us)
Sparse Core Ops, SparseCore 0:
  339.6 166.6 all-reduce.86
  1095.8 96.0 all-reduce.88
  1581.2 95.1 all-reduce.90
  2201.6 95.8 all-reduce.92
  2978.2 95.0 all-reduce.94
  3604.7 97.1 all-reduce.96
  4129.0 95.4 all-reduce.98
  4753.8 95.8 all-reduce.100
Sparse Core Ops, SparseCore 1:
  343.0 153.2 all-gather.3
  2436.0 134.2 reduce-scatter.2
  4989.8 149.6 all-reduce.102
  5141.8 185.4 reduce-scatter.4
where the time goes:
time: 5400 us; the launch traced here: 5370 us
  other arithmetic  2210 us (41%)
  waiting for transfers between devices  1120 us (21%)
  local copies, waits for them, and re-layouts  1050 us (19%)
  matrix products  736 us (14%)
  blocking collectives  161 us (3%)
  starting transfers between devices  67.9 us (1%)
    scatter-add x8, other arithmetic, environ_op(): jnp.zeros(tensor.shape[:2] + (atoms,), jnp.float32).at[:, :, row_source]  1980 us
    psum x8, waiting for transfers between devices, environ_op(): summed = lax.psum(partial_sum, 'edge')  720 us
    unnamed x1145, local copies, waits for them, and re-layouts  298 us
    gather x16, local copies, waits for them, and re-layouts, environ_op(): return summed[:, :, row_source] * scale  251 us
    dot_general x56, matrix products, product_piece(): jnp.einsum('bk,bce->kce', table[first], environ, precision=HIGH)  196 us
    reduce_scatter x1, waiting for transfers between devices, local(): lax.psum_scatter(slot_grads, ('irrep', 'edge'), scatter_dimension=0, tile...  172 us
    dot_general x16, matrix products, update_piece(): jnp.dot(jax.nn.silu(preact), second_w, precision=HIGH)  162 us
    dot_general x16, matrix products, update_piece(): jnp.dot(latent, x_in, precision=HIGH) + contract_first(previous[0], scal_in)  144 us
  transfers between devices with their start and end apart: 27, of which 20 were waited for; matrix products, arithmetic and copies ran while one was open for 11% of the time, Pallas kernels for 0%

commit v1 on v0

v1 whole, which is shorter than its diff:
```python
from functools import partial
import math

import jax
import jax.numpy as jnp
import numpy as np
from jax import lax
from jax.sharding import PartitionSpec as P

D = 1024
NB = 8
SPECIES = 4
LAYERS = 2
BS = 128
NS_STEPS = 4
ADAM_STEP = 10
SIDE = D // BS
AX = ("irrep", "edge")

HIGH = lax.Precision.HIGH
FULL = lax.Precision.HIGHEST
CUTOFF = 5.0
ROOT_TWO = math.sqrt(2.0)
ROOT_THREE = math.sqrt(3.0)
ROOT_SIX = math.sqrt(6.0)
HARMONIC = math.sqrt(7.5)
RES = 1.0 / math.sqrt(2.0)


def shape_basis():
    return [
        np.array([[0.0, 1, 0], [1, 0, 0], [0, 0, 0]]) / ROOT_TWO,
        np.array([[0.0, 0, 0], [0, 0, 1], [0, 1, 0]]) / ROOT_TWO,
        np.array([[0.0, 0, 1], [0, 0, 0], [1, 0, 0]]) / ROOT_TWO,
        np.array([[1.0, 0, 0], [0, -1, 0], [0, 0, 0]]) / ROOT_TWO,
        np.array([[-1.0, 0, 0], [0, -1, 0], [0, 0, 2]]) / ROOT_SIX,
    ]


def cross_three(left_vec, right_vec):
    return np.array(
        [
            left_vec[1] * right_vec[2] - left_vec[2] * right_vec[1],
            left_vec[2] * right_vec[0] - left_vec[0] * right_vec[2],
            left_vec[0] * right_vec[1] - left_vec[1] * right_vec[0],
        ]
    )


def product_table():
    tensors = shape_basis()
    table = np.zeros((9, 9, 9))
    unit_rows = np.eye(9)
    for first in range(9):
        for second in range(9):
            left = unit_rows[first]
            right = unit_rows[second]
            left_mat = sum((left[4 + slot] * tensors[slot] for slot in range(5)))
            right_mat = sum((right[4 + slot] * tensors[slot] for slot in range(5)))
            left_vec = left[1:4]
            right_vec = right[1:4]
            scalar = left[0] * right[0] + left_vec @ right_vec + np.sum(left_mat * right_mat.T)
            vector = (
                left[0] * right_vec
                + right[0] * left_vec
                + cross_three(left_vec, right_vec)
                + left_mat @ right_vec
                + right_mat @ left_vec
            )
            matrix = (
                left[0] * right_mat
                + right[0] * left_mat
                + (np.outer(left_vec, right_vec) + np.outer(right_vec, left_vec)) / 2
                + (left_mat @ right_mat + right_mat @ left_mat) / 2
            )
            table[first, second, 0] = scalar
            table[first, second, 1:4] = vector
            for slot in range(5):
                table[first, second, 4 + slot] = np.sum(tensors[slot] * matrix)
    return (table / 3.0).astype(np.float32)


TABLE = product_table()
TERMS = [
    (a, b, k, float(TABLE[a, b, k]))
    for a in range(9)
    for b in range(9)
    for k in range(9)
    if abs(TABLE[a, b, k]) > 1e-7
]


def dot(left, right, dims, precision=HIGH):
    return lax.dot_general(left, right, ((dims[0], dims[1]), ((), ())), precision=precision)


def nn(left, right):
    return dot(left, right, ((1,), (0,)))


def tn(left, right):
    return dot(left, right, ((0,), (0,)))


def nt(left, right):
    return dot(left, right, ((1,), (1,)))


def device_of(y, x, z, core):
    return (y * 2 + x) * 8 + z * 2 + core


CUBE = [(y, x, z, c) for y in range(2) for x in range(2) for z in range(4) for c in range(2)]
HOP_X = [(device_of(y, x, z, c), device_of(y, 1 - x, z, c)) for y, x, z, c in CUBE]
HOP_Y = [(device_of(y, x, z, c), device_of(1 - y, x, z, c)) for y, x, z, c in CUBE]
HOP_XY = [(device_of(y, x, z, c), device_of(1 - y, 1 - x, z, c)) for y, x, z, c in CUBE]
HOP_CORE = [(device_of(y, x, z, c), device_of(y, x, z, 1 - c)) for y, x, z, c in CUBE]


def along_z(pairs):
    return [
        (device_of(y, x, s, c), device_of(y, x, t, c))
        for s, t in pairs
        for y in range(2)
        for x in range(2)
        for c in range(2)
    ]


HOP_IN = along_z([(0, 1), (3, 2)])
HOP_MID = along_z([(1, 2), (2, 1)])
HOP_OUT = along_z([(1, 0), (2, 3)])
HOP_Z = [along_z([(s, s ^ k) for s in range(4)]) for k in range(1, 4)]


def hop(value, pairs):
    return lax.ppermute(value, AX, pairs)


def place():
    irrep = lax.axis_index("irrep")
    edge = lax.axis_index("edge")
    return irrep // 2, irrep % 2, edge // 2, edge % 2


Z_ORDER = np.array([[3, 2, 1, 0], [3, 2, 0, 1], [0, 1, 3, 2], [0, 1, 2, 3]], np.int32)


def relative_devices():
    y, x, z, core = place()
    zs = jnp.asarray(Z_ORDER)[z]
    two = jnp.arange(2, dtype=jnp.int32)
    irrep = (two[None, :] ^ y) * 2 + (two[:, None] ^ x)
    return (
        irrep[None, :, :, None] * 8 + zs[:, None, None, None] * 2 + (two ^ core)[None, None, None, :]
    )


def reduce_plane(block):
    half = block.shape[2] // 2
    upper, lower = block[:, :, :half], block[:, :, half:]
    a1 = upper[0] + hop(upper[1], HOP_X)
    b1 = lower[:, 0] + hop(lower[:, 1], HOP_Y)
    a2 = a1[0] + hop(a1[1], HOP_Y)
    b2 = b1[0] + hop(b1[1], HOP_X)
    return jnp.concatenate([a2, b2], axis=0)


def reduce_chips(chunks):
    q0 = reduce_plane(chunks[0])
    p0 = q0 + hop(q0, HOP_IN)
    q1 = reduce_plane(chunks[1])
    q2 = reduce_plane(chunks[2])
    q3 = reduce_plane(chunks[3])
    p1 = q1 + hop(q1, HOP_IN)
    p2 = q2 + hop(p0, HOP_MID)
    return q3 + hop(q2, HOP_IN) + hop(p1, HOP_MID) + hop(p2, HOP_OUT)


def spread_plane(own):
    half = own.shape[0] // 2
    upper, lower = own[:half], own[half:]
    a1 = jnp.stack([upper, hop(upper, HOP_Y)])
    b1 = jnp.stack([lower, hop(lower, HOP_X)])
    a2 = jnp.stack([a1, hop(a1, HOP_X)])
    b2 = jnp.stack([b1, hop(b1, HOP_Y)], axis=1)
    return jnp.concatenate([a2, b2], axis=2)


def spread_chips(own):
    from_inner = hop(own, HOP_OUT)
    from_mid = hop(own, HOP_MID)
    from_outer = hop(own, HOP_IN)
    c2 = from_inner + from_outer
    far = hop(from_outer, HOP_MID)
    c1 = from_mid + hop(from_mid, HOP_OUT)
    c0 = far + hop(far, HOP_OUT)
    return [spread_plane(c) for c in (c0, c1, c2, own)]


def is_cube(sizes):
    return sizes == (4, 8)


def gather_small(value, sizes):
    if not is_cube(sizes):
        return lax.all_gather(value, AX, axis=0, tiled=False)
    y, x, z, core = place()
    plane = jnp.stack([value, hop(value, HOP_X), hop(value, HOP_Y), hop(value, HOP_XY)])
    column = jnp.stack([plane] + [hop(plane, pairs) for pairs in HOP_Z])
    every = jnp.stack([column, hop(column, HOP_CORE)])
    flat = every.reshape((32,) + value.shape)
    ids = np.arange(32, dtype=np.int32)
    core_of, z_of, x_of, y_of = ids % 2, ids // 2 % 4, ids // 8 % 2, ids // 16
    index = (core_of ^ core) * 16 + (z_of ^ z) * 4 + (y_of ^ y) * 2 + (x_of ^ x)
    return flat[index]


def sum_small(value, sizes):
    if not is_cube(sizes):
        return lax.psum(value, AX)
    total = value + hop(value, HOP_CORE)
    plane = total + hop(total, HOP_X) + (hop(total, HOP_Y) + hop(total, HOP_XY))
    one, two, three = [hop(plane, pairs) for pairs in HOP_Z]
    return (plane + one) + (two + three)


def geometry(vec, live):
    dist = jnp.sqrt(jnp.sum(vec * vec, axis=0))
    inv = 1.0 / dist
    unit = vec * inv[None]
    ratio = dist / CUTOFF
    r5 = ratio**5
    env = (1.0 - r5 * ratio * (28.0 - 48.0 * ratio + 21.0 * ratio * ratio)) * live
    denv = -(168.0 / CUTOFF) * r5 * (1.0 - ratio) * (1.0 - ratio) * live
    order = jnp.arange(1, NB + 1).astype(jnp.float32)[:, None] * (math.pi / CUTOFF)
    angle = order * dist[None]
    norm = math.sqrt(2.0 / CUTOFF)
    bessel = norm * jnp.sin(angle) * inv[None]
    dbessel = norm * order * jnp.cos(angle) * inv[None] - bessel * inv[None]
    return inv, unit, env, denv, bessel, dbessel


def harmonics(unit):
    x, y, z = unit
    h = HARMONIC
    return jnp.stack(
        [
            jnp.ones_like(x),
            ROOT_THREE * x,
            ROOT_THREE * y,
            ROOT_THREE * z,
            h * ROOT_TWO * x * y,
            h * ROOT_TWO * y * z,
            h * ROOT_TWO * x * z,
            h * (x * x - y * y) / ROOT_TWO,
            h * (2.0 * z * z - x * x - y * y) / ROOT_SIX,
        ]
    )


def harmonics_dot(unit, dunit):
    x, y, z = unit
    dx, dy, dz = dunit
    h = HARMONIC
    return jnp.stack(
        [
            jnp.zeros_like(x),
            ROOT_THREE * dx,
            ROOT_THREE * dy,
            ROOT_THREE * dz,
            h * ROOT_TWO * (dx * y + x * dy),
            h * ROOT_TWO * (dy * z + y * dz),
            h * ROOT_TWO * (dx * z + x * dz),
            h * ROOT_TWO * (x * dx - y * dy),
            (2.0 * h / ROOT_SIX) * (2.0 * z * dz - x * dx - y * dy),
        ]
    )


def harmonics_back(unit, bar):
    x, y, z = unit
    a, b = HARMONIC * ROOT_TWO, 2.0 * HARMONIC / ROOT_SIX
    return jnp.stack(
        [
            ROOT_THREE * bar[1] + a * (y * bar[4] + z * bar[6] + x * bar[7]) - b * x * bar[8],
            ROOT_THREE * bar[2] + a * (x * bar[4] + z * bar[5] - y * bar[7]) - b * y * bar[8],
            ROOT_THREE * bar[3] + a * (y * bar[5] + x * bar[6]) + 2.0 * b * z * bar[8],
        ]
    )


def silu(v):
    return v * jax.nn.sigmoid(v)


def silu_one(v):
    s = jax.nn.sigmoid(v)
    return s * (1.0 + v * (1.0 - s))


def silu_two(v):
    s = jax.nn.sigmoid(v)
    return s * (1.0 - s) * (2.0 + v * (1.0 - 2.0 * s))


def bilinear(sets, out, size):
    total = [None] * size
    for index in TERMS:
        a, b, k, value = index
        slot = index[out]
        for (li, left), (ri, right) in sets:
            term = left[index[li]] * right[index[ri]]
            term = value * term
            total[slot] = term if total[slot] is None else total[slot] + term
    return jnp.stack(total)


def product(feature, environ):
    return bilinear([((0, feature), (1, environ))], 2, 9)


def mix(mixing, tensor, transposed):
    op = tn if transposed else nn
    out = []
    for order, (start, stop) in enumerate(((0, 1), (1, 4), (4, 9))):
        for k in range(start, stop):
            out.append(op(mixing[order], tensor[k]))
    return jnp.stack(out)


def mix_gradient(left, right):
    out = []
    for start, stop in ((0, 1), (1, 4), (4, 9)):
        out.append(sum(nt(left[k], right[k]) for k in range(start, stop)))
    return out


def chain(weights, load_matrices, environ, force_to_tangent, vec, live, species_source, species_target):
    pair_in, pair_out, env_weight, scalar_weight, mix_weight, energy_head = weights
    head = energy_head[:D]
    factor = jnp.sum(
        energy_head[D:, None] * species_source, axis=0
    )
    inv, unit, env, denv, bessel, dbessel = geometry(vec, live)
    shape = harmonics(unit)
    feat = jnp.concatenate([bessel, species_source, species_target], axis=0)
    col = lambda v: v[:, None]
    pre0 = tn(feat, pair_in)
    hid = silu(pre0)
    out0 = nn(hid, pair_out)
    lat0 = col(env) * out0
    w0 = nt(env_weight[0], lat0)
    emb0 = shape[:, None] * w0[None]
    env0 = environ(emb0)
    res0 = product(emb0, env0)
    matrices = load_matrices(res0)
    pre1 = nn(lat0, matrices[0]) + tn(res0[0], scalar_weight[0])
    act1 = silu(pre1)
    out1 = nn(act1, matrices[1])
    lat1 = (lat0 + col(env) * out1) * RES
    w1 = nt(env_weight[1], lat1)
    emb1 = shape[:, None] * w1[None]
    env1 = environ(emb1)
    feat1 = mix(mix_weight, res0, False)
    res1 = jnp.sum(feat1 * env1, axis=0) / 3.0
    pre2 = nn(lat1, matrices[2]) + tn(res1, scalar_weight[1])
    act2 = silu(pre2)
    top = dot(matrices[3], head, ((1,), (0,)))
    slope = env * factor
    per1 = jnp.sum(lat1 * head[None], axis=1)
    per2 = jnp.sum(act2 * top[None], axis=1)
    env_bar = RES * factor * (per1 + 2.0 * env * per2)
    alpha = RES * slope
    lead = alpha * env
    slope2 = silu_one(pre2)
    pre2_bar = col(lead) * top[None] * slope2
    lat1_bar = col(alpha) * head[None] + nt(pre2_bar, matrices[2])
    res1_bar = nt(scalar_weight[1], pre2_bar)
    feat1_bar = res1_bar[None] * env1 / 3.0
    emb1_bar = environ(res1_bar[None] * feat1 / 3.0)
    shape_bar = jnp.sum(emb1_bar * w1[None], axis=1)
    w1_bar = jnp.sum(shape[:, None] * emb1_bar, axis=0)
    lat1_bar = lat1_bar + tn(w1_bar, env_weight[1])
    res0_bar = mix(mix_weight, feat1_bar, True)
    env_bar = env_bar + RES * jnp.sum(lat1_bar * out1, axis=1)
    out1_bar = RES * col(env) * lat1_bar
    act1_bar = nt(out1_bar, matrices[1])
    slope1 = silu_one(pre1)
    pre1_bar = act1_bar * slope1
    lat0_bar = RES * lat1_bar + nt(pre1_bar, matrices[0])
    res0_bar = res0_bar.at[0].add(nt(scalar_weight[0], pre1_bar))
    emb0_bar = bilinear([((2, res0_bar), (1, env0))], 0, 9) + environ(
        bilinear([((2, res0_bar), (0, emb0))], 1, 9)
    )
    shape_bar = shape_bar + jnp.sum(emb0_bar * w0[None], axis=1)
    w0_bar = jnp.sum(shape[:, None] * emb0_bar, axis=0)
    lat0_bar = lat0_bar + tn(w0_bar, env_weight[0])
    env_bar = env_bar + jnp.sum(lat0_bar * out0, axis=1)
    out0_bar = col(env) * lat0_bar
    hid_bar = nt(out0_bar, pair_out)
    slope0 = silu_one(pre0)
    pre0_bar = hid_bar * slope0
    bessel_bar = nt(pair_in[:NB], pre0_bar)
    dist_bar = env_bar * denv + jnp.sum(bessel_bar * dbessel, axis=0)
    unit_bar = harmonics_back(unit, shape_bar)
    along = jnp.sum(unit * unit_bar, axis=0)
    vec_bar = dist_bar[None] * unit + (unit_bar - unit * along[None]) * inv[None]
    vec_dot, loss_parts = force_to_tangent(vec_bar)
    dist_dot = jnp.sum(unit * vec_dot, axis=0)
    unit_dot = (vec_dot - unit * dist_dot[None]) * inv[None]
    env_dot = denv * dist_dot
    bessel_dot = dbessel * dist_dot[None]
    shape_dot = harmonics_dot(unit, unit_dot)
    pre0_dot = tn(bessel_dot, pair_in[:NB])
    hid_dot = slope0 * pre0_dot
    lat0_dot = col(env_dot) * out0 + col(env) * nn(hid_dot, pair_out)
    w0_dot = nt(env_weight[0], lat0_dot)
    emb0_dot = shape_dot[:, None] * w0[None] + shape[:, None] * w0_dot[None]
    env0_dot = environ(emb0_dot)
    res0_dot = bilinear(
        [((0, emb0_dot), (1, env0)), ((0, emb0), (1, env0_dot))], 2, 9
    )
    pre1_dot = nn(lat0_dot, matrices[0]) + tn(res0_dot[0], scalar_weight[0])
    act1_dot = slope1 * pre1_dot
    lat1_dot = (lat0_dot + col(env_dot) * out1 + col(env) * nn(act1_dot, matrices[1])) * RES
    w1_dot = nt(env_weight[1], lat1_dot)
    emb1_dot = shape_dot[:, None] * w1[None] + shape[:, None] * w1_dot[None]
    env1_dot = environ(emb1_dot)
    feat1_dot = mix(mix_weight, res0_dot, False)
    res1_dot = jnp.sum(feat1_dot * env1 + feat1 * env1_dot, axis=0) / 3.0
    pre2_dot = nn(lat1_dot, matrices[2]) + tn(res1_dot, scalar_weight[1])
    act2_dot = slope2 * pre2_dot
    lead_dot = 2.0 * RES * slope * env_dot
    last = jnp.sum(col(lead_dot) * act2 + col(lead) * act2_dot, axis=0)
    head_grad = RES * jnp.sum(
        col(factor * env_dot) * lat1 + col(slope) * lat1_dot, axis=0
    ) + jnp.sum(last[:, None] * matrices[3], axis=0)
    per1_dot = jnp.sum(lat1_dot * head[None], axis=1)
    per2_dot = jnp.sum(act2_dot * top[None], axis=1)
    energy_dot = env_dot * RES * (per1 + env * per2) + env * RES * (
        per1_dot + env_dot * per2 + env * per2_dot
    )
    scale_grad = jnp.sum(species_source * energy_dot[None], axis=1)
    head_grad = jnp.concatenate([head_grad, scale_grad])
    pre2_hat = top[None] * (col(lead_dot) * slope2 + col(lead) * silu_two(pre2) * pre2_dot)
    lat1_hat = col(RES * factor * env_dot) * head[None] + nt(pre2_hat, matrices[2])
    res1_hat = nt(scalar_weight[1], pre2_hat)
    feat1_hat = (res1_hat[None] * env1 + res1_bar[None] * env1_dot) / 3.0
    emb1_hat = environ((res1_hat[None] * feat1 + res1_bar[None] * feat1_dot) / 3.0)
    w1_hat = jnp.sum(shape_dot[:, None] * emb1_bar + shape[:, None] * emb1_hat, axis=0)
    lat1_hat = lat1_hat + tn(w1_hat, env_weight[1])
    res0_hat = mix(mix_weight, feat1_hat, True)
    out1_hat = RES * (col(env_dot) * lat1_bar + col(env) * lat1_hat)
    act1_hat = nt(out1_hat, matrices[1])
    pre1_hat = act1_hat * slope1 + act1_bar * silu_two(pre1) * pre1_dot
    lat0_hat = RES * lat1_hat + nt(pre1_hat, matrices[0])
    res0_hat = res0_hat.at[0].add(nt(scalar_weight[0], pre1_hat))
    emb0_hat = bilinear(
        [((2, res0_hat), (1, env0)), ((2, res0_bar), (1, env0_dot))], 0, 9
    ) + environ(bilinear([((2, res0_hat), (0, emb0)), ((2, res0_bar), (0, emb0_dot))], 1, 9))
    w0_hat = jnp.sum(shape_dot[:, None] * emb0_bar + shape[:, None] * emb0_hat, axis=0)
    lat0_hat = lat0_hat + tn(w0_hat, env_weight[0])
    out0_hat = col(env_dot) * lat0_bar + col(env) * lat0_hat
    pre0_hat = nt(out0_hat, pair_out) * slope0 + hid_bar * silu_two(pre0) * pre0_dot
    both = lambda first, second: jnp.concatenate([first, second], axis=0)
    pair_in_grad = nn(feat, pre0_hat)
    pair_in_grad = pair_in_grad.at[:NB].add(nn(bessel_dot, pre0_bar))
    mix_grad = jnp.stack(
        [
            first + second
            for first, second in zip(
                mix_gradient(feat1_bar, res0_dot), mix_gradient(feat1_hat, res0)
            )
        ]
    )
    env_grad = jnp.stack(
        [nn(w0_bar, lat0_dot) + nn(w0_hat, lat0), nn(w1_bar, lat1_dot) + nn(w1_hat, lat1)]
    )
    scalar_grad = jnp.stack(
        [
            nn(res0_dot[0], pre1_bar) + nn(res0[0], pre1_hat),
            nn(res1_dot, pre2_bar) + nn(res1, pre2_hat),
        ]
    )
    pair_out_grad = tn(both(hid_dot, hid), both(out0_bar, out0_hat))
    matrix_grad = [
        tn(both(lat0_dot, lat0), both(pre1_bar, pre1_hat)),
        tn(both(act1_dot, act1), both(out1_bar, out1_hat)),
        tn(both(lat1_dot, lat1), both(pre2_bar, pre2_hat)),
        last[:, None] * head[None],
    ]
    return (
        pair_in_grad,
        pair_out_grad,
        env_grad,
        scalar_grad,
        mix_grad,
        head_grad,
        matrix_grad,
        loss_parts,
    )


def adamw(weight, first, second, grad):
    first_new = 0.9 * first + 0.1 * grad
    second_new = 0.99 * second + 0.01 * grad * grad
    normal = (
        first_new
        / (1.0 - 0.9**ADAM_STEP)
        / (jnp.sqrt(second_new / (1.0 - 0.99**ADAM_STEP)) + 1e-08)
    )
    return (weight - 0.01 * (normal + 0.01 * weight), first_new, second_new)


def orthogonalize(matrix):
    current = matrix / jnp.sqrt(jnp.sum(matrix * matrix))
    for step_no in range(NS_STEPS):
        current = 1.5 * current - 0.5 * nn(nt(current, current), current)
    return current


def soap_slot(grad, weight, first, second, left, right, lstat, rstat, average):
    rotated = nn(tn(left, grad), right)
    first_new = 0.9 * first + 0.1 * rotated
    second_new = 0.99 * second + 0.01 * rotated * rotated
    normal = (
        first_new
        / (1.0 - 0.9**ADAM_STEP)
        / (jnp.sqrt(second_new / (1.0 - 0.99**ADAM_STEP)) + 1e-08)
    )
    weight_new = weight - 0.01 * (nt(nn(left, normal), right) + 0.01 * weight)
    lstat_new = 0.95 * lstat + 0.05 * nt(grad, grad)
    rstat_new = 0.95 * rstat + 0.05 * tn(grad, grad)
    left_new = orthogonalize(nn(lstat_new, left))
    right_new = orthogonalize(nn(rstat_new, right))
    plain = nt(nn(left, first_new), right)
    first_out = nn(tn(left_new, plain), right_new)
    average_new = 0.99 * average + 0.01 * weight_new
    return (
        weight_new,
        first_out,
        second_new,
        left_new,
        right_new,
        lstat_new,
        rstat_new,
        average_new,
    )


def gather_blocks(soap_weight, block_owner, sizes):
    inverse = jnp.zeros_like(block_owner).at[block_owner].set(
        jnp.arange(block_owner.shape[0], dtype=jnp.int32)
    )
    if not is_cube(sizes):
        return lax.all_gather(soap_weight, AX, axis=0, tiled=True)[inverse]
    per = soap_weight.shape[0]
    pieces = []
    for piece in spread_chips(soap_weight):
        pieces.append(jnp.stack([piece, hop(piece, HOP_CORE)], axis=2))
    every = jnp.concatenate(pieces, axis=0).reshape((-1,) + soap_weight.shape[1:])
    where = jnp.zeros((32,), jnp.int32).at[relative_devices().reshape(-1)].set(
        jnp.arange(32, dtype=jnp.int32)
    )
    return every[where[inverse // per] * per + inverse % per]


def to_matrices(blocks):
    return (
        blocks.reshape(2 * LAYERS, SIDE, SIDE, BS, BS).transpose(0, 1, 3, 2, 4).reshape(2 * LAYERS, D, D)
    )


def to_blocks(matrices):
    return (
        matrices.reshape(2 * LAYERS, SIDE, BS, SIDE, BS)
        .transpose(0, 1, 3, 2, 4)
        .reshape(2 * LAYERS * SIDE * SIDE, BS, BS)
    )


def scatter_blocks(blocks, block_owner, sizes, slots):
    if not is_cube(sizes):
        return lax.psum_scatter(blocks[block_owner], AX, scatter_dimension=0, tiled=True)
    core = lax.axis_index("edge") % 2
    chip = relative_devices()[..., :1] // 2 * (2 * slots)
    owner = block_owner[(chip + jnp.arange(2 * slots, dtype=jnp.int32)).reshape(-1)]
    laid = blocks[owner].reshape(4, 2, 2, 2 * slots, 2, BS // 2, BS)
    swapped = jnp.where(core == 0, laid, laid[:, :, :, :, ::-1])
    chunks = [swapped[p, :, :, :, 0] + hop(swapped[p, :, :, :, 1], HOP_CORE) for p in range(4)]
    total = reduce_chips(chunks)
    mine = jnp.where(core == 0, total[:slots], total[slots:])
    other = hop(jnp.where(core == 0, total[slots:], total[:slots]), HOP_CORE)
    return jnp.where(
        core == 0,
        jnp.concatenate([mine, other], axis=1),
        jnp.concatenate([other, mine], axis=1),
    )


ROWS = 336


def sum_large(trees, sizes):
    if not is_cube(sizes):
        return lax.psum(trees, AX)
    core = lax.axis_index("edge") % 2
    flat = jnp.concatenate([leaf.reshape(-1) for leaf in trees])
    count = flat.shape[0]
    flat = jnp.pad(flat, (0, 32 * ROWS * BS - count)).reshape(32, ROWS, BS)
    devices = relative_devices()
    laid = flat[devices.reshape(-1)].reshape(4, 2, 2, 2, ROWS, BS)
    chunks = [laid[p, :, :, 0] + hop(laid[p, :, :, 1], HOP_CORE) for p in range(4)]
    total = reduce_chips(chunks)
    pieces = []
    for piece in spread_chips(total):
        pieces.append(jnp.stack([piece, hop(piece, HOP_CORE)], axis=2))
    every = jnp.concatenate(pieces, axis=0).reshape(32, ROWS, BS)
    where = jnp.zeros((32,), jnp.int32).at[devices.reshape(-1)].set(
        jnp.arange(32, dtype=jnp.int32)
    )
    flat = every[where].reshape(-1)
    out, start = [], 0
    for leaf in trees:
        out.append(flat[start : start + leaf.size].reshape(leaf.shape))
        start += leaf.size
    return out


def local(
    sizes,
    edge_vec,
    edge_live,
    source,
    target,
    species,
    force_label,
    force_mask,
    block_owner,
    pair_in_weight,
    pair_in_first,
    pair_in_second,
    pair_out_weight,
    pair_out_first,
    pair_out_second,
    env_weight,
    env_first,
    env_second,
    scalar_weight,
    scalar_first,
    scalar_second,
    mix_weight,
    mix_first,
    mix_second,
    energy_head,
    head_first,
    head_second,
    soap_weight,
    soap_first,
    soap_second,
    soap_left,
    soap_right,
    soap_lstat,
    soap_rstat,
    soap_average,
):
    devices = sizes[0] * sizes[1]
    edges = edge_vec.shape[1]
    per_atoms = force_label.shape[1]
    atoms = per_atoms * devices
    me = lax.axis_index("irrep") * sizes[1] + lax.axis_index("edge")
    scale = math.sqrt(per_atoms / edges)
    as_float = lambda v: v.astype(jnp.float32)

    labels = jnp.concatenate([force_label, as_float(force_mask)[None]], axis=0).reshape(-1)
    packed = jnp.concatenate(
        [
            edge_vec,
            as_float(source)[None],
            as_float(target)[None],
            as_float(edge_live)[None],
            jnp.pad(labels, (0, edges - labels.shape[0]))[None],
        ],
        axis=0,
    )
    every = gather_small(packed, sizes)
    label_all = every[:, 6, : 4 * per_atoms].reshape(devices, 4, per_atoms)
    label_all = label_all.transpose(1, 0, 2).reshape(4, atoms)
    label_mask = label_all[3]
    label_total = jnp.sum(label_mask)
    payload = every[:, :5].transpose(0, 2, 1).reshape(devices * edges, 5)
    all_source = every[:, 3].reshape(-1).astype(jnp.int32)
    all_live = every[:, 5].reshape(-1)

    low = (all_source[:, None] % 32 == jnp.arange(32)[None]).astype(jnp.bfloat16)
    high = (all_source[None] // 32 == jnp.arange(-(-atoms // 32))[:, None]) & (all_live[None] > 0)
    counts = jnp.dot(
        high.astype(jnp.bfloat16), low, preferred_element_type=jnp.float32
    ).reshape(-1)[:atoms]
    atom_ids = jnp.arange(atoms)
    before = jnp.dot(
        (atom_ids[:, None] > atom_ids[None]).astype(jnp.float32), counts, precision=FULL
    )
    middle = (2.0 * before + counts).astype(jnp.int32)
    total = jnp.sum(counts).astype(jnp.int32)
    owner = jnp.minimum((middle * devices) // (2 * total), devices - 1)
    loads = jnp.sum(
        jnp.where(owner[None] == jnp.arange(devices)[:, None], counts[None], 0.0), axis=1
    )
    fits = jnp.max(loads) <= edges
    first_atom = jnp.sum(owner < me)
    last_atom = jnp.sum(owner <= me)
    mine = (all_live > 0) & (all_source >= first_atom) & (all_source < last_atom)
    flags = as_float(mine).reshape(-1, 128)
    tri = jnp.arange(128)
    inside = jnp.dot(flags, as_float(tri[:, None] <= tri[None]))
    row_ids = jnp.arange(flags.shape[0])
    row_sum = jnp.sum(flags, axis=1)
    offset = jnp.sum(
        jnp.where(row_ids[None] < row_ids[:, None], row_sum[None], 0.0), axis=1
    )
    rank = (inside + offset[:, None]).reshape(-1)
    slot_ids = jnp.arange(edges).astype(jnp.float32)
    index = jnp.sum((rank[None] <= slot_ids[:, None]).astype(jnp.float32), axis=1).astype(jnp.int32)
    valid = slot_ids < rank[-1]
    chosen = payload[jnp.minimum(index, devices * edges - 1)].T
    safe = jnp.asarray([1.5, 0.0, 0.0], jnp.float32)[:, None]
    my_vec = jnp.where(valid[None], chosen[:3], safe)
    my_source = jnp.where(valid, chosen[3], 0.0).astype(jnp.int32)
    my_target = jnp.where(valid, chosen[4], 0.0).astype(jnp.int32)
    my_live = as_float(valid)

    weights = (pair_in_weight, pair_out_weight, env_weight, scalar_weight, mix_weight[0], energy_head)
    slots = soap_weight.shape[0]
    kinds = jnp.arange(SPECIES, dtype=jnp.int32)[:, None]
    matrices_all = to_matrices(gather_blocks(soap_weight, block_owner, sizes))

    def run(vec, live, src, tgt, environ_of, hold):
        from_atom = (src[:, None] == atom_ids[None]).astype(jnp.float32)
        to_atom = (tgt[:, None] == atom_ids[None]).astype(jnp.float32)
        spec = (species[None] == kinds).astype(jnp.float32)
        species_source = dot(spec, from_atom, ((1,), (1,)), None)
        species_target = dot(spec, to_atom, ((1,), (1,)), None)
        ends = from_atom - to_atom

        def force_to_tangent(vec_bar):
            force = sum_small(nn(vec_bar, ends), sizes)
            residual = force - label_all[:3]
            loss = jnp.sum(label_mask[None] * residual * residual)
            cot = 2.0 * label_mask[None] * residual / label_total
            return nt(cot, ends), loss

        return chain(
            weights,
            lambda after: matrices_all,
            environ_of(from_atom),
            force_to_tangent,
            vec,
            live,
            species_source,
            species_target,
        )

    def environ_local(from_atom):
        same = dot(from_atom, from_atom, ((1,), (1,)), None)
        return lambda tensor: scale * nn(tensor.reshape(-1, edges), same).reshape(tensor.shape)

    def environ_global(from_atom):
        def apply(tensor):
            sums = lax.psum(nn(tensor.reshape(-1, edges), from_atom), AX)
            return scale * nt(sums, from_atom).reshape(tensor.shape)

        return apply

    def pack(out):
        return tuple(out[:6]) + (jnp.stack(out[6]), out[7])

    grads = lax.cond(
        fits,
        lambda: pack(run(my_vec, my_live, my_source, my_target, environ_local, None)),
        lambda: pack(run(edge_vec, as_float(edge_live), source, target, environ_global, None)),
    )
    pair_in_grad, pair_out_grad, env_grad, scalar_grad, mix_grad, head_grad = sum_large(
        grads[:6], sizes
    )
    own_grads = scatter_blocks(to_blocks(grads[6]), block_owner, sizes, slots)
    loss_sum = grads[7]
    new_pair_in = adamw(pair_in_weight, pair_in_first, pair_in_second, pair_in_grad)
    new_pair_out = adamw(pair_out_weight, pair_out_first, pair_out_second, pair_out_grad)
    new_env = adamw(env_weight, env_first, env_second, env_grad)
    new_scalar = adamw(scalar_weight, scalar_first, scalar_second, scalar_grad)
    new_mix = adamw(mix_weight, mix_first, mix_second, mix_grad[None])
    new_head = adamw(energy_head, head_first, head_second, head_grad)
    soap = jax.vmap(soap_slot)(
        own_grads,
        soap_weight,
        soap_first,
        soap_second,
        soap_left,
        soap_right,
        soap_lstat,
        soap_rstat,
        soap_average,
    )
    return (
        (loss_sum, label_total)
        + new_pair_in
        + new_pair_out
        + new_env
        + new_scalar
        + new_mix
        + new_head
        + tuple(soap)
    )


def solution(mesh):
    shared, split = P(), P(AX)
    column = P(None, AX)
    blocks = P(AX, None, None)
    placed = (
        (column, split, split, split, shared, column, split, shared) + (shared,) * 18 + (blocks,) * 8
    )
    return jax.shard_map(
        partial(local, (mesh.shape["irrep"], mesh.shape["edge"])),
        mesh=mesh,
        in_specs=placed,
        out_specs=(shared,) * 20 + (blocks,) * 8,
        check_vma=False,
    )
```

time: 5400 us -> 990 us (0.18)
  other arithmetic: 2210 us -> 172 us
  waiting for transfers between devices: 1120 us -> 181 us
  local copies, waits for them, and re-layouts: 1050 us -> 193 us
  matrix products: 736 us -> 250 us
  blocking collectives: 161 us -> 0 us
  starting transfers between devices: 67.9 us -> 153 us
    scatter-add x10 -> x0, other arithmetic: 1990 us -> none  [the longest x8 1980 us: environ_op(): jnp.zeros(tensor.shape[:2] + (atoms,), jnp.float32).at[:, :, row_source]]
    psum x9 -> x0, waiting for transfers between devices: 751 us -> none  [the longest x8 720 us: environ_op(): summed = lax.psum(partial_sum, 'edge')]
    dot_general x193 -> x148, matrix products: 736 us -> 250 us  [the longest x145 248 us: dot(): lax.dot_general(left, right, ((dims[0], dims[1]), ((), ())), precision=pr...]
    unnamed x1145 -> x117, local copies, waits for them, and re-layouts: 298 us -> 20.6 us
    reduce_scatter x2 -> x0, waiting for transfers between devices: 261 us -> none  [the longest x1 172 us: local(): lax.psum_scatter(slot_grads, ('irrep', 'edge'), scatter_dimension=0, tile...]
    gather x23 -> x9, local copies, waits for them, and re-layouts: 285 us -> 55.7 us  [the longest x3 19 us: gather_blocks(): return every[where[inverse // per] * per + inverse % per]]
    ppermute x0 -> x119, waiting for transfers between devices: none -> 181 us  [hop(): return lax.ppermute(value, AX, pairs)]
    ppermute x0 -> x119, starting transfers between devices: none -> 153 us  [hop(): return lax.ppermute(value, AX, pairs)]
  transfers between devices with their start and end apart: 27 -> 119, of which waited for: 20 -> 46; matrix products, arithmetic and copies ran while one was open for 11% -> 21% of each run, Pallas kernels for 0% -> 0%
where the time goes in v1:
time: 990 us; the launch traced here: 980 us
  matrix products  250 us (25%)
  local copies, waits for them, and re-layouts  193 us (19%)
  waiting for transfers between devices  181 us (18%)
  other arithmetic  172 us (17%)
  starting transfers between devices  153 us (15%)
  between operations  17.8 us (2%)
  loops' own time  12.3 us (1%)
    dot_general x145, matrix products, dot(): lax.dot_general(left, right, ((dims[0], dims[1]), ((), ())), precision=pr...  248 us
    ppermute x119, waiting for transfers between devices, hop(): return lax.ppermute(value, AX, pairs)  181 us
    ppermute x119, starting transfers between devices, hop(): return lax.ppermute(value, AX, pairs)  153 us
    select_n x1, other arithmetic, gather_blocks(): return every[where[inverse // per] * per + inverse % per]  20.6 us
    unnamed x117, local copies, waits for them, and re-layouts  20.6 us
  transfers between devices with their start and end apart: 119, of which 46 were waited for; matrix products, arithmetic and copies ran while one was open for 21% of the time, Pallas kernels for 0%

profile of v1, /device:TPU:0, one launch (start us, length us, event | category | flops | bytes accessed | tf_op | source)
XLA Modules:
  0.0 979.7 jit_solution(11284898211539185914)
XLA Ops:
  30.8 20.6 %compare_select_fusion.3 = s32[256]{0:T(256)S(1)} fusion(s32[256]{0:T(256)S(1)} %scatter_custom_fusion.1, s32[]{:T(128)} %bitcast.427, s32[]{:T(128)} %bitcast.428, s32[]{:T(128)} %bitcast.429, s32[]{:T(128)} %bitcast.430, s32[]{:T(128)} %bitcast.431, s32[]{:T(128)} %bitcast.432, s32[]{:T(128)} %bitcast.433, s32[]{:T(128)} %bitcast.434, s32[]{:T(128)} %bitcast.435, ...), kind=kLoop, calls=%fused_computation.2665 | loop fusion | flops 22784 | bytes 2176 | tf_op jit(solution)/shard_map/select_n | solution.py:566
  62.4 7.7 collective-permute-start.21
  86.2 10.7 %collective-permute-done.30 = f32[8,128,128]{2,1,0:T(8,128)} collective-permute-done((f32[8,128,128]{2,1,0:T(8,128)}, f32[8,128,128]{2,1,0:T(8,128)}, u32[]{:S(2)}, u32[]{:S(2)}) %collective-permute-start.30) | collective-permute-done | bytes 524320 | tf_op jit(solution)/shard_map/ppermute | solution.py:137
  114.8 11.1 %collective-permute-done.24 = f32[4,128,128]{2,1,0:T(8,128)S(1)} collective-permute-done((f32[4,128,128]{2,1,0:T(8,128)S(1)}, f32[4,128,128]{2,1,0:T(8,128)S(1)}, u32[]{:S(2)}, u32[]{:S(2)}) %collective-permute-start.24) | collective-permute-done | bytes 262176 | tf_op jit(solution)/shard_map/ppermute | solution.py:137
  143.8 8.2 collective-permute-done.32
  183.1 10.9 %maximum_maximum_fusion = f32[8,2,2,8,128,128]{5,4,3,2,1,0:T(8,128)} fusion(f32[2,2,1,8,128,128]{5,4,3,2,1,0:T(8,128)} %bitcast.423, f32[2,2,1,8,128,128]{5,4,3,2,1,0:T(8,128)S(1)} %get-tuple-element.565, f32[2,2,1,8,128,128]{5,4,3,2,1,0:T(8,128)} %bitcast.411, f32[2,2,1,8,128,128]{5,4,3,2,1,0:T(8,128)} %get-tuple-element.563, ...), kind=kLoop, calls=%fused_computation.2382 | loop fusion | flops 26214400 | bytes 33554432 | tf_op jit(solution)/shard_map/concatenate | solution.py:562
  194.0 17.7 %gather_fusion.1 = f32[256,128,128]{2,1,0:T(8,128)} fusion(f32[256,128,128]{2,1,0:T(8,128)} %bitcast.2787, s32[1024]{0:T(1024)S(1)} %pad_clamp_fusion.5), kind=kCustom, calls=%fused_computation.1 | custom fusion | bytes 33555456 | tf_op jit(solution)/shard_map/gather | solution.py:566
  211.7 18.7 %copy.200 = f32[4,8,128,8,128]{4,3,2,1,0:T(8,128)} copy(f32[4,8,128,8,128]{4,2,3,1,0:T(8,128)} %bitcast.2788) | data formatting | bytes 33554432 | tf_op jit(solution)/shard_map/transpose | solution.py:571
  230.5 18.1 %reshape.1154 = f32[4,1024,1024]{2,1,0:T(8,128)} reshape(f32[4,8,128,8,128]{4,3,2,1,0:T(8,128)} %copy.200) | data formatting | bytes 33554432 | tf_op jit(solution)/shard_map/reshape | solution.py:571
  249.8 323.0 %conditional.1 = (f32[1028]{0:T(1024)}, f32[4,1024,1024]{2,1,0:T(8,128)}, f32[]{:T(128)}, f32[16384]{0:T(1024)S(1)}, f32[1048576]{0:T(1024)S(1)}, /*index=5*/f32[131072]{0:T(1024)}, f32[131072]{0:T(1024)}, f32[12288]{0:T(1024)}) conditional(s32[]{:T(128)} %convert_element_type.146, (f32[3,512]{1,0:T(4,128)S(1)}, s32[512]{0:T(512)S(1)}, ...), branch_computations={%region_11.44_spmd, %region_44.69_spmd} | conditional | flops 97724276736 | bytes 1392813312 | solution.py:779
  287.4 6.9 broadcast_multiply_fusion.34
  321.6 8.9 fusion.1884
  407.3 9.0 add_reduce_fusion.6
  454.7 8.6 fusion.1061
  469.6 10.4 %fusion.1044 = f32[1,1024,1024]{2,1,0:T(8,128)} fusion(f32[512,1024]{1,0:T(8,128)} %copy-done.116, f32[512,1024]{1,0:T(8,128)} %copy-done.108, f32[512,1024]{1,0:T(8,128)S(1)} %copy-done.100, f32[512,1024]{1,0:T(8,128)S(1)} %copy-done.51), kind=kOutput, calls=%fused_computation.1292 | convolution fusion | flops 6444548096 | bytes 12582912 | tf_op jit(solution)/shard_map/cond/branch_1_fun/dot_general | solution.py:94
  498.8 10.4 %fusion.1039 = f32[1,1024,1024]{2,1,0:T(8,128)} fusion(f32[512,1024]{1,0:T(8,128)S(1)} %copy-done.218, f32[512,1024]{1,0:T(8,128)S(1)} %copy-done.217, f32[512,1024]{1,0:T(8,128)} %get-tuple-element.464, f32[512,1024]{1,0:T(8,128)S(1)} %copy-done.191), kind=kOutput, calls=%fused_computation.1291 | convolution fusion | flops 6444548096 | bytes 12582912 | tf_op jit(solution)/shard_map/cond/branch_1_fun/dot_general | solution.py:94
  541.2 7.7 fusion.1029
  557.8 7.5 fusion.1034
  594.6 9.4 copy.282
  604.0 6.9 copy.222
  610.9 17.8 %gather_fusion.6 = f32[256,128,128]{2,1,0:T(8,128)} fusion(f32[256,128,128]{2,1,0:T(8,128)} %bitcast.2789, s32[1024]{0:T(1024)} %pad_clamp_fusion), kind=kCustom, calls=%fused_computation.6 | custom fusion | bytes 33555456 | tf_op jit(solution)/shard_map/gather | solution.py:589
  628.7 19.7 %reverse_select_fusion = f32[4,2,2,16,2,64,128]{6,5,4,3,2,1,0:T(8,128)} fusion(f32[4,2,2,16,2,64,128]{6,5,4,3,2,1,0:T(8,128)} %bitcast.2790, pred[]{:T(512)S(6)} %eq.150), kind=kLoop, calls=%fused_computation.2381 | loop fusion | flops 4194304 | bytes 33554432 | tf_op jit(solution)/shard_map/jit(_where)/select_n | solution.py:590
  648.5 11.1 %fusion.2036 = (f32[1,2,2,16,1,64,128]{6,5,4,3,2,1,0:T(8,128)}, f32[1,2,2,16,1,64,128]{6,5,4,3,2,1,0:T(8,128)}, f32[1,2,2,16,1,64,128]{6,5,4,3,2,1,0:T(8,128)}, ...) fusion(f32[4,2,2,16,2,64,128]{6,5,4,3,2,1,0:T(8,128)} %reverse_, ...), kind=kLoop, calls=%fused_computation.2802 | loop fusion | bytes 29360128 | tf_op jit(solution)/shard_map/slice | solution.py:591
  704.1 10.3 %collective-permute-start.57 = (f32[336,128]{1,0:T(8,128)S(1)}, f32[336,128]{1,0:T(8,128)S(1)}, u32[]{:S(2)}, u32[]{:S(2)}) collective-permute-start(f32[336,128]{1,0:T(8,128)S(1)} %get-tuple-element.653), channel_id=1, source_target_pairs={{0,2},{1,3},{8,10},{9,11},{16,18},{17,19},{24,26},{25,27},{6,4},{7... | collective-permute-start | bytes 516104 | tf_op jit(solution)/shard_map/ppermute | solution.py:137
  788.0 10.1 %collective-permute-done.111 = f32[2,8,64,128]{3,2,1,0:T(8,128)S(1)} collective-permute-done((f32[2,8,64,128]{3,2,1,0:T(8,128)S(1)}, f32[2,8,64,128]{3,2,1,0:T(8,128)S(1)}, u32[]{:S(2)}, u32[]{:S(2)}) %collective-permute-start.111) | collective-permute-done | bytes 524320 | tf_op jit(solution)/shard_map/ppermute | solution.py:137
  800.5 10.9 %collective-permute-done.100 = f32[2,8,64,128]{3,2,1,0:T(8,128)S(1)} collective-permute-done((f32[2,8,64,128]{3,2,1,0:T(8,128)S(1)}, f32[2,8,64,128]{3,2,1,0:T(8,128)S(1)}, u32[]{:S(2)}, u32[]{:S(2)}) %collective-permute-start.100) | collective-permute-done | bytes 524320 | tf_op jit(solution)/shard_map/ppermute | solution.py:137
  813.7 10.0 %collective-permute-done.105 = f32[2,8,64,128]{3,2,1,0:T(8,128)S(1)} collective-permute-done((f32[2,8,64,128]{3,2,1,0:T(8,128)S(1)}, f32[2,8,64,128]{3,2,1,0:T(8,128)S(1)}, u32[]{:S(2)}, u32[]{:S(2)}) %collective-permute-start.105) | collective-permute-done | bytes 524320 | tf_op jit(solution)/shard_map/ppermute | solution.py:137
  826.1 9.7 collective-permute-done.118
  892.3 6.8 slice.818
  901.2 10.8 %multiply_subtract_fusion = (f32[1024,1024]{1,0:T(8,128)}, f32[1024,1024]{1,0:T(8,128)}, f32[1024,1024]{1,0:T(8,128)}) fusion(f32[1024,1024]{1,0:T(8,128)} %param.65, f32[1344,1024]{1,0:T(8,128)} %slice.818, f32[1024,1024]{1,0:T(8,128)} %param.66, f32[1024,1024]{1,0:T(8,128)} %param.67), kind=kLoop, calls=%fused_computation.2387 | loop fusion | flops 15728640 | bytes 29360128 | tf_op jit(solution)/shard_map/sub | solution.py:513
  919.9 11.3 %collective-permute-start.109 = (f32[16,64,128]{2,1,0:T(8,128)S(1)}, f32[16,64,128]{2,1,0:T(8,128)S(1)}, u32[]{:S(2)}, u32[]{:S(2)}) collective-permute-start(f32[16,64,128]{2,1,0:T(8,128)S(1)} %get-tuple-element.585), channel_id=1, source_target_pairs={{0,2},{1,3},{8,10},{9,11},{16,18},{17,19},{24,26},{25,27},{6,4},{7... | collective-permute-start | bytes 1572872 | tf_op jit(solution)/shard_map/ppermute | solution.py:137
  944.0 9.1 slice.823
  (1251 shorter events, 602.4 us)
Async XLA Ops:
  11.5 40.4 %collective-permute-start.16 = (f32[7,512]{1,0:T(8,128)S(1)}, f32[7,512]{1,0:T(8,128)S(1)}, u32[]{:S(2)}, u32[]{:S(2)}) collective-permute-start(f32[7,512]{1,0:T(8,128)S(1)} %concatenate.142), channel_id=1, source_target_pairs={{0,24},{1,25},{2,26},{3,27},{4,28},{5,29},{6,30},{7,31},{8,16},{9,... | collective-permute-start | bytes 43016 | tf_op jit(solution)/shard_map/ppermute | solution.py:137
  15.5 36.5 %collective-permute-start.15 = (f32[7,512]{1,0:T(8,128)S(1)}, f32[7,512]{1,0:T(8,128)S(1)}, u32[]{:S(2)}, u32[]{:S(2)}) collective-permute-start(f32[7,512]{1,0:T(8,128)S(1)} %concatenate.142), channel_id=1, source_target_pairs={{0,16},{1,17},{2,18},{3,19},{4,20},{5,21},{6,22},{7,23},{8,24},{9,... | collective-permute-start | bytes 43016 | tf_op jit(solution)/shard_map/ppermute | solution.py:137
  16.0 36.0 %collective-permute-start.14 = (f32[7,512]{1,0:T(8,128)S(1)}, f32[7,512]{1,0:T(8,128)S(1)}, u32[]{:S(2)}, u32[]{:S(2)}) collective-permute-start(f32[7,512]{1,0:T(8,128)S(1)} %concatenate.142), channel_id=1, source_target_pairs={{0,8},{1,9},{2,10},{3,11},{4,12},{5,13},{6,14},{7,15},{8,0},{9,1},... | collective-permute-start | bytes 43016 | tf_op jit(solution)/shard_map/ppermute | solution.py:137
  17.3 52.9 %collective-permute-start.42 = (f32[4,128,128]{2,1,0:T(8,128)S(1)}, f32[4,128,128]{2,1,0:T(8,128)S(1)}, u32[]{:S(2)}, u32[]{:S(2)}) collective-permute-start(f32[4,128,128]{2,1,0:T(8,128)S(1)} %get-tuple-element.615), channel_id=1, source_target_pairs={{0,16},{1,17},{2,18},{3,19},{4,20},{5,21},{6,22},{7,23},{8,24},{9,... | collective-permute-start | bytes 786440 | tf_op jit(solution)/shard_map/ppermute | solution.py:137
  19.3 52.1 %collective-permute-start.44 = (f32[4,128,128]{2,1,0:T(8,128)S(1)}, f32[4,128,128]{2,1,0:T(8,128)S(1)}, u32[]{:S(2)}, u32[]{:S(2)}) collective-permute-start(f32[4,128,128]{2,1,0:T(8,128)S(1)} %get-tuple-element.616), channel_id=1, source_target_pairs={{0,8},{1,9},{2,10},{3,11},{4,12},{5,13},{6,14},{7,15},{8,0},{9,1},... | collective-permute-start | bytes 786440 | tf_op jit(solution)/shard_map/ppermute | solution.py:137
  58.7 22.4 %collective-permute-start.36 = (f32[8,128,128]{2,1,0:T(8,128)S(1)}, f32[8,128,128]{2,1,0:T(8,128)}, u32[]{:S(2)}, u32[]{:S(2)}) collective-permute-start(f32[8,128,128]{2,1,0:T(8,128)S(1)} %copy-done.211), channel_id=1, source_target_pairs={{2,0},{3,1},{10,8},{11,9},{18,16},{19,17},{26,24},{27,25},{4,6},{5... | collective-permute-start | bytes 1572872 | tf_op jit(solution)/shard_map/ppermute | solution.py:137
  60.1 19.1 %collective-permute-start.29 = (f32[8,128,128]{2,1,0:T(8,128)S(1)}, f32[8,128,128]{2,1,0:T(8,128)}, u32[]{:S(2)}, u32[]{:S(2)}) collective-permute-start(f32[8,128,128]{2,1,0:T(8,128)S(1)} %copy-done.211), channel_id=1, source_target_pairs={{2,4},{3,5},{10,12},{11,13},{18,20},{19,21},{26,28},{27,29},{4,2},... | collective-permute-start | bytes 1572872 | tf_op jit(solution)/shard_map/ppermute | solution.py:137
  71.4 58.9 %collective-permute-start.43 = (f32[2,4,128,128]{3,2,1,0:T(8,128)}, f32[2,4,128,128]{3,2,1,0:T(8,128)S(1)}, u32[]{:S(2)}, u32[]{:S(2)}) collective-permute-start(f32[2,4,128,128]{3,2,1,0:T(8,128)} %get-tuple-element.612), channel_id=1, source_target_pairs={{0,8},{1,9},{2,10},{3,11},{4,12},{5,13},{6,14},{7,15},{8,0},{9,1},... | collective-permute-start | bytes 1572872 | tf_op jit(solution)/shard_map/ppermute | solution.py:137
  73.0 57.4 %collective-permute-start.45 = (f32[2,4,128,128]{3,2,1,0:T(8,128)}, f32[2,4,128,128]{3,2,1,0:T(8,128)}, u32[]{:S(2)}, u32[]{:S(2)}) collective-permute-start(f32[2,4,128,128]{3,2,1,0:T(8,128)} %get-tuple-element.618), channel_id=1, source_target_pairs={{0,16},{1,17},{2,18},{3,19},{4,20},{5,21},{6,22},{7,23},{8,24},{9,... | collective-permute-start | bytes 1572872 | tf_op jit(solution)/shard_map/ppermute | solution.py:137
  83.8 20.1 %collective-permute-start.23 = (f32[8,128,128]{2,1,0:T(8,128)S(1)}, f32[8,128,128]{2,1,0:T(8,128)}, u32[]{:S(2)}, u32[]{:S(2)}) collective-permute-start(f32[8,128,128]{2,1,0:T(8,128)S(1)} %collective-permute-done.22), channel_id=1, source_target_pairs={{2,0},{3,1},{10,8},{11,9},{18,16},{19,17},{26,24},{27,25},{4,6},{5... | collective-permute-start | bytes 1572872 | tf_op jit(solution)/shard_map/ppermute | solution.py:137
  106.6 23.9 %collective-permute-start.40 = (f32[2,4,128,128]{3,2,1,0:T(8,128)S(1)}, f32[2,4,128,128]{3,2,1,0:T(8,128)S(1)}, u32[]{:S(2)}, u32[]{:S(2)}) collective-permute-start(f32[2,4,128,128]{3,2,1,0:T(8,128)S(1)} %get-tuple-element.610), channel_id=1, source_target_pairs={{0,16},{1,17},{2,18},{3,19},{4,20},{5,21},{6,22},{7,23},{8,24},{9,... | collective-permute-start | bytes 1572872 | tf_op jit(solution)/shard_map/ppermute | solution.py:137
  130.3 21.7 %collective-permute-start.32 = (f32[2,4,128,128]{3,2,1,0:T(8,128)S(1)}, f32[2,4,128,128]{3,2,1,0:T(8,128)S(1)}, u32[]{:S(2)}, u32[]{:S(2)}) collective-permute-start(f32[2,4,128,128]{3,2,1,0:T(8,128)S(1)} %get-tuple-element.596), channel_id=1, source_target_pairs={{0,8},{1,9},{2,10},{3,11},{4,12},{5,13},{6,14},{7,15},{8,0},{9,1},... | collective-permute-start | bytes 1572872 | tf_op jit(solution)/shard_map/ppermute | solution.py:137
  130.4 24.1 %collective-permute-start.27 = (f32[2,4,128,128]{3,2,1,0:T(8,128)S(1)}, f32[2,4,128,128]{3,2,1,0:T(8,128)S(1)}, u32[]{:S(2)}, u32[]{:S(2)}) collective-permute-start(f32[2,4,128,128]{3,2,1,0:T(8,128)S(1)} %get-tuple-element.594), channel_id=1, source_target_pairs={{0,16},{1,17},{2,18},{3,19},{4,20},{5,21},{6,22},{7,23},{8,24},{9,... | collective-permute-start | bytes 1572872 | tf_op jit(solution)/shard_map/ppermute | solution.py:137
  130.4 27.7 %collective-permute-start.25 = (f32[2,4,128,128]{3,2,1,0:T(8,128)S(1)}, f32[2,4,128,128]{3,2,1,0:T(8,128)S(1)}, u32[]{:S(2)}, u32[]{:S(2)}) collective-permute-start(f32[2,4,128,128]{3,2,1,0:T(8,128)S(1)} %get-tuple-element.588), channel_id=1, source_target_pairs={{0,8},{1,9},{2,10},{3,11},{4,12},{5,13},{6,14},{7,15},{8,0},{9,1},... | collective-permute-start | bytes 1572872 | tf_op jit(solution)/shard_map/ppermute | solution.py:137
  140.7 42.3 %collective-permute-start.46 = (f32[2,2,8,128,128]{4,3,2,1,0:T(8,128)}, f32[2,2,8,128,128]{4,3,2,1,0:T(8,128)}, u32[]{:S(2)}, u32[]{:S(2)}) collective-permute-start(f32[2,2,8,128,128]{4,3,2,1,0:T(8,128)} %get-tuple-element.566), channel_id=1, source_target_pairs={{0,1},{1,0},{2,3},{3,2},{4,5},{5,4},{6,7},{7,6},{8,9},{9,8},{10,11... | collective-permute-start | bytes 6291464 | tf_op jit(solution)/shard_map/ppermute | solution.py:137
  143.3 39.8 %collective-permute-start.41 = (f32[2,2,8,128,128]{4,3,2,1,0:T(8,128)}, f32[2,2,8,128,128]{4,3,2,1,0:T(8,128)}, u32[]{:S(2)}, u32[]{:S(2)}) collective-permute-start(f32[2,2,8,128,128]{4,3,2,1,0:T(8,128)} %get-tuple-element.564), channel_id=1, source_target_pairs={{0,1},{1,0},{2,3},{3,2},{4,5},{5,4},{6,7},{7,6},{8,9},{9,8},{10,11... | collective-permute-start | bytes 6291464 | tf_op jit(solution)/shard_map/ppermute | solution.py:137
  154.5 28.6 %collective-permute-start.35 = (f32[2,2,8,128,128]{4,3,2,1,0:T(8,128)}, f32[2,2,8,128,128]{4,3,2,1,0:T(8,128)}, u32[]{:S(2)}, u32[]{:S(2)}) collective-permute-start(f32[2,2,8,128,128]{4,3,2,1,0:T(8,128)} %get-tuple-element.562), channel_id=1, source_target_pairs={{0,1},{1,0},{2,3},{3,2},{4,5},{5,4},{6,7},{7,6},{8,9},{9,8},{10,11... | collective-permute-start | bytes 6291464 | tf_op jit(solution)/shard_map/ppermute | solution.py:137
  160.7 22.4 %collective-permute-start.28 = (f32[2,2,8,128,128]{4,3,2,0,1:T(8,128)}, f32[2,2,8,128,128]{4,3,2,0,1:T(8,128)}, u32[]{:S(2)}, u32[]{:S(2)}) collective-permute-start(f32[2,2,8,128,128]{4,3,2,0,1:T(8,128)} %get-tuple-element.560), channel_id=1, source_target_pairs={{0,1},{1,0},{2,3},{3,2},{4,5},{5,4},{6,7},{7,6},{8,9},{9,8},{10,11... | collective-permute-start | bytes 6291464 | tf_op jit(solution)/shard_map/ppermute | solution.py:137
  593.6 67.9 %collective-permute-start.58 = (f32[2,2,336,128]{3,2,0,1:T(8,128)}, f32[2,2,336,128]{3,2,0,1:T(8,128)}, u32[]{:S(2)}, u32[]{:S(2)}) collective-permute-start(f32[2,2,336,128]{3,2,0,1:T(8,128)} %bitcast.2775), channel_id=1, source_target_pairs={{0,1},{1,0},{2,3},{3,2},{4,5},{5,4},{6,7},{7,6},{8,9},{9,8},{10,11... | collective-permute-start | bytes 2064392 | tf_op jit(solution)/shard_map/ppermute | solution.py:137
  593.6 71.0 %collective-permute-start.47 = (f32[2,2,336,128]{3,2,0,1:T(8,128)}, f32[2,2,336,128]{3,2,0,1:T(8,128)}, u32[]{:S(2)}, u32[]{:S(2)}) collective-permute-start(f32[2,2,336,128]{3,2,0,1:T(8,128)} %bitcast.2777), channel_id=1, source_target_pairs={{0,1},{1,0},{2,3},{3,2},{4,5},{5,4},{6,7},{7,6},{8,9},{9,8},{10,11... | collective-permute-start | bytes 2064392 | tf_op jit(solution)/shard_map/ppermute | solution.py:137
  594.1 72.3 %collective-permute-start.52 = (f32[2,2,336,128]{3,2,0,1:T(8,128)}, f32[2,2,336,128]{3,2,0,1:T(8,128)}, u32[]{:S(2)}, u32[]{:S(2)}) collective-permute-start(f32[2,2,336,128]{3,2,0,1:T(8,128)} %bitcast.2776), channel_id=1, source_target_pairs={{0,1},{1,0},{2,3},{3,2},{4,5},{5,4},{6,7},{7,6},{8,9},{9,8},{10,11... | collective-permute-start | bytes 2064392 | tf_op jit(solution)/shard_map/ppermute | solution.py:137
  594.1 74.3 %collective-permute-start.65 = (f32[2,2,336,128]{3,2,1,0:T(8,128)}, f32[2,2,336,128]{3,2,1,0:T(8,128)}, u32[]{:S(2)}, u32[]{:S(2)}) collective-permute-start(f32[2,2,336,128]{3,2,1,0:T(8,128)} %get-tuple-element.549), channel_id=1, source_target_pairs={{0,1},{1,0},{2,3},{3,2},{4,5},{5,4},{6,7},{7,6},{8,9},{9,8},{10,11... | collective-permute-start | bytes 2064392 | tf_op jit(solution)/shard_map/ppermute | solution.py:137
  661.4 117.6 %collective-permute-start.110 = (f32[2,2,16,64,128]{4,3,2,0,1:T(8,128)S(1)}, f32[2,2,16,64,128]{4,3,2,0,1:T(8,128)S(1)}, u32[]{:S(2)}, u32[]{:S(2)}) collective-permute-start(f32[2,2,16,64,128]{4,3,2,0,1:T(8,128)S(1)} %bitcast.2821), channel_id=1, source_target_pairs={{0,1},{1,0},{2,3},{3,2},{4,5},{5,4},{6,7},{7,6},{8,9},{9,8},{10,11... | collective-permute-start | bytes 6291464 | tf_op jit(solution)/shard_map/ppermute | solution.py:137
  683.3 32.4 %collective-permute-start.49 = (f32[168,128]{1,0:T(8,128)S(1)}, f32[168,128]{1,0:T(8,128)S(1)}, u32[]{:S(2)}, u32[]{:S(2)}) collective-permute-start(f32[168,128]{1,0:T(8,128)S(1)} %slice_bitcast_fusion.195), channel_id=1, source_target_pairs={{0,16},{1,17},{2,18},{3,19},{4,20},{5,21},{6,22},{7,23},{8,24},{9,... | collective-permute-start | bytes 258056 | tf_op jit(solution)/shard_map/ppermute | solution.py:137
  731.2 49.1 %collective-permute-start.99 = (f32[2,2,16,64,128]{4,3,2,0,1:T(8,128)S(1)}, f32[2,2,16,64,128]{4,3,2,0,1:T(8,128)S(1)}, u32[]{:S(2)}, u32[]{:S(2)}) collective-permute-start(f32[2,2,16,64,128]{4,3,2,0,1:T(8,128)S(1)} %bitcast.2823), channel_id=1, source_target_pairs={{0,1},{1,0},{2,3},{3,2},{4,5},{5,4},{6,7},{7,6},{8,9},{9,8},{10,11... | collective-permute-start | bytes 6291464 | tf_op jit(solution)/shard_map/ppermute | solution.py:137
  759.4 23.1 %collective-permute-start.104 = (f32[2,2,16,64,128]{4,3,2,0,1:T(8,128)S(1)}, f32[2,2,16,64,128]{4,3,2,0,1:T(8,128)S(1)}, u32[]{:S(2)}, u32[]{:S(2)}) collective-permute-start(f32[2,2,16,64,128]{4,3,2,0,1:T(8,128)S(1)} %bitcast.2822), channel_id=1, source_target_pairs={{0,1},{1,0},{2,3},{3,2},{4,5},{5,4},{6,7},{7,6},{8,9},{9,8},{10,11... | collective-permute-start | bytes 6291464 | tf_op jit(solution)/shard_map/ppermute | solution.py:137
  778.9 101.9 %collective-permute-start.98 = (f32[2,2,336,128]{3,2,0,1:T(8,128)S(1)}, f32[2,2,336,128]{3,2,0,1:T(8,128)S(1)}, u32[]{:S(2)}, u32[]{:S(2)}) collective-permute-start(f32[2,2,336,128]{3,2,0,1:T(8,128)S(1)} %get-tuple-element.574), channel_id=1, source_target_pairs={{0,1},{1,0},{2,3},{3,2},{4,5},{5,4},{6,7},{7,6},{8,9},{9,8},{10,11... | collective-permute-start | bytes 2064392 | tf_op jit(solution)/shard_map/ppermute | solution.py:137
  787.3 95.5 %collective-permute-start.93 = (f32[2,2,336,128]{3,2,0,1:T(8,128)S(1)}, f32[2,2,336,128]{3,2,0,1:T(8,128)S(1)}, u32[]{:S(2)}, u32[]{:S(2)}) collective-permute-start(f32[2,2,336,128]{3,2,0,1:T(8,128)S(1)} %get-tuple-element.572), channel_id=1, source_target_pairs={{0,1},{1,0},{2,3},{3,2},{4,5},{5,4},{6,7},{7,6},{8,9},{9,8},{10,11... | collective-permute-start | bytes 2064392 | tf_op jit(solution)/shard_map/ppermute | solution.py:137
  787.6 95.2 %collective-permute-start.87 = (f32[2,2,336,128]{3,2,0,1:T(8,128)S(1)}, f32[2,2,336,128]{3,2,0,1:T(8,128)S(1)}, u32[]{:S(2)}, u32[]{:S(2)}) collective-permute-start(f32[2,2,336,128]{3,2,0,1:T(8,128)S(1)} %get-tuple-element.570), channel_id=1, source_target_pairs={{0,1},{1,0},{2,3},{3,2},{4,5},{5,4},{6,7},{7,6},{8,9},{9,8},{10,11... | collective-permute-start | bytes 2064392 | tf_op jit(solution)/shard_map/ppermute | solution.py:137
  859.5 23.4 %collective-permute-start.80 = (f32[2,2,336,128]{3,2,0,1:T(8,128)S(1)}, f32[2,2,336,128]{3,2,0,1:T(8,128)S(1)}, u32[]{:S(2)}, u32[]{:S(2)}) collective-permute-start(f32[2,2,336,128]{3,2,0,1:T(8,128)S(1)} %get-tuple-element.568), channel_id=1, source_target_pairs={{0,1},{1,0},{2,3},{3,2},{4,5},{5,4},{6,7},{7,6},{8,9},{9,8},{10,11... | collective-permute-start | bytes 2064392 | tf_op jit(solution)/shard_map/ppermute | solution.py:137
  875.4 42.4 %collective-permute-start.115 = (f32[16,64,128]{2,1,0:T(8,128)}, f32[16,64,128]{2,1,0:T(8,128)}, u32[]{:S(2)}, u32[]{:S(2)}) collective-permute-start(f32[16,64,128]{2,1,0:T(8,128)} %pad_maximum_fusion.31), channel_id=1, source_target_pairs={{0,2},{1,3},{8,10},{9,11},{16,18},{17,19},{24,26},{25,27},{6,4},{7... | collective-permute-start | bytes 1572872 | tf_op jit(solution)/shard_map/ppermute | solution.py:137
  880.8 32.5 %collective-permute-start.122 = (f32[16,64,128]{2,1,0:T(8,128)}, f32[16,64,128]{2,1,0:T(8,128)}, u32[]{:S(2)}, u32[]{:S(2)}) collective-permute-start(f32[16,64,128]{2,1,0:T(8,128)} %pad_maximum_fusion.32), channel_id=1, source_target_pairs={{0,2},{1,3},{8,10},{9,11},{16,18},{17,19},{24,26},{25,27},{6,4},{7... | collective-permute-start | bytes 1572872 | tf_op jit(solution)/shard_map/ppermute | solution.py:137
  (365 other events, 4240.3 us)

commit v2 on v1

--- a/solution.py
+++ b/solution.py
@@ -1,10 +1,13 @@
 from functools import partial
 import math
+from types import SimpleNamespace
 
 import jax
 import jax.numpy as jnp
 import numpy as np
 from jax import lax
+from jax.experimental import pallas as pl
+from jax.experimental.pallas import tpu as pltpu
 from jax.sharding import PartitionSpec as P
 
 D = 1024
@@ -156,46 +159,32 @@
     )
 
 
-def reduce_plane(block):
-    half = block.shape[2] // 2
-    upper, lower = block[:, :, :half], block[:, :, half:]
-    a1 = upper[0] + hop(upper[1], HOP_X)
-    b1 = lower[:, 0] + hop(lower[:, 1], HOP_Y)
-    a2 = a1[0] + hop(a1[1], HOP_Y)
-    b2 = b1[0] + hop(b1[1], HOP_X)
-    return jnp.concatenate([a2, b2], axis=0)
-
-
 def reduce_chips(chunks):
-    q0 = reduce_plane(chunks[0])
+    first, planes_done = [], []
+
+    def second(p):
+        (a0, a1), (b0, b1) = first[p]
+        planes_done.append(
+            jnp.concatenate([a0 + hop(a1, HOP_Y), b0 + hop(b1, HOP_X)], axis=0)
+        )
+
+    for p in range(4):
+        block = chunks[p]
+        if p >= 2:
+            block, first[p - 2] = lax.optimization_barrier((block, first[p - 2]))
+            second(p - 2)
+        half = block.shape[2] // 2
+        upper, lower = block[:, :, :half], block[:, :, half:]
+        a = upper[0] + hop(upper[1], HOP_X)
+        b = lower[:, 0] + hop(lower[:, 1], HOP_Y)
+        first.append(((a[0], a[1]), (b[0], b[1])))
+    second(2)
+    second(3)
+    q0, q1, q2, q3 = planes_done
     p0 = q0 + hop(q0, HOP_IN)
-    q1 = reduce_plane(chunks[1])
-    q2 = reduce_plane(chunks[2])
-    q3 = reduce_plane(chunks[3])
     p1 = q1 + hop(q1, HOP_IN)
     p2 = q2 + hop(p0, HOP_MID)
-    return q3 + hop(q2, HOP_IN) + hop(p1, HOP_MID) + hop(p2, HOP_OUT)
-
-
-def spread_plane(own):
-    half = own.shape[0] // 2
-    upper, lower = own[:half], own[half:]
-    a1 = jnp.stack([upper, hop(upper, HOP_Y)])
-    b1 = jnp.stack([lower, hop(lower, HOP_X)])
-    a2 = jnp.stack([a1, hop(a1, HOP_X)])
-    b2 = jnp.stack([b1, hop(b1, HOP_Y)], axis=1)
-    return jnp.concatenate([a2, b2], axis=2)
-
-
-def spread_chips(own):
-    from_inner = hop(own, HOP_OUT)
-    from_mid = hop(own, HOP_MID)
-    from_outer = hop(own, HOP_IN)
-    c2 = from_inner + from_outer
-    far = hop(from_outer, HOP_MID)
-    c1 = from_mid + hop(from_mid, HOP_OUT)
-    c0 = far + hop(far, HOP_OUT)
-    return [spread_plane(c) for c in (c0, c1, c2, own)]
+    return q3 + hop(q2, HOP_IN) + hop(p1, HOP_MID) + hop(p2, HOP_OUT), p2
 
 
 def is_cube(sizes):
@@ -502,6 +491,1095 @@
     )
 
 
+def split(v):
+    high = v.astype(jnp.bfloat16)
+    return high, (v - high.astype(jnp.float32)).astype(jnp.bfloat16)
+
+
+def split_outside(v):
+    high = lax.reduce_precision(v, exponent_bits=8, mantissa_bits=7)
+    return high.astype(jnp.bfloat16), (v - high).astype(jnp.bfloat16)
+
+
+def one_pass(left, right, dims=((1,), (0,))):
+    return lax.dot_general(left, right, (dims, ((), ())), preferred_element_type=jnp.float32)
+
+
+def three_pass(left, right, dims=((1,), (0,))):
+    lh, ll = left
+    rh, rl = right
+    return one_pass(lh, rh, dims) + (one_pass(lh, rl, dims) + one_pass(ll, rh, dims))
+
+
+NT = ((1,), (1,))
+
+
+def kernel_call(
+    body,
+    ins,
+    outs,
+    scratch,
+    late=None,
+    sent=None,
+    hbm=None,
+    smem=None,
+    hbm_out=None,
+    flops=0,
+    limit=60,
+):
+    late, sent, hbm, smem, hbm_out = late or {}, sent or {}, hbm or {}, smem or {}, hbm_out or {}
+    leaves, tree = jax.tree.flatten((ins, smem, hbm, late))
+    out_leaves, out_tree = jax.tree.flatten((outs, hbm_out, sent))
+    buffers = jax.tree.map(lambda v: pltpu.VMEM(v.shape, v.dtype), (late, sent))
+    late_count, sent_count = len(jax.tree.leaves(late)), len(jax.tree.leaves(sent))
+    own = (scratch, buffers)
+    own_leaves, own_tree = jax.tree.flatten(own)
+
+    def kernel(*refs):
+        n, m = len(leaves), len(leaves) + len(out_leaves)
+        given = jax.tree.unflatten(tree, refs[:n])
+        made = jax.tree.unflatten(out_tree, refs[n:m])
+        temps, (landed, leaving) = jax.tree.unflatten(own_tree, refs[m : m + len(own_leaves)])
+        sems = refs[m + len(own_leaves) :]
+        r = SimpleNamespace(
+            **given[0], **given[1], **given[2], **made[0], **made[1], **temps, **landed, **leaving
+        )
+        coming, going, started = {}, {}, []
+        index = 0
+        for name in sorted(late):
+            sources, targets = jax.tree.leaves(given[3][name]), jax.tree.leaves(landed[name])
+            coming[id(landed[name])] = []
+            for source, target in zip(sources, targets):
+                coming[id(landed[name])].append(
+                    pltpu.make_async_copy(source, target, sems[0].at[index])
+                )
+                index += 1
+        index = 0
+        for name in sorted(sent):
+            sources, targets = jax.tree.leaves(leaving[name]), jax.tree.leaves(made[2][name])
+            going[id(leaving[name])] = []
+            for source, target in zip(sources, targets):
+                going[id(leaving[name])].append(
+                    pltpu.make_async_copy(source, target, sems[1].at[index])
+                )
+                index += 1
+
+        def fetch(*items):
+            for item in items:
+                for copy in coming[id(item)]:
+                    copy.start()
+
+        def need(*items):
+            for item in items:
+                for copy in coming[id(item)]:
+                    copy.wait()
+
+        def send(*items):
+            for item in items:
+                for copy in going[id(item)]:
+                    copy.start()
+                    started.append(copy)
+
+        r.fetch, r.need, r.send = fetch, need, send
+        body(r)
+        for copy in started:
+            copy.wait()
+        assert len(started) == sent_count
+
+    vmem, hbm_spec = pl.BlockSpec(memory_space=pltpu.VMEM), pl.BlockSpec(memory_space=pl.ANY)
+    count = lambda v: len(jax.tree.leaves(v))
+    in_specs = [vmem] * count(ins) + [pl.BlockSpec(memory_space=pltpu.SMEM)] * count(smem)
+    in_specs += [hbm_spec] * (count(hbm) + count(late))
+    out_specs = [vmem] * count(outs) + [hbm_spec] * (count(hbm_out) + count(sent))
+    size = sum(v.size * v.dtype.itemsize for v in leaves + out_leaves)
+    result = pl.pallas_call(
+        kernel,
+        out_shape=out_leaves,
+        in_specs=in_specs,
+        out_specs=out_specs,
+        scratch_shapes=own_leaves
+        + [pltpu.SemaphoreType.DMA((max(late_count, 1),)), pltpu.SemaphoreType.DMA((max(sent_count, 1),))],
+        compiler_params=pltpu.CompilerParams(vmem_limit_bytes=limit * 2**20),
+        cost_estimate=pl.CostEstimate(flops=flops, bytes_accessed=size, transcendentals=0),
+    )(*leaves)
+    made = jax.tree.unflatten(out_tree, result)
+    return SimpleNamespace(**made[0], **made[1], **made[2])
+
+
+def f32(*shape):
+    return jax.ShapeDtypeStruct(shape, jnp.float32)
+
+
+def b16(*shape):
+    return jax.ShapeDtypeStruct(shape, jnp.bfloat16)
+
+
+def pair_of(*shape):
+    return (b16(*shape), b16(*shape))
+
+
+def pair(refs, rows=None):
+    high, low = refs
+    return (high[...], low[...]) if rows is None else (high[rows, :], low[rows, :])
+
+
+def put(refs, rows, value):
+    high, low = split(value)
+    refs[0][rows, :] = high
+    refs[1][rows, :] = low
+
+
+HALF = D // 2
+
+
+class Stream:
+    def __init__(self, r, sources):
+        self.r, self.sources, self.step = r, sources, 0
+        self.copies(0, True)
+
+    def copies(self, step, start):
+        rows = pl.ds((step % 2) * HALF, HALF)
+        refs, index = self.sources[step // 2]
+        for part, ref in enumerate(refs):
+            view = ref.at[rows, :] if index is None else ref.at[index, rows, :]
+            copy = pltpu.make_async_copy(
+                view, self.r.held.at[step % 2, part], self.r.arrived.at[step % 2, part]
+            )
+            copy.start() if start else copy.wait()
+
+    def product(self, right, store, extra=None):
+        held = self.r.held
+        for half in range(2):
+            step = self.step
+            self.step += 1
+            if step + 1 < 2 * len(self.sources):
+                self.copies(step + 1, True)
+            self.copies(step, False)
+            rows = pl.ds(half * HALF, HALF)
+            acc = three_pass((held[half, 0], held[half, 1]), pair(right))
+            if extra is not None:
+                acc = acc + three_pass(pair(extra[0], rows), extra[1])
+            store[rows, :] = acc
+
+
+def stream_scratch():
+    return dict(
+        held=pltpu.VMEM((2, 2, HALF, D), jnp.bfloat16),
+        arrived=pltpu.SemaphoreType.DMA((2, 2)),
+    )
+
+
+def each(body, carry=(), step=128, count=D):
+    def run(i, state):
+        return body(pl.ds(pl.multiple_of(i * step, step), step), *state)
+
+    return lax.fori_loop(0, count // step, run, carry)
+
+
+def fold(v):
+    return jnp.sum(v.reshape(v.shape[0] // 8, 8, v.shape[1]), axis=0)
+
+
+def planes(channels, edges, body):
+    lanes = edges // 128
+
+    def run(i, state):
+        base = pl.multiple_of((i // lanes) * 16, 16)
+        lane = pl.ds(pl.multiple_of((i % lanes) * 128, 128), 128)
+        body(base, lane)
+        return state
+
+    lax.fori_loop(0, (channels // 16) * lanes, run, 0)
+
+
+def get9(ref, channels, base, lane):
+    return [ref[pl.ds(k * channels + base, 16), lane] for k in range(9)]
+
+
+def put9(ref, channels, base, lane, values):
+    for k, v in enumerate(values):
+        ref[pl.ds(k * channels + base, 16), lane] = v
+
+
+def put9_split(r, channels, base, lane, values):
+    for k, v in enumerate(values):
+        high, low = split(v)
+        r.t_h[pl.ds(k * channels + base, 16), lane] = high
+        r.t_l[pl.ds(k * channels + base, 16), lane] = low
+
+
+def row9(ref, lane):
+    return [ref[k : k + 1, lane] for k in range(9)]
+
+
+def terms_sum(sets, out):
+    total = [None] * 9
+    pairs = {}
+    for index in TERMS:
+        for n, ((li, left), (ri, right)) in enumerate(sets):
+            key = (n, index[li], index[ri])
+            if key not in pairs:
+                pairs[key] = left[index[li]] * right[index[ri]]
+    for index in TERMS:
+        for n, ((li, left), (ri, right)) in enumerate(sets):
+            term = index[3] * pairs[(n, index[li], index[ri])]
+            slot = index[out]
+            total[slot] = term if total[slot] is None else total[slot] + term
+    return total
+
+
+TILE9 = 192
+
+
+def same_atom(r, scale, store, rows9):
+    @pl.loop(0, rows9 // TILE9)
+    def _(t):
+        rows = pl.ds(pl.multiple_of(t * TILE9, TILE9), TILE9)
+        store[rows, :] = scale * (
+            one_pass(r.t_h[rows, :], r.same[...]) + one_pass(r.t_l[rows, :], r.same[...])
+        )
+
+
+def mixed(r, mixing, store, rows9):
+    @pl.loop(0, rows9 // TILE9)
+    def _(t):
+        rows = pl.ds(pl.multiple_of(t * TILE9, TILE9), TILE9)
+        store[rows, :] = three_pass(pair(mixing, rows), (r.t_h[...], r.t_l[...]))
+
+
+def clear_tail(r, rows9):
+    tail = r.t_h.shape[0] - rows9
+    r.t_h[rows9:, :] = jnp.zeros((tail, r.t_h.shape[1]), jnp.bfloat16)
+    r.t_l[rows9:, :] = jnp.zeros((tail, r.t_l.shape[1]), jnp.bfloat16)
+
+
+def plane_scratch(rows9, edges):
+    depth = -(-rows9 // 128) * 128
+    return dict(
+        t_h=pltpu.VMEM((depth, edges), jnp.bfloat16), t_l=pltpu.VMEM((depth, edges), jnp.bfloat16)
+    )
+
+
+def sig(v):
+    return 1.0 / (1.0 + jnp.exp(-v))
+
+
+def silu_parts(v):
+    s = sig(v)
+    return v * s, s * (1.0 + v * (1.0 - s))
+
+
+def silu_slopes(v):
+    s = sig(v)
+    t = 1.0 - s
+    return s * (1.0 + v * t), s * t * (2.0 + v * (t - s))
+
+
+def first_layer(r, channels, edges, scale):
+    rows9 = 9 * channels
+    stream = Stream(r, [(r.out_t, None)])
+    feat = split(r.feat[...])
+
+    @pl.loop(0, 2)
+    def _(t):
+        rows = pl.ds(pl.multiple_of(t * 512, 512), 512)
+        r.pre0[rows, :] = three_pass(pair(r.in_t, rows), feat)
+
+    def hidden(rows):
+        put(r.hid, rows, silu_parts(r.pre0[rows, :])[0])
+        return ()
+
+    r.send(r.pre0)
+    each(hidden)
+    r.send(r.hid)
+    stream.product(r.hid, r.out0)
+
+    def latent(rows):
+        put(r.lat0, rows, r.rows[0:1, :] * r.out0[rows, :])
+        return ()
+
+    r.send(r.out0)
+    each(latent)
+    r.send(r.lat0)
+    r.w0[...] = three_pass(pair(r.env0w), pair(r.lat0))
+
+    def embed(base, lane):
+        w = r.w0[pl.ds(base, 16), lane]
+        put9_split(r, channels, base, lane, [y * w for y in row9(r.shape, lane)])
+
+    planes(channels, edges, embed)
+    same_atom(r, scale, r.env0, rows9)
+    r.send(r.env0)
+
+    def multiply(base, lane):
+        w = r.w0[pl.ds(base, 16), lane]
+        emb = [y * w for y in row9(r.shape, lane)]
+        env = get9(r.env0, channels, base, lane)
+        put9(r.res0, channels, base, lane, terms_sum([((0, emb), (1, env))], 2))
+
+    planes(channels, edges, multiply)
+    r.send(r.res0)
+
+
+def energy_up(r, channels, edges, scale):
+    rows9 = 9 * channels
+    env, factor = lambda: r.rows[0:1, :], lambda: r.rows[1:2, :]
+    alpha = lambda: RES * r.rows[0:1, :] * r.rows[1:2, :]
+    stream = Stream(
+        r,
+        [
+            (r.mt, 0),
+            (r.mt, 1),
+            (r.mt, 2),
+        ],
+    )
+    r.fetch(r.out0, r.mix)
+    clear_tail(r, rows9)
+    nothing = jnp.zeros((8, edges), jnp.float32)
+    stream.product(r.lat0, r.pre1, (r.sc0_t, split(r.res0[0:channels, :])))
+
+    def act1(rows):
+        put(r.act1, rows, silu_parts(r.pre1[rows, :])[0])
+        return ()
+
+    r.send(r.pre1)
+    each(act1)
+    r.send(r.act1)
+    stream.product(r.act1, r.out1)
+
+    def lat1(rows, per):
+        value = RES * env() * (r.out0[rows, :] + r.out1[rows, :])
+        put(r.lat1, rows, value)
+        return (per + fold(value * r.head[rows, :]),)
+
+    r.send(r.out1)
+    r.need(r.out0)
+    (per1,) = each(lat1, (nothing,))
+    r.send(r.lat1)
+    r.w1[...] = three_pass(pair(r.env1w), pair(r.lat1))
+
+    def embed(base, lane):
+        w = r.w1[pl.ds(base, 16), lane]
+        put9_split(r, channels, base, lane, [y * w for y in row9(r.shape, lane)])
+
+    planes(channels, edges, embed)
+    same_atom(r, scale, r.env1, rows9)
+    r.send(r.env1)
+
+    def take(base, lane):
+        put9_split(r, channels, base, lane, get9(r.res0, channels, base, lane))
+
+    planes(channels, edges, take)
+    r.need(r.mix)
+    mixed(r, r.mix, r.feat1, rows9)
+    r.send(r.feat1)
+
+    def scalar(base, lane):
+        f, e = get9(r.feat1, channels, base, lane), get9(r.env1, channels, base, lane)
+        r.res1[pl.ds(base, 16), lane] = sum(a * b for a, b in zip(f, e)) * (1.0 / 3.0)
+
+    planes(channels, edges, scalar)
+    stream.product(r.lat1, r.pre2, (r.sc1_t, split(r.res1[...])))
+
+    def act2(rows, per):
+        act, slope = silu_parts(r.pre2[rows, :])
+        put(r.pre2_bar, rows, (alpha() * env()) * r.top[rows, :] * slope)
+        return (per + fold(act * r.top[rows, :]),)
+
+    r.send(r.pre2)
+    (per2,) = each(act2, (nothing,))
+    r.send(r.pre2_bar)
+    per1 = jnp.sum(per1, axis=0, keepdims=True)
+    per2 = jnp.sum(per2, axis=0, keepdims=True)
+    r.per[...] = jnp.zeros_like(r.per)
+    r.per[0:1, :] = per1
+    r.per[1:2, :] = per2
+
+
+def energy_down(r, channels, edges, scale):
+    rows9 = 9 * channels
+    env, factor = lambda: r.rows[0:1, :], lambda: r.rows[1:2, :]
+    alpha = lambda: RES * r.rows[0:1, :] * r.rows[1:2, :]
+    stream = Stream(r, [(r.m, 2), (r.m, 1), (r.m, 0), (r.out, None)])
+    r.fetch(r.feat1, r.env1)
+    clear_tail(r, rows9)
+    nothing = jnp.zeros((8, edges), jnp.float32)
+    stream.product(r.pre2_bar, r.lat1_bar)
+    r.fetch(r.out1, r.mix_t, r.pre1)
+    r.need(r.feat1, r.env1)
+    r.res1_bar[...] = three_pass(pair(r.sc1), pair(r.pre2_bar))
+
+    def back1(base, lane):
+        g = r.res1_bar[pl.ds(base, 16), lane] * (1.0 / 3.0)
+        put9_split(r, channels, base, lane, [g * f for f in get9(r.feat1, channels, base, lane)])
+        put9(r.feat1_bar, channels, base, lane, [g * e for e in get9(r.env1, channels, base, lane)])
+
+    planes(channels, edges, back1)
+    r.send(r.feat1_bar)
+    same_atom(r, scale, r.emb1_bar, rows9)
+    r.send(r.emb1_bar)
+    r.shape_bar[...] = jnp.zeros_like(r.shape_bar)
+
+    def collect(w_ref, emb_ref, out_ref):
+        def run(base, lane):
+            w = w_ref[pl.ds(base, 16), lane]
+            emb = get9(emb_ref, channels, base, lane)
+            out_ref[pl.ds(base, 16), lane] = sum(y * v for y, v in zip(row9(r.shape, lane), emb))
+            for k in range(9):
+                r.shape_bar[k : k + 1, lane] += jnp.sum(emb[k] * w, axis=0, keepdims=True)
+
+        planes(channels, edges, run)
+
+    collect(r.w1, r.emb1_bar, r.w1_bar)
+    w_pair = split(r.w1_bar[...])
+
+    @pl.loop(0, 2)
+    def _(t):
+        rows = pl.ds(pl.multiple_of(t * 512, 512), 512)
+        r.lat1_bar[rows, :] += three_pass(pair(r.env1w_t, rows), w_pair)
+
+    def out1_bar(rows, total):
+        value = r.lat1_bar[rows, :] + alpha() * r.head[rows, :]
+        r.lat1_bar[rows, :] = value
+        put(r.out1_bar, rows, (RES * env()) * value)
+        return (total + fold(value * r.out1[rows, :]),)
+
+    r.need(r.out1)
+    (env_bar1,) = each(out1_bar, (nothing,))
+    r.send(r.lat1_bar, r.out1_bar)
+    r.fetch(r.env0, r.out0)
+    stream.product(r.out1_bar, r.act1_bar)
+    r.send(r.act1_bar)
+    r.need(r.mix_t)
+
+    def take_bar(base, lane):
+        put9_split(r, channels, base, lane, get9(r.feat1_bar, channels, base, lane))
+
+    planes(channels, edges, take_bar)
+    mixed(r, r.mix_t, r.res0_bar, rows9)
+
+    def pre1_bar(rows):
+        put(r.pre1_bar, rows, r.act1_bar[rows, :] * silu_parts(r.pre1[rows, :])[1])
+        return ()
+
+    r.need(r.pre1)
+    each(pre1_bar)
+    r.send(r.pre1_bar)
+    stream.product(r.pre1_bar, r.lat0_bar)
+    r.res0_bar[0:channels, :] += three_pass(pair(r.sc0), pair(r.pre1_bar))
+    r.send(r.res0_bar)
+    r.fetch(r.pre0)
+
+    def back0(base, lane):
+        w = r.w0[pl.ds(base, 16), lane]
+        emb = [y * w for y in row9(r.shape, lane)]
+        g = get9(r.res0_bar, channels, base, lane)
+        put9_split(r, channels, base, lane, terms_sum([((2, g), (0, emb))], 1))
+
+    planes(channels, edges, back0)
+    same_atom(r, scale, r.emb0_bar, rows9)
+
+    def back0_feature(base, lane):
+        g = get9(r.res0_bar, channels, base, lane)
+        e = get9(r.env0, channels, base, lane)
+        more = terms_sum([((2, g), (1, e))], 0)
+        have = get9(r.emb0_bar, channels, base, lane)
+        put9(r.emb0_bar, channels, base, lane, [a + b for a, b in zip(have, more)])
+
+    r.need(r.env0)
+    planes(channels, edges, back0_feature)
+    r.send(r.emb0_bar)
+    collect(r.w0, r.emb0_bar, r.w0_bar)
+    w_pair0 = split(r.w0_bar[...])
+
+    @pl.loop(0, 2)
+    def _(t):
+        rows = pl.ds(pl.multiple_of(t * 512, 512), 512)
+        r.lat0_bar[rows, :] += three_pass(pair(r.env0w_t, rows), w_pair0)
+
+    def out0_bar(rows, total):
+        value = r.lat0_bar[rows, :] + RES * r.lat1_bar[rows, :]
+        r.lat0_bar[rows, :] = value
+        put(r.out0_bar, rows, env() * value)
+        return (total + fold(value * r.out0[rows, :]),)
+
+    r.need(r.out0)
+    (env_bar0,) = each(out0_bar, (nothing,))
+    r.send(r.lat0_bar, r.out0_bar)
+    stream.product(r.out0_bar, r.hid_bar)
+
+    def pre0_bar(rows):
+        put(r.pre0_bar, rows, r.hid_bar[rows, :] * silu_parts(r.pre0[rows, :])[1])
+        return ()
+
+    r.send(r.hid_bar)
+    r.need(r.pre0)
+    each(pre0_bar)
+    r.send(r.pre0_bar)
+    r.bessel_bar[...] = three_pass(pair(r.in_w), pair(r.pre0_bar))
+    down = lambda v: jnp.sum(v, axis=0, keepdims=True)
+    r.env_bar[...] = jnp.zeros_like(r.env_bar)
+    r.env_bar[0:1, :] = (
+        RES * factor() * (r.per[0:1, :] + 2.0 * env() * r.per[1:2, :])
+        + RES * down(env_bar1)
+        + down(env_bar0)
+    )
+
+
+def tangent_up(r, channels, edges, scale):
+    rows9 = 9 * channels
+    env, factor, env_dot = (
+        lambda: r.rows[0:1, :],
+        lambda: r.rows[1:2, :],
+        lambda: r.rows[2:3, :],
+    )
+    lead = lambda: RES * env() * env() * factor()
+    lead_dot = lambda: 2.0 * RES * env() * factor() * env_dot()
+    stream = Stream(
+        r,
+        [
+            (r.out_t, None),
+            (r.mt, 0),
+            (r.mt, 1),
+            (r.mt, 2),
+        ],
+    )
+    r.fetch(r.pre0, r.out0)
+    clear_tail(r, rows9)
+    nothing = jnp.zeros((8, edges), jnp.float32)
+    bessel = split(r.bessel_dot[...])
+
+    @pl.loop(0, 2)
+    def _(t):
+        rows = pl.ds(pl.multiple_of(t * 512, 512), 512)
+        r.pre0_dot[rows, :] = three_pass(pair(r.in_t, rows), bessel)
+
+    def hidden(rows):
+        put(r.hid_dot, rows, r.pre0_dot[rows, :] * silu_parts(r.pre0[rows, :])[1])
+        return ()
+
+    r.send(r.pre0_dot)
+    r.need(r.pre0)
+    each(hidden)
+    r.send(r.hid_dot)
+    r.fetch(r.env0)
+    stream.product(r.hid_dot, r.tmp)
+
+    def lat0(rows):
+        value = env_dot() * r.out0[rows, :] + env() * r.tmp[rows, :]
+        r.keep[rows, :] = value
+        put(r.lat0_dot, rows, value)
+        return ()
+
+    r.need(r.out0)
+    each(lat0)
+    r.send(r.lat0_dot)
+    r.fetch(r.pre1, r.out1)
+    r.w0_dot[...] = three_pass(pair(r.env0w), pair(r.lat0_dot))
+
+    def embed_dot(w_ref, w_dot_ref, base, lane):
+        w, wd = w_ref[pl.ds(base, 16), lane], w_dot_ref[pl.ds(base, 16), lane]
+        return [
+            yd * w + y * wd for y, yd in zip(row9(r.shape, lane), row9(r.shape_dot, lane))
+        ]
+
+    def embed0(base, lane):
+        put9_split(r, channels, base, lane, embed_dot(r.w0, r.w0_dot, base, lane))
+
+    planes(channels, edges, embed0)
+    same_atom(r, scale, r.env0_dot, rows9)
+    r.send(r.env0_dot)
+    r.need(r.env0)
+
+    def multiply(base, lane):
+        w = r.w0[pl.ds(base, 16), lane]
+        emb = [y * w for y in row9(r.shape, lane)]
+        emb_dot = embed_dot(r.w0, r.w0_dot, base, lane)
+        e, ed = get9(r.env0, channels, base, lane), get9(r.env0_dot, channels, base, lane)
+        put9(
+            r.res0_dot,
+            channels,
+            base,
+            lane,
+            terms_sum([((0, emb_dot), (1, e)), ((0, emb), (1, ed))], 2),
+        )
+
+    planes(channels, edges, multiply)
+    r.send(r.res0_dot)
+    r.fetch(r.lat1, r.mix)
+    stream.product(r.lat0_dot, r.pre1_dot, (r.sc0_t, split(r.res0_dot[0:channels, :])))
+
+    def act1(rows):
+        put(r.act1_dot, rows, r.pre1_dot[rows, :] * silu_parts(r.pre1[rows, :])[1])
+        return ()
+
+    r.send(r.pre1_dot)
+    r.need(r.pre1)
+    each(act1)
+    r.send(r.act1_dot)
+    r.fetch(r.feat1, r.env1, r.pre2)
+    stream.product(r.act1_dot, r.tmp)
+
+    def lat1(rows, per):
+        value = RES * (
+            r.keep[rows, :] + env_dot() * r.out1[rows, :] + env() * r.tmp[rows, :]
+        )
+        put(r.lat1_dot, rows, value)
+        lat = r.lat1[0][rows, :].astype(jnp.float32) + r.lat1[1][rows, :].astype(jnp.float32)
+        part = factor() * (env_dot() * lat + env() * value)
+        r.head_part[rows, :] = sum(part[:, s : s + 128] for s in range(0, edges, 128))
+        return (per + fold(value * r.head[rows, :]),)
+
+    r.need(r.out1, r.lat1)
+    (per1,) = each(lat1, (nothing,))
+    r.send(r.lat1_dot)
+    r.w1_dot[...] = three_pass(pair(r.env1w), pair(r.lat1_dot))
+
+    def embed1(base, lane):
+        put9_split(r, channels, base, lane, embed_dot(r.w1, r.w1_dot, base, lane))
+
+    planes(channels, edges, embed1)
+    same_atom(r, scale, r.env1_dot, rows9)
+    r.send(r.env1_dot)
+    r.need(r.mix)
+
+    def take(base, lane):
+        put9_split(r, channels, base, lane, get9(r.res0_dot, channels, base, lane))
+
+    planes(channels, edges, take)
+    mixed(r, r.mix, r.feat1_dot, rows9)
+    r.send(r.feat1_dot)
+    r.need(r.feat1, r.env1)
+
+    def scalar(base, lane):
+        f, fd = get9(r.feat1, channels, base, lane), get9(r.feat1_dot, channels, base, lane)
+        e, ed = get9(r.env1, channels, base, lane), get9(r.env1_dot, channels, base, lane)
+        total = sum(fd[k] * e[k] + f[k] * ed[k] for k in range(9))
+        r.res1_dot[pl.ds(base, 16), lane] = total * (1.0 / 3.0)
+
+    planes(channels, edges, scalar)
+    stream.product(r.lat1_dot, r.tmp, (r.sc1_t, split(r.res1_dot[...])))
+
+    def act2(rows, per):
+        v, vd, top = r.pre2[rows, :], r.tmp[rows, :], r.top[rows, :]
+        s = sig(v)
+        t = 1.0 - s
+        slope, curve = s * (1.0 + v * t), s * t * (2.0 + v * (t - s))
+        act_dot = slope * vd
+        part = lead_dot() * (v * s) + lead() * act_dot
+        r.last_part[rows, :] = sum(part[:, k : k + 128] for k in range(0, edges, 128))
+        put(r.pre2_hat, rows, top * (lead_dot() * slope + lead() * curve * vd))
+        return (per + fold(act_dot * top),)
+
+    r.need(r.pre2)
+    (per2,) = each(act2, (nothing,))
+    r.send(r.pre2_hat)
+    r.per_dot[...] = jnp.zeros_like(r.per_dot)
+    r.per_dot[0:1, :] = jnp.sum(per1, axis=0, keepdims=True)
+    r.per_dot[1:2, :] = jnp.sum(per2, axis=0, keepdims=True)
+
+
+def tangent_down(r, channels, edges, scale):
+    rows9 = 9 * channels
+    env, factor, env_dot = (
+        lambda: r.rows[0:1, :],
+        lambda: r.rows[1:2, :],
+        lambda: r.rows[2:3, :],
+    )
+    stream = Stream(
+        r,
+        [
+            (r.m, 2),
+            (r.m, 1),
+            (r.m, 0),
+            (r.out, None),
+        ],
+    )
+    r.fetch(r.feat1, r.feat1_dot, r.env1, r.env1_dot)
+    clear_tail(r, rows9)
+    stream.product(r.pre2_hat, r.hat1)
+    r.fetch(r.emb1_bar, r.lat1_bar)
+    r.need(r.feat1, r.feat1_dot, r.env1, r.env1_dot)
+    r.small[...] = three_pass(pair(r.sc1), pair(r.pre2_hat))
+
+    def back1(base, lane):
+        gh = r.small[pl.ds(base, 16), lane] * (1.0 / 3.0)
+        g = r.res1_bar[pl.ds(base, 16), lane] * (1.0 / 3.0)
+        f, fd = get9(r.feat1, channels, base, lane), get9(r.feat1_dot, channels, base, lane)
+        e, ed = get9(r.env1, channels, base, lane), get9(r.env1_dot, channels, base, lane)
+        put9_split(r, channels, base, lane, [gh * f[k] + g * fd[k] for k in range(9)])
+        put9(r.feat1_hat, channels, base, lane, [gh * e[k] + g * ed[k] for k in range(9)])
+
+    planes(channels, edges, back1)
+    r.send(r.feat1_hat)
+    r.fetch(r.mix_t, r.pre1, r.act1_bar, r.pre1_dot)
+    same_atom(r, scale, r.plane, rows9)
+
+    def collect(bar_ref, out_ref):
+        def run(base, lane):
+            bar = get9(bar_ref, channels, base, lane)
+            hat = get9(r.plane, channels, base, lane)
+            y, yd = row9(r.shape, lane), row9(r.shape_dot, lane)
+            out_ref[pl.ds(base, 16), lane] = sum(
+                yd[k] * bar[k] + y[k] * hat[k] for k in range(9)
+            )
+
+        planes(channels, edges, run)
+
+    r.need(r.emb1_bar)
+    collect(r.emb1_bar, r.w1_hat)
+    w_pair = split(r.w1_hat[...])
+
+    @pl.loop(0, 2)
+    def _(t):
+        rows = pl.ds(pl.multiple_of(t * 512, 512), 512)
+        r.hat1[rows, :] += three_pass(pair(r.env1w_t, rows), w_pair)
+
+    def out1(rows):
+        value = r.hat1[rows, :] + (RES * factor() * env_dot()) * r.head[rows, :]
+        r.hat1[rows, :] = value
+        put(r.out1_hat, rows, RES * (env_dot() * r.lat1_bar[rows, :] + env() * value))
+        return ()
+
+    r.need(r.lat1_bar)
+    each(out1)
+    r.send(r.out1_hat)
+    r.fetch(r.res0_bar, r.env0, r.env0_dot)
+    stream.product(r.out1_hat, r.tmp)
+    r.need(r.mix_t)
+
+    def take(base, lane):
+        put9_split(r, channels, base, lane, get9(r.feat1_hat, channels, base, lane))
+
+    planes(channels, edges, take)
+    mixed(r, r.mix_t, r.res0_hat, rows9)
+
+    def pre1(rows):
+        slope, curve = silu_slopes(r.pre1[rows, :])
+        put(
+            r.pre1_hat,
+            rows,
+            r.tmp[rows, :] * slope + r.act1_bar[rows, :] * curve * r.pre1_dot[rows, :],
+        )
+        return ()
+
+    r.need(r.pre1, r.act1_bar, r.pre1_dot)
+    each(pre1)
+    r.send(r.pre1_hat)
+    r.fetch(r.emb0_bar, r.lat0_bar)
+    stream.product(r.pre1_hat, r.tmp)
+    r.res0_hat[0:channels, :] += three_pass(pair(r.sc0), pair(r.pre1_hat))
+
+    def embed_pair(base, lane):
+        w, wd = r.w0[pl.ds(base, 16), lane], r.w0_dot[pl.ds(base, 16), lane]
+        y, yd = row9(r.shape, lane), row9(r.shape_dot, lane)
+        emb = [a * w for a in y]
+        emb_dot = [b * w + a * wd for a, b in zip(y, yd)]
+        return emb, emb_dot
+
+    def back0(base, lane):
+        emb, emb_dot = embed_pair(base, lane)
+        gh, g = get9(r.res0_hat, channels, base, lane), get9(r.res0_bar, channels, base, lane)
+        put9_split(
+            r, channels, base, lane, terms_sum([((2, gh), (0, emb)), ((2, g), (0, emb_dot))], 1)
+        )
+
+    r.need(r.res0_bar)
+    planes(channels, edges, back0)
+    r.fetch(r.pre0, r.hid_bar, r.pre0_dot)
+    same_atom(r, scale, r.plane, rows9)
+
+    def back0_feature(base, lane):
+        gh, g = get9(r.res0_hat, channels, base, lane), get9(r.res0_bar, channels, base, lane)
+        e, ed = get9(r.env0, channels, base, lane), get9(r.env0_dot, channels, base, lane)
+        more = terms_sum([((2, gh), (1, e)), ((2, g), (1, ed))], 0)
+        have = get9(r.plane, channels, base, lane)
+        put9(r.plane, channels, base, lane, [a + b for a, b in zip(have, more)])
+
+    r.need(r.env0, r.env0_dot)
+    planes(channels, edges, back0_feature)
+    r.need(r.emb0_bar)
+    collect(r.emb0_bar, r.w0_hat)
+    w_pair0 = split(r.w0_hat[...])
+
+    @pl.loop(0, 2)
+    def _(t):
+        rows = pl.ds(pl.multiple_of(t * 512, 512), 512)
+        r.tmp[rows, :] += three_pass(pair(r.env0w_t, rows), w_pair0)
+
+    def out0(rows):
+        value = r.tmp[rows, :] + RES * r.hat1[rows, :]
+        put(r.out0_hat, rows, env_dot() * r.lat0_bar[rows, :] + env() * value)
+        return ()
+
+    r.need(r.lat0_bar)
+    each(out0)
+    r.send(r.out0_hat)
+    stream.product(r.out0_hat, r.tmp)
+
+    def pre0(rows):
+        slope, curve = silu_slopes(r.pre0[rows, :])
+        put(
+            r.pre0_hat,
+            rows,
+            r.tmp[rows, :] * slope + r.hid_bar[rows, :] * curve * r.pre0_dot[rows, :],
+        )
+        return ()
+
+    r.need(r.pre0, r.hid_bar, r.pre0_dot)
+    each(pre0)
+    r.send(r.pre0_hat)
+
+
+def small_gradients(r, channels, edges):
+    r.fetch(r.hid, r.out0_hat, r.pre0_bar, r.pre0_hat)
+    tiles = [pl.ds(t * HALF, HALF) for t in range(2)]
+    for rows in tiles:
+        r.out_grad[rows, :] = three_pass(pair(r.hid_dot, rows), pair(r.out0_bar), NT)
+    r.need(r.hid, r.out0_hat)
+    for rows in tiles:
+        r.out_grad[rows, :] += three_pass(pair(r.hid, rows), pair(r.out0_hat), NT)
+    r.send(r.out_grad)
+    r.need(r.pre0_bar, r.pre0_hat)
+    r.fetch(r.feat1_bar, r.res0_dot, r.feat1_hat, r.res0)
+    r.in_grad[...] = three_pass(split(r.bessel_dot[...]), pair(r.pre0_bar), NT) + three_pass(
+        split(r.feat[...]), pair(r.pre0_hat), NT
+    )
+    r.fetch(r.lat0_dot, r.lat0, r.pre1_bar, r.pre1_hat)
+
+    def twice(first, second, third, fourth):
+        return three_pass(split(first), pair(second), NT) + three_pass(split(third), pair(fourth), NT)
+
+    r.need(r.feat1_bar, r.res0_dot, r.feat1_hat, r.res0)
+    r.fetch(r.lat1_dot, r.lat1, r.pre2_bar, r.pre2_hat)
+    r.need(r.lat0_dot, r.lat0, r.pre1_bar, r.pre1_hat)
+    r.env_grad[0] = twice(r.w0_bar[...], r.lat0_dot, r.w0_hat[...], r.lat0)
+    r.sc_grad[0] = twice(r.res0_dot[0:channels, :], r.pre1_bar, r.res0[0:channels, :], r.pre1_hat)
+    r.need(r.lat1_dot, r.lat1, r.pre2_bar, r.pre2_hat)
+    r.env_grad[1] = twice(r.w1_bar[...], r.lat1_dot, r.w1_hat[...], r.lat1)
+    r.sc_grad[1] = twice(r.res1_dot[...], r.pre2_bar, r.res1[...], r.pre2_hat)
+    for order, (start, stop) in enumerate(((0, 1), (1, 4), (4, 9))):
+        total = None
+        for k in range(start, stop):
+            part = slice(k * channels, (k + 1) * channels)
+            term = three_pass(split(r.feat1_bar[part, :]), split(r.res0_dot[part, :]), NT)
+            term = term + three_pass(split(r.feat1_hat[part, :]), split(r.res0[part, :]), NT)
+            total = term if total is None else total + term
+        r.mix_grad[order] = total
+
+
+def load_blocks(r):
+    depth = 3
+
+    def incoming(step):
+        slot = lax.rem(step, depth)
+        return [
+            pltpu.make_async_copy(
+                r.piece.at[r.where[step * SIDE + j]], r.blocks.at[slot, j], r.sem.at[slot, j]
+            )
+            for j in range(SIDE)
+        ]
+
+    def outgoing(step):
+        slot, m, i = step % 2, step // SIDE, step % SIDE
+        rows = pl.ds(pl.multiple_of(i * BS, BS), BS)
+        plain = [
+            pltpu.make_async_copy(
+                r.flat.at[slot, part], r.m[part].at[m, rows, :], r.out_sem.at[slot, part]
+            )
+            for part in range(2)
+        ]
+        turned = [
+            pltpu.make_async_copy(
+                r.turned.at[slot, part], r.mt[part].at[m, :, rows], r.out_sem.at[slot, 2 + part]
+            )
+            for part in range(2)
+        ]
+        return plain + turned
+
+    steps = 3 * SIDE
+    for step in range(depth - 1):
+        for copy in incoming(step):
+            copy.start()
+    eye = (
+        lax.broadcasted_iota(jnp.int32, (BS, BS), 0) == lax.broadcasted_iota(jnp.int32, (BS, BS), 1)
+    ).astype(jnp.bfloat16)
+
+    @pl.loop(0, steps)
+    def _(step):
+        @pl.when(step + depth - 1 < steps)
+        def _():
+            for copy in incoming(step + depth - 1):
+                copy.start()
+
+        for copy in incoming(step):
+            copy.wait()
+
+        @pl.when(step >= 2)
+        def _():
+            for copy in outgoing(step - 2):
+                copy.wait()
+
+        slot, source = step % 2, lax.rem(step, depth)
+        for j in range(SIDE):
+            part = slice(j * BS, (j + 1) * BS)
+            high, low = split(r.blocks[source, j])
+            r.flat[slot, 0, :, part] = high
+            r.flat[slot, 1, :, part] = low
+            r.turned[slot, 0, part, :] = one_pass(eye, high, NT).astype(jnp.bfloat16)
+            r.turned[slot, 1, part, :] = one_pass(eye, low, NT).astype(jnp.bfloat16)
+        for copy in outgoing(step):
+            copy.start()
+
+    def last(i):
+        return [
+            pltpu.make_async_copy(
+                r.piece.at[r.where[(3 * SIDE + i) * SIDE + j]],
+                r.last.at[pl.ds(i * BS, BS), pl.ds(j * BS, BS)],
+                r.last_sem.at[i, j],
+            )
+            for j in range(SIDE)
+        ]
+
+    for i in range(SIDE):
+        for copy in last(i):
+            copy.start()
+    for step in (steps - 2, steps - 1):
+        for copy in outgoing(step):
+            copy.wait()
+    head = r.head[...]
+    for i in range(SIDE):
+        for copy in last(i):
+            copy.wait()
+
+    def top(rows):
+        r.top[rows, :] = jnp.sum(r.last[rows, :] * head, axis=1, keepdims=True)
+        return ()
+
+    each(top)
+
+
+def block_gradients(r, channels, edges, targets):
+    names = [(r.lat0_dot, r.lat0, r.pre1_bar, r.pre1_hat)]
+    names.append((r.act1_dot, r.act1, r.out1_bar, r.out1_hat))
+    names.append((r.lat1_dot, r.lat1, r.pre2_bar, r.pre2_hat))
+    tile = HALF
+    count = tile // BS * SIDE
+
+    def incoming(m):
+        return [
+            pltpu.make_async_copy(ref, r.held.at[m % 2, a, part], r.arrived.at[m % 2, a, part])
+            for a, refs in enumerate(names[m])
+            for part, ref in enumerate(refs)
+        ]
+
+    for copy in incoming(0):
+        copy.start()
+
+    def spot(q):
+        rows = pl.ds(pl.multiple_of((q // SIDE) * BS, BS), BS)
+        return rows, pl.ds(pl.multiple_of((q % SIDE) * BS, BS), BS)
+
+    def wait_tile(slot):
+        whole = r.out[0].at[pl.ds(0, count)]
+        pltpu.make_async_copy(whole, whole, r.sent_sem.at[slot]).wait()
+
+    def send_tile(first, slot):
+        def one(q, state):
+            which, where = r.which[first + q], r.where[first + q]
+            for n in range(targets):
+
+                @pl.when(which == n)
+                def _(n=n):
+                    pltpu.make_async_copy(
+                        r.stage.at[slot, *spot(q)], r.out[n].at[where], r.sent_sem.at[slot]
+                    ).start()
+
+            return state
+
+        lax.fori_loop(0, count, one, 0)
+
+    for m in (3, 0, 1, 2):
+        if m < 3:
+            if m + 1 < 3:
+                for copy in incoming(m + 1):
+                    copy.start()
+            for copy in incoming(m):
+                copy.wait()
+            held = lambda a, which=slice(None): (
+                r.held[m % 2, a, 0, which, :],
+                r.held[m % 2, a, 1, which, :],
+            )
+        for t in range(2):
+            if m != 3:
+                wait_tile(t)
+            rows = pl.ds(t * tile, tile)
+            if m < 3:
+                r.stage[t] = three_pass(held(0, rows), held(2), NT) + three_pass(
+                    held(1, rows), held(3), NT
+                )
+            else:
+                r.stage[t] = r.lead[rows, :] * r.head[...]
+            send_tile((m * SIDE + t * (tile // BS)) * SIDE, t)
+    wait_tile(0)
+    wait_tile(1)
+
+
+def soap_kernel(count, *refs):
+    grad, weight, first, second, left, right, lstat, rstat, average = refs[:9]
+    outs = refs[9:]
+    tn_dims = ((0,), (0,))
+
+    def mm(a, b, dims=((1,), (0,))):
+        return [three_pass(split(x), split(y), dims) for x, y in zip(a, b)]
+
+    load = lambda ref: [ref[s] for s in range(count)]
+    g, l, rr = load(grad), load(left), load(right)
+    rotated = mm(mm(l, g, tn_dims), rr)
+    first_new = [0.9 * first[s] + 0.1 * rotated[s] for s in range(count)]
+    second_new = [0.99 * second[s] + 0.01 * rotated[s] * rotated[s] for s in range(count)]
+    normal = [
+        a * (1.0 / (1.0 - 0.9**ADAM_STEP)) / (jnp.sqrt(b * (1.0 / (1.0 - 0.99**ADAM_STEP))) + 1e-08)
+        for a, b in zip(first_new, second_new)
+    ]
+    step = mm(mm(l, normal), rr, NT)
+    for s in range(count):
+        new = weight[s] - 0.01 * (step[s] + 0.01 * weight[s])
+        outs[0][s] = new
+        outs[7][s] = 0.99 * average[s] + 0.01 * new
+        outs[2][s] = second_new[s]
+    plain = mm(mm(l, first_new), rr, NT)
+    ls = [0.95 * lstat[s] + 0.05 * v for s, v in enumerate(mm(g, g, NT))]
+    rs = [0.95 * rstat[s] + 0.05 * v for s, v in enumerate(mm(g, g, tn_dims))]
+    for s in range(count):
+        outs[5][s] = ls[s]
+        outs[6][s] = rs[s]
+    x = mm(ls, l) + mm(rs, rr)
+    x = [v / jnp.sqrt(jnp.sum(v * v)) for v in x]
+    for _ in range(NS_STEPS):
+        x = [1.5 * a - 0.5 * b for a, b in zip(x, mm(mm(x, x, NT), x))]
+    ln, rn = x[:count], x[count:]
+    out = mm(mm(ln, plain, tn_dims), rn)
+    for s in range(count):
+        outs[3][s] = ln[s]
+        outs[4][s] = rn[s]
+        outs[1][s] = out[s]
+
+
+def soap_update(arrays):
+    slots = arrays[0].shape[0]
+    count = 2 if slots % 2 == 0 else 1
+    spec = pl.BlockSpec((count, BS, BS), lambda s: (s, 0, 0))
+    return pl.pallas_call(
+        partial(soap_kernel, count),
+        grid=(slots // count,),
+        out_shape=[f32(slots, BS, BS)] * 8,
+        in_specs=[spec] * 9,
+        out_specs=[spec] * 8,
+        compiler_params=pltpu.CompilerParams(vmem_limit_bytes=40 * 2**20),
+    )(*arrays)
+
+
 def adamw(weight, first, second, grad):
     first_new = 0.9 * first + 0.1 * grad
     second_new = 0.99 * second + 0.01 * grad * grad
@@ -513,59 +1591,6 @@
     return (weight - 0.01 * (normal + 0.01 * weight), first_new, second_new)
 
 
-def orthogonalize(matrix):
-    current = matrix / jnp.sqrt(jnp.sum(matrix * matrix))
-    for step_no in range(NS_STEPS):
-        current = 1.5 * current - 0.5 * nn(nt(current, current), current)
-    return current
-
-
-def soap_slot(grad, weight, first, second, left, right, lstat, rstat, average):
-    rotated = nn(tn(left, grad), right)
-    first_new = 0.9 * first + 0.1 * rotated
-    second_new = 0.99 * second + 0.01 * rotated * rotated
-    normal = (
-        first_new
-        / (1.0 - 0.9**ADAM_STEP)
-        / (jnp.sqrt(second_new / (1.0 - 0.99**ADAM_STEP)) + 1e-08)
-    )
-    weight_new = weight - 0.01 * (nt(nn(left, normal), right) + 0.01 * weight)
-    lstat_new = 0.95 * lstat + 0.05 * nt(grad, grad)
-    rstat_new = 0.95 * rstat + 0.05 * tn(grad, grad)
-    left_new = orthogonalize(nn(lstat_new, left))
-    right_new = orthogonalize(nn(rstat_new, right))
-    plain = nt(nn(left, first_new), right)
-    first_out = nn(tn(left_new, plain), right_new)
-    average_new = 0.99 * average + 0.01 * weight_new
-    return (
-        weight_new,
-        first_out,
-        second_new,
-        left_new,
-        right_new,
-        lstat_new,
-        rstat_new,
-        average_new,
-    )
-
-
-def gather_blocks(soap_weight, block_owner, sizes):
-    inverse = jnp.zeros_like(block_owner).at[block_owner].set(
-        jnp.arange(block_owner.shape[0], dtype=jnp.int32)
-    )
-    if not is_cube(sizes):
-        return lax.all_gather(soap_weight, AX, axis=0, tiled=True)[inverse]
-    per = soap_weight.shape[0]
-    pieces = []
-    for piece in spread_chips(soap_weight):
-        pieces.append(jnp.stack([piece, hop(piece, HOP_CORE)], axis=2))
-    every = jnp.concatenate(pieces, axis=0).reshape((-1,) + soap_weight.shape[1:])
-    where = jnp.zeros((32,), jnp.int32).at[relative_devices().reshape(-1)].set(
-        jnp.arange(32, dtype=jnp.int32)
-    )
-    return every[where[inverse // per] * per + inverse % per]
-
-
 def to_matrices(blocks):
     return (
         blocks.reshape(2 * LAYERS, SIDE, SIDE, BS, BS).transpose(0, 1, 3, 2, 4).reshape(2 * LAYERS, D, D)
@@ -580,52 +1605,396 @@
     )
 
 
-def scatter_blocks(blocks, block_owner, sizes, slots):
+def tables(block_owner, slots, sizes):
+    ids = jnp.arange(block_owner.shape[0], dtype=jnp.int32)
+    inverse = jnp.sum(jnp.where(block_owner[None] == ids[:, None], ids[None], 0), axis=1)
     if not is_cube(sizes):
-        return lax.psum_scatter(blocks[block_owner], AX, scatter_dimension=0, tiled=True)
-    core = lax.axis_index("edge") % 2
-    chip = relative_devices()[..., :1] // 2 * (2 * slots)
-    owner = block_owner[(chip + jnp.arange(2 * slots, dtype=jnp.int32)).reshape(-1)]
-    laid = blocks[owner].reshape(4, 2, 2, 2 * slots, 2, BS // 2, BS)
-    swapped = jnp.where(core == 0, laid, laid[:, :, :, :, ::-1])
-    chunks = [swapped[p, :, :, :, 0] + hop(swapped[p, :, :, :, 1], HOP_CORE) for p in range(4)]
-    total = reduce_chips(chunks)
-    mine = jnp.where(core == 0, total[:slots], total[slots:])
-    other = hop(jnp.where(core == 0, total[slots:], total[:slots]), HOP_CORE)
-    return jnp.where(
-        core == 0,
-        jnp.concatenate([mine, other], axis=1),
-        jnp.concatenate([other, mine], axis=1),
-    )
-
-
-ROWS = 336
-
-
-def sum_large(trees, sizes):
+        return jnp.zeros_like(inverse), inverse, inverse
+    y, x, z, core = place()
+    device, slot = inverse // slots, inverse % slots
+    rank = jnp.sum(
+        jnp.where(
+            jnp.asarray(Z_ORDER)[z][:, None] == (device // 2 % 4)[None],
+            jnp.arange(4, dtype=jnp.int32)[:, None],
+            0,
+        ),
+        axis=0,
+    )
+    which = ((device % 2) ^ core) * 4 + rank
+    where = (((device // 8 % 2) ^ x) * 2 + ((device // 16) ^ y)) * slots + slot
+    return which, where, inverse
+
+
+def sum_pieces(pieces, sizes, slots):
     if not is_cube(sizes):
-        return lax.psum(trees, AX)
-    core = lax.axis_index("edge") % 2
-    flat = jnp.concatenate([leaf.reshape(-1) for leaf in trees])
-    count = flat.shape[0]
-    flat = jnp.pad(flat, (0, 32 * ROWS * BS - count)).reshape(32, ROWS, BS)
-    devices = relative_devices()
-    laid = flat[devices.reshape(-1)].reshape(4, 2, 2, 2, ROWS, BS)
-    chunks = [laid[p, :, :, 0] + hop(laid[p, :, :, 1], HOP_CORE) for p in range(4)]
-    total = reduce_chips(chunks)
-    pieces = []
-    for piece in spread_chips(total):
-        pieces.append(jnp.stack([piece, hop(piece, HOP_CORE)], axis=2))
-    every = jnp.concatenate(pieces, axis=0).reshape(32, ROWS, BS)
-    where = jnp.zeros((32,), jnp.int32).at[devices.reshape(-1)].set(
-        jnp.arange(32, dtype=jnp.int32)
-    )
-    flat = every[where].reshape(-1)
-    out, start = [], 0
-    for leaf in trees:
-        out.append(flat[start : start + leaf.size].reshape(leaf.shape))
-        start += leaf.size
-    return out
+        total = lax.psum_scatter(pieces[0], AX, scatter_dimension=0, tiled=True)
+        return total, total
+    chunks = [pieces[p] + hop(pieces[4 + p], HOP_CORE) for p in range(4)]
+    return reduce_chips([c.reshape(2, 2, slots, BS, BS) for c in chunks])
+
+
+def block_diagonal(mixing, depth):
+    channels = mixing.shape[-1]
+    rows = []
+    for k in range(9):
+        block = mixing[0 if k == 0 else 1 if k < 4 else 2]
+        rows.append(jnp.pad(block, ((0, 0), (k * channels, depth - (k + 1) * channels))))
+    return jnp.concatenate(rows, axis=0)
+
+
+def fast_chain(weights, every, inverse, targets, which, where, scale, force_to_tangent, vec, live, src, ss, st):
+    pair_in, pair_out, env_weight, scalar_weight, mix_weight, energy_head = weights
+    channels, edges = env_weight.shape[1], vec.shape[1]
+    rows9 = 9 * channels
+    depth = -(-rows9 // 128) * 128
+    head = energy_head[:D]
+    factor = jnp.sum(energy_head[D:, None] * ss, axis=0)
+    inv, unit, env, denv, bessel, dbessel = geometry(vec, live)
+    pad_rows = lambda v, n: jnp.pad(v, ((0, n - v.shape[0]), (0, 0)))
+    shape = pad_rows(harmonics(unit), 16)
+    feat = jnp.concatenate([bessel, ss, st], axis=0)
+    rows = pad_rows(jnp.stack([env, factor]), 8)
+    same = (src[:, None] == src[None]).astype(jnp.bfloat16)
+    cut = split_outside
+    in_t, in_w, out_t, out_w = cut(pair_in.T), cut(pair_in), cut(pair_out.T), cut(pair_out)
+    env_w, env_t = cut(env_weight), cut(env_weight.transpose(0, 2, 1))
+    sc_w, sc_t = cut(scalar_weight), cut(scalar_weight.transpose(0, 2, 1))
+    layer = lambda parts, l: tuple(v[l] for v in parts)
+    mix_w = cut(block_diagonal(mix_weight, depth))
+    mix_t = cut(block_diagonal(mix_weight.transpose(0, 2, 1), depth))
+    wide, plane, narrow = (D, edges), (rows9, edges), (channels, edges)
+    unit_flops = 6 * D * D * edges
+    temps = dict(**stream_scratch(), **plane_scratch(rows9, edges))
+    args = (channels, edges, scale)
+
+    one = kernel_call(
+        lambda r: first_layer(r, *args),
+        dict(shape=shape, rows=rows, same=same, feat=feat, in_t=in_t, env0w=layer(env_w, 0)),
+        dict(w0=f32(*narrow)),
+        temps,
+        sent=dict(
+            pre0=f32(*wide),
+            out0=f32(*wide),
+            hid=pair_of(*wide),
+            lat0=pair_of(*wide),
+            env0=f32(*plane),
+            res0=f32(*plane),
+        ),
+        hbm=dict(out_t=out_t),
+        flops=unit_flops,
+    )
+    loaded = kernel_call(
+        load_blocks,
+        dict(head=head[None]),
+        dict(last=f32(D, D), top=f32(D, 1)),
+        dict(
+            blocks=pltpu.VMEM((3, SIDE, BS, BS), jnp.float32),
+            flat=pltpu.VMEM((2, 2, BS, D), jnp.bfloat16),
+            turned=pltpu.VMEM((2, 2, D, BS), jnp.bfloat16),
+            sem=pltpu.SemaphoreType.DMA((3, SIDE)),
+            out_sem=pltpu.SemaphoreType.DMA((2, 4)),
+            last_sem=pltpu.SemaphoreType.DMA((SIDE, SIDE)),
+        ),
+        hbm=dict(piece=every),
+        hbm_out=dict(m=pair_of(3, D, D), mt=pair_of(3, D, D)),
+        smem=dict(where=inverse),
+    )
+    head_col = head[:, None]
+    up = kernel_call(
+        lambda r: energy_up(r, *args),
+        dict(
+            shape=shape,
+            rows=rows,
+            same=same,
+            head=head_col,
+            top=loaded.top,
+            lat0=one.lat0,
+            res0=one.res0,
+            sc0_t=layer(sc_t, 0),
+            sc1_t=layer(sc_t, 1),
+            env1w=layer(env_w, 1),
+        ),
+        dict(w1=f32(*narrow), res1=f32(*narrow), per=f32(8, edges)),
+        temps,
+        late=dict(out0=one.out0, mix=mix_w),
+        sent=dict(
+            pre1=f32(*wide),
+            out1=f32(*wide),
+            pre2=f32(*wide),
+            act1=pair_of(*wide),
+            lat1=pair_of(*wide),
+            pre2_bar=pair_of(*wide),
+            env1=f32(*plane),
+            feat1=f32(*plane),
+        ),
+        hbm=dict(mt=loaded.mt),
+        flops=3 * unit_flops,
+    )
+    down = kernel_call(
+        lambda r: energy_down(r, *args),
+        dict(
+            shape=shape,
+            rows=rows,
+            same=same,
+            head=head_col,
+            w0=one.w0,
+            w1=up.w1,
+            per=up.per,
+            pre2_bar=up.pre2_bar,
+            sc0=layer(sc_w, 0),
+            sc1=layer(sc_w, 1),
+            env0w_t=layer(env_t, 0),
+            env1w_t=layer(env_t, 1),
+            in_w=in_w,
+        ),
+        dict(
+            res1_bar=f32(*narrow),
+            w1_bar=f32(*narrow),
+            w0_bar=f32(*narrow),
+            shape_bar=f32(16, edges),
+            env_bar=f32(8, edges),
+            bessel_bar=f32(16, edges),
+        ),
+        temps,
+        late=dict(
+            pre0=one.pre0,
+            out0=one.out0,
+            env0=one.env0,
+            pre1=up.pre1,
+            out1=up.out1,
+            env1=up.env1,
+            feat1=up.feat1,
+            mix_t=mix_t,
+        ),
+        sent=dict(
+            lat1_bar=f32(*wide),
+            act1_bar=f32(*wide),
+            lat0_bar=f32(*wide),
+            hid_bar=f32(*wide),
+            out1_bar=pair_of(*wide),
+            pre1_bar=pair_of(*wide),
+            out0_bar=pair_of(*wide),
+            pre0_bar=pair_of(*wide),
+            feat1_bar=f32(*plane),
+            emb1_bar=f32(*plane),
+            res0_bar=f32(*plane),
+            emb0_bar=f32(*plane),
+        ),
+        hbm=dict(m=loaded.m, out=out_w),
+        flops=4 * unit_flops,
+    )
+    dist_bar = down.env_bar[0] * denv + jnp.sum(down.bessel_bar[:NB] * dbessel, axis=0)
+    unit_bar = harmonics_back(unit, down.shape_bar)
+    along = jnp.sum(unit * unit_bar, axis=0)
+    vec_bar = dist_bar[None] * unit + (unit_bar - unit * along[None]) * inv[None]
+    vec_dot, loss = force_to_tangent(vec_bar)
+    dist_dot = jnp.sum(unit * vec_dot, axis=0)
+    unit_dot = (vec_dot - unit * dist_dot[None]) * inv[None]
+    env_dot = denv * dist_dot
+    bessel_dot = pad_rows(dbessel * dist_dot[None], 2 * NB)
+    shape_dot = pad_rows(harmonics_dot(unit, unit_dot), 16)
+    rows = pad_rows(jnp.stack([env, factor, env_dot]), 8)
+    tan = kernel_call(
+        lambda r: tangent_up(r, *args),
+        dict(
+            shape=shape,
+            rows=rows,
+            same=same,
+            shape_dot=shape_dot,
+            bessel_dot=bessel_dot,
+            head=head_col,
+            top=loaded.top,
+            w0=one.w0,
+            w1=up.w1,
+            in_t=in_t,
+            sc0_t=layer(sc_t, 0),
+            sc1_t=layer(sc_t, 1),
+            env0w=layer(env_w, 0),
+            env1w=layer(env_w, 1),
+        ),
+        dict(
+            w0_dot=f32(*narrow),
+            w1_dot=f32(*narrow),
+            res1_dot=f32(*narrow),
+            head_part=f32(D, 128),
+            last_part=f32(D, 128),
+            per_dot=f32(8, edges),
+        ),
+        dict(
+            **temps,
+            tmp=pltpu.VMEM(wide, jnp.float32),
+            keep=pltpu.VMEM(wide, jnp.float32),
+        ),
+        late=dict(
+            pre0=one.pre0,
+            out0=one.out0,
+            env0=one.env0,
+            pre1=up.pre1,
+            out1=up.out1,
+            pre2=up.pre2,
+            env1=up.env1,
+            feat1=up.feat1,
+            lat1=up.lat1,
+            mix=mix_w,
+        ),
+        sent=dict(
+            pre0_dot=f32(*wide),
+            pre1_dot=f32(*wide),
+            hid_dot=pair_of(*wide),
+            lat0_dot=pair_of(*wide),
+            act1_dot=pair_of(*wide),
+            lat1_dot=pair_of(*wide),
+            pre2_hat=pair_of(*wide),
+            env0_dot=f32(*plane),
+            res0_dot=f32(*plane),
+            env1_dot=f32(*plane),
+            feat1_dot=f32(*plane),
+        ),
+        hbm=dict(out_t=out_t, mt=loaded.mt),
+        flops=4 * unit_flops,
+    )
+    hat = kernel_call(
+        lambda r: tangent_down(r, *args),
+        dict(
+            shape=shape,
+            rows=rows,
+            same=same,
+            shape_dot=shape_dot,
+            head=head_col,
+            pre2_hat=tan.pre2_hat,
+            w0=one.w0,
+            w0_dot=tan.w0_dot,
+            res1_bar=down.res1_bar,
+            sc0=layer(sc_w, 0),
+            sc1=layer(sc_w, 1),
+            env0w_t=layer(env_t, 0),
+            env1w_t=layer(env_t, 1),
+        ),
+        dict(w1_hat=f32(*narrow), w0_hat=f32(*narrow)),
+        dict(
+            **temps,
+            hat1=pltpu.VMEM(wide, jnp.float32),
+            tmp=pltpu.VMEM(wide, jnp.float32),
+            small=pltpu.VMEM(narrow, jnp.float32),
+            plane=pltpu.VMEM(plane, jnp.float32),
+            res0_hat=pltpu.VMEM(plane, jnp.float32),
+        ),
+        late=dict(
+            pre0=one.pre0,
+            env0=one.env0,
+            pre1=up.pre1,
+            env1=up.env1,
+            feat1=up.feat1,
+            lat1_bar=down.lat1_bar,
+            act1_bar=down.act1_bar,
+            lat0_bar=down.lat0_bar,
+            hid_bar=down.hid_bar,
+            emb1_bar=down.emb1_bar,
+            emb0_bar=down.emb0_bar,
+            res0_bar=down.res0_bar,
+            pre0_dot=tan.pre0_dot,
+            pre1_dot=tan.pre1_dot,
+            env1_dot=tan.env1_dot,
+            feat1_dot=tan.feat1_dot,
+            env0_dot=tan.env0_dot,
+            mix_t=mix_t,
+        ),
+        sent=dict(
+            out1_hat=pair_of(*wide),
+            pre1_hat=pair_of(*wide),
+            out0_hat=pair_of(*wide),
+            pre0_hat=pair_of(*wide),
+            feat1_hat=f32(*plane),
+        ),
+        hbm=dict(m=loaded.m, out=out_w),
+        flops=4 * unit_flops,
+    )
+    lead_sum = jnp.sum(tan.last_part, axis=1)
+    head_grad = RES * jnp.sum(tan.head_part, axis=1) + jnp.sum(
+        lead_sum[:, None] * loaded.last, axis=0
+    )
+    per1, per2 = up.per[0], up.per[1]
+    energy_dot = env_dot * RES * (per1 + env * per2) + env * RES * (
+        tan.per_dot[0] + env_dot * per2 + env * tan.per_dot[1]
+    )
+    head_grad = jnp.concatenate([head_grad, jnp.sum(ss * energy_dot[None], axis=1)])
+    made = kernel_call(
+        lambda r: block_gradients(r, channels, edges, targets),
+        dict(
+            lead=lead_sum[:, None],
+            head=head[None],
+        ),
+        {},
+        dict(
+            held=pltpu.VMEM((2, 4, 2, D, edges), jnp.bfloat16),
+            arrived=pltpu.SemaphoreType.DMA((2, 4, 2)),
+            stage=pltpu.VMEM((2, HALF, D), jnp.float32),
+            sent_sem=pltpu.SemaphoreType.DMA((2,)),
+        ),
+        hbm=dict(
+            lat0_dot=tan.lat0_dot,
+            act1_dot=tan.act1_dot,
+            lat1_dot=tan.lat1_dot,
+            pre2_hat=tan.pre2_hat,
+            lat0=one.lat0,
+            act1=up.act1,
+            lat1=up.lat1,
+            pre2_bar=up.pre2_bar,
+            pre1_bar=down.pre1_bar,
+            out1_bar=down.out1_bar,
+            pre1_hat=hat.pre1_hat,
+            out1_hat=hat.out1_hat,
+        ),
+        hbm_out=dict(out=[f32(every.shape[0] // targets, BS, BS) for _ in range(targets)]),
+        smem=dict(which=which, where=where),
+        flops=6 * unit_flops,
+    )
+
+    feat = lax.optimization_barrier((feat, made.out[0]))[0]
+    small = kernel_call(
+        lambda r: small_gradients(r, channels, edges),
+        dict(
+            feat=feat,
+            bessel_dot=bessel_dot,
+            hid_dot=tan.hid_dot,
+            out0_bar=down.out0_bar,
+            w0_bar=down.w0_bar,
+            w1_bar=down.w1_bar,
+            w0_hat=hat.w0_hat,
+            w1_hat=hat.w1_hat,
+            res1=up.res1,
+            res1_dot=tan.res1_dot,
+        ),
+        dict(
+            in_grad=f32(2 * NB, D),
+            mix_grad=f32(3, channels, channels),
+            env_grad=f32(2, channels, D),
+            sc_grad=f32(2, channels, D),
+        ),
+        {},
+        late=dict(
+            hid=one.hid,
+            out0_hat=hat.out0_hat,
+            pre0_bar=down.pre0_bar,
+            pre0_hat=hat.pre0_hat,
+            feat1_bar=down.feat1_bar,
+            res0_dot=tan.res0_dot,
+            feat1_hat=hat.feat1_hat,
+            res0=one.res0,
+            lat0_dot=tan.lat0_dot,
+            lat0=one.lat0,
+            pre1_bar=down.pre1_bar,
+            pre1_hat=hat.pre1_hat,
+            lat1_dot=tan.lat1_dot,
+            lat1=up.lat1,
+            pre2_bar=up.pre2_bar,
+            pre2_hat=tan.pre2_hat,
+        ),
+        sent=dict(out_grad=f32(D, D)),
+        flops=2 * unit_flops,
+    )
+
+    return small, head_grad, loss, made
 
 
 def local(
@@ -727,16 +2096,18 @@
     chosen = payload[jnp.minimum(index, devices * edges - 1)].T
     safe = jnp.asarray([1.5, 0.0, 0.0], jnp.float32)[:, None]
     my_vec = jnp.where(valid[None], chosen[:3], safe)
-    my_source = jnp.where(valid, chosen[3], 0.0).astype(jnp.int32)
-    my_target = jnp.where(valid, chosen[4], 0.0).astype(jnp.int32)
+    my_source = jnp.where(valid, chosen[3], -1.0).astype(jnp.int32)
+    my_target = jnp.where(valid, chosen[4], -1.0).astype(jnp.int32)
     my_live = as_float(valid)
 
     weights = (pair_in_weight, pair_out_weight, env_weight, scalar_weight, mix_weight[0], energy_head)
     slots = soap_weight.shape[0]
     kinds = jnp.arange(SPECIES, dtype=jnp.int32)[:, None]
-    matrices_all = to_matrices(gather_blocks(soap_weight, block_owner, sizes))
-
-    def run(vec, live, src, tgt, environ_of, hold):
+    every_block = lax.all_gather(soap_weight, AX, axis=0, tiled=True)
+    targets = 8 if is_cube(sizes) else 1
+    which, where, inverse = tables(block_owner, slots, sizes)
+
+    def views(src, tgt):
         from_atom = (src[:, None] == atom_ids[None]).astype(jnp.float32)
         to_atom = (tgt[:, None] == atom_ids[None]).astype(jnp.float32)
         spec = (species[None] == kinds).astype(jnp.float32)
@@ -745,64 +2116,108 @@
         ends = from_atom - to_atom
 
         def force_to_tangent(vec_bar):
-            force = sum_small(nn(vec_bar, ends), sizes)
+            force = sum_small(dot(vec_bar, ends, ((1,), (0,)), FULL), sizes)
             residual = force - label_all[:3]
             loss = jnp.sum(label_mask[None] * residual * residual)
             cot = 2.0 * label_mask[None] * residual / label_total
-            return nt(cot, ends), loss
-
-        return chain(
-            weights,
-            lambda after: matrices_all,
-            environ_of(from_atom),
-            force_to_tangent,
-            vec,
-            live,
-            species_source,
-            species_target,
-        )
-
-    def environ_local(from_atom):
-        same = dot(from_atom, from_atom, ((1,), (1,)), None)
-        return lambda tensor: scale * nn(tensor.reshape(-1, edges), same).reshape(tensor.shape)
-
-    def environ_global(from_atom):
-        def apply(tensor):
+            return dot(cot, ends, ((1,), (1,)), FULL), loss
+
+        return from_atom, species_source, species_target, force_to_tangent
+
+    def general():
+        from_atom, ss, st, force_to_tangent = views(source, target)
+        blocks = every_block[inverse]
+
+        def environ(tensor):
             sums = lax.psum(nn(tensor.reshape(-1, edges), from_atom), AX)
             return scale * nt(sums, from_atom).reshape(tensor.shape)
 
-        return apply
-
-    def pack(out):
-        return tuple(out[:6]) + (jnp.stack(out[6]), out[7])
-
-    grads = lax.cond(
-        fits,
-        lambda: pack(run(my_vec, my_live, my_source, my_target, environ_local, None)),
-        lambda: pack(run(edge_vec, as_float(edge_live), source, target, environ_global, None)),
-    )
-    pair_in_grad, pair_out_grad, env_grad, scalar_grad, mix_grad, head_grad = sum_large(
-        grads[:6], sizes
-    )
-    own_grads = scatter_blocks(to_blocks(grads[6]), block_owner, sizes, slots)
-    loss_sum = grads[7]
+        matrices = to_matrices(blocks)
+        out = chain(
+            weights,
+            lambda after: matrices,
+            environ,
+            force_to_tangent,
+            edge_vec,
+            as_float(edge_live),
+            ss,
+            st,
+        )
+        flat = to_blocks(jnp.stack(out[6]))
+        per = inverse.shape[0] // targets
+        place_of = which * per + where
+        order = jnp.zeros_like(place_of).at[place_of].set(jnp.arange(place_of.shape[0]))
+        laid = flat[order].reshape(targets, per, BS, BS)
+        return out[:6] + (tuple(laid[n] for n in range(targets)), out[7])
+
+    def pack_first(in_grad, out_grad, mix_grad, head_grad):
+        rest = jnp.concatenate([mix_grad.reshape(-1), head_grad])
+        rest = jnp.pad(rest, (0, -rest.shape[0] % (8 * D))).reshape(-1, D)
+        return jnp.concatenate([in_grad, rest], axis=0), out_grad
+
+    flat_rows = lambda env_grad, sc_grad: (env_grad.reshape(-1, D), sc_grad.reshape(-1, D))
+    def replace(state):
+        out = general()
+        parts = pack_first(out[0], out[1], out[4], out[5]) + flat_rows(out[2], out[3])
+        own, _ = sum_pieces(out[6], sizes, slots)
+        return (jnp.asarray(False), own, lax.psum(parts, AX), out[7])
+
+    rest_rows = 8 * (-(-(mix_weight.size + energy_head.shape[0]) // (8 * D))) + 2 * NB
+    zeros = lambda n: jnp.zeros((n, D), jnp.float32)
+    wide_rows = env_weight.shape[0] * env_weight.shape[1]
+    _, general_own, general_shared, general_loss = lax.while_loop(
+        lambda state: state[0],
+        replace,
+        (
+            jnp.logical_not(fits),
+            jnp.zeros_like(soap_weight),
+            (zeros(rest_rows), zeros(D), zeros(wide_rows), zeros(wide_rows)),
+            jnp.zeros((), jnp.float32),
+        ),
+    )
+    every_block, general_loss = lax.optimization_barrier((every_block, general_loss))
+    _, my_ss, my_st, my_force = views(my_source, my_target)
+    fast = fast_chain(
+        weights, every_block, inverse, targets, which, where, scale, my_force, my_vec, my_live, my_source, my_ss, my_st
+    )
+
+    small, head_part, fast_loss, made = fast
+    local_sums = pack_first(small.in_grad, small.out_grad, small.mix_grad, head_part)
+    local_sums = local_sums + flat_rows(small.env_grad, small.sc_grad)
+    summed = lax.psum(local_sums, AX)
+    loss_sum = jnp.where(fits, fast_loss, general_loss)
+
+    own_grads, nearly = sum_pieces(tuple(made.out), sizes, slots)
+    own_grads = jnp.where(fits, own_grads, general_own)
+    soap = soap_update(
+        (
+            own_grads,
+            soap_weight,
+            soap_first,
+            soap_second,
+            soap_left,
+            soap_right,
+            soap_lstat,
+            soap_rstat,
+            soap_average,
+        )
+    )
+    (summed, general_shared), soap = lax.optimization_barrier(((summed, general_shared), tuple(soap)))
+    misc, pair_out_grad, env_grad, scalar_grad = jax.tree.map(
+        lambda a, b: jnp.where(fits, a, b), summed, general_shared
+    )
+    pair_in_grad = misc[: 2 * NB]
+    rest = misc[2 * NB :].reshape(-1)
+    mix_grad = rest[: mix_weight.size].reshape(mix_weight.shape[1:])
+    head_grad = rest[mix_weight.size : mix_weight.size + energy_head.shape[0]]
+    env_grad = env_grad.reshape(env_weight.shape)
+    scalar_grad = scalar_grad.reshape(scalar_weight.shape)
     new_pair_in = adamw(pair_in_weight, pair_in_first, pair_in_second, pair_in_grad)
     new_pair_out = adamw(pair_out_weight, pair_out_first, pair_out_second, pair_out_grad)
     new_env = adamw(env_weight, env_first, env_second, env_grad)
     new_scalar = adamw(scalar_weight, scalar_first, scalar_second, scalar_grad)
     new_mix = adamw(mix_weight, mix_first, mix_second, mix_grad[None])
     new_head = adamw(energy_head, head_first, head_second, head_grad)
-    soap = jax.vmap(soap_slot)(
-        own_grads,
-        soap_weight,
-        soap_first,
-        soap_second,
-        soap_left,
-        soap_right,
-        soap_lstat,
-        soap_rstat,
-        soap_average,
-    )
     return (
         (loss_sum, label_total)
         + new_pair_in

time: 990 us -> 627 us (0.63)
  Pallas kernels: 0 us -> 270 us
  matrix products: 250 us -> 6.6 us
  local copies, waits for them, and re-layouts: 193 us -> 48.5 us
  other arithmetic: 172 us -> 78.4 us
  starting transfers between devices: 153 us -> 61.5 us
  waiting for transfers between devices: 181 us -> 124 us
    pallas_call x0 -> x9, Pallas kernels: none -> 270 us  [the longest x8 254 us: kernel_call(): pl.pallas_call(kernel, out_shape=out_leaves, in_specs=in_specs, out_specs...]
    dot_general x145 -> x4, matrix products: 248 us -> 4.9 us  [dot(): lax.dot_general(left, right, ((dims[0], dims[1]), ((), ())), precision=pr...]
    ppermute x119 -> x40, waiting for transfers between devices: 181 us -> 87.3 us  [hop(): return lax.ppermute(value, AX, pairs)]
    ppermute x119 -> x40, starting transfers between devices: 153 us -> 61.4 us  [hop(): return lax.ppermute(value, AX, pairs)]
    gather x7 -> x0, local copies, waits for them, and re-layouts: 50.7 us -> none  [the longest x3 19 us: gather_blocks(): return every[where[inverse // per] * per + inverse % per]]
    select_n x8 -> x4, other arithmetic: 41.6 us -> 4.04 us  [the longest x2 2.42 us: local(): jnp.where(fits, a, b)]
    slice x7 -> x6, local copies, waits for them, and re-layouts: 33.2 us -> 1.56 us  [the longest x1 0.69 us: fast_chain(): factor = jnp.sum(energy_head[D:, None] * ss, axis=0)]
    transpose x2 -> x0, local copies, waits for them, and re-layouts: 25.5 us -> none  [the longest x1 18.7 us: to_matrices(): blocks.reshape(2 * LAYERS, SIDE, SIDE, BS, BS).transpose(0, 1, 3, 2, 4)]
  transfers between devices with their start and end apart: 119 -> 42, of which waited for: 46 -> 23; matrix products, arithmetic and copies ran while one was open for 21% -> 15% of each run, Pallas kernels for 0% -> 9%
where the time goes in v2:
time: 627 us; the launch traced here: 616 us
  Pallas kernels  270 us (43%)
  waiting for transfers between devices  124 us (20%)
  other arithmetic  78.4 us (13%)
  starting transfers between devices  61.5 us (10%)
  local copies, waits for them, and re-layouts  48.5 us (8%)
  between operations  19.3 us (3%)
  loops' own time  8.34 us (1%)
  matrix products  6.6 us (1%)
    pallas_call x8, Pallas kernels, kernel_call(): pl.pallas_call(kernel, out_shape=out_leaves, in_specs=in_specs, out_specs...  254 us
    ppermute x40, waiting for transfers between devices, hop(): return lax.ppermute(value, AX, pairs)  87.3 us
    ppermute x40, starting transfers between devices, hop(): return lax.ppermute(value, AX, pairs)  61.4 us
    all_gather x1, waiting for transfers between devices, local(): every_block = lax.all_gather(soap_weight, AX, axis=0, tiled=True)  20.4 us
    pallas_call x1, Pallas kernels, soap_update(): pl.pallas_call(partial(soap_kernel, count), grid=(slots // count,), out_s...  15.9 us
    sub x6, other arithmetic, adamw(): return (weight - 0.01 * (normal + 0.01 * weight), first_new, second_new)  15.7 us
    psum x1, waiting for transfers between devices, local(): summed = lax.psum(local_sums, AX)  15.2 us
  transfers between devices with their start and end apart: 42, of which 23 were waited for; matrix products, arithmetic and copies ran while one was open for 15% of the time, Pallas kernels for 9%

profile of v2, /device:TPU:0, one launch (start us, length us, event | category | flops | bytes accessed | tf_op | source)
XLA Modules:
  0.0 615.9 jit_solution(4522399620370047551)
XLA Ops:
  12.1 3.0 collective-permute-start.33
  16.7 5.4 copy.259
  40.1 3.1 fusion.927
  50.9 4.6 collective-permute-done.36
  55.5 4.7 collective-permute-done.37
  72.7 5.3 copy.256
  80.7 4.4 convert_reduce_fusion
  85.1 4.6 gather_fusion.3
  99.1 13.0 %shard_map.591 = (f32[64,512]{1,0:T(8,128)}, f32[576,512]{1,0:T(8,128)}, bf16[1024,512]{1,0:T(8,128)(2,1)}, bf16[1024,512]{1,0:T(8,128)(2,1)}, bf16[1024,512]{1,...) custom-call(bf16[64,1024]{1,0:T(8,128)(2,1)} %get-tuple-element.1002, ...), custom_call_target="tpu_custom_call" | custom-call | flops 3221225472 | bytes 16007168 | tf_op jit(solution)/shard_map/pallas_call | solution.py:595
  112.2 20.4 %all-gather.2.cloned.1.call-done.refs_2_ = f32[256,128,128]{2,1,0:T(8,128)} async-done(((f32[8,128,128]{2,1,0:T(8,128)}), f32[256,128,128]{2,1,0:T(8,128)}) %all-gather.2.cloned.1.call-update) | async-done | bytes 16777232 | tf_op jit(solution)/shard_map/all_gather | solution.py:2106
  138.2 8.3 %while.24 = (pred[]{:T(512)}, f32[8,128,128]{2,1,0:T(8,128)}, f32[32,1024]{1,0:T(8,128)}, f32[1024,1024]{1,0:T(8,128)}, f32[128,1024]{1,0:T(8,128)}, /*index=5*/...) while((pred[]{:T(512)}, f32[8,128,128]{2,1,0:T(8,128)}, ...), condition=%region_51.52_spmd.clone.clone, body=%region_13.51_spmd.clone.clone | while | flops 97740455936 | bytes 1994839040 | solution.py:2168
  146.6 24.2 %shard_map.592 = (f32[1024,1024]{1,0:T(8,128)}, f32[1024,1]{1,0:T(8,128)}, bf16[3,1024,1024]{2,1,0:T(8,128)(2,1)}, bf16[3,1024,1024]{2,1,0:T(8,128)(2,1)}, bf16[...) custom-call(f32[1,1024]{1,0:T(1,128)} %bitcast.2047, s32[256]{0:T(256)} %select_reduce_fusion.refs_1_, ...), custom_call_target="tpu_custom_call" | custom-call | bytes 46146560 | tf_op jit(solution)/shard_map/pallas_call | solution.py:595
  170.8 27.5 %shard_map.593 = (f32[8,512]{1,0:T(8,128)}, f32[64,512]{1,0:T(8,128)}, f32[64,512]{1,0:T(8,128)}, bf16[1024,512]{1,0:T(8,128)(2,1)}, bf16[1024,512]{1,0:T(8,128)...) custom-call(bf16[64,1024]{1,0:T(8,128)(2,1)} %get-tuple-element.1003, ...), custom_call_target="tpu_custom_call" | custom-call | flops 9663676416 | bytes 36020224 | tf_op jit(solution)/shard_map/pallas_call | solution.py:595
  198.5 41.3 %shard_map.594 = (f32[16,512]{1,0:T(8,128)}, f32[8,512]{1,0:T(8,128)}, f32[64,512]{1,0:T(8,128)}, f32[16,512]{1,0:T(8,128)}, f32[64,512]{1,0:T(8,128)}, /*index=...) custom-call(bf16[1024,64]{1,0:T(8,128)(2,1)} %get-tuple-element.995., ...), custom_call_target="tpu_custom_call" | custom-call | flops 12884901888 | bytes 56217600 | tf_op jit(solution)/shard_map/pallas_call | solution.py:595
  265.0 44.0 %shard_map.595 = (f32[1024,128]{1,0:T(8,128)}, f32[1024,128]{1,0:T(8,128)}, f32[8,512]{1,0:T(8,128)}, f32[64,512]{1,0:T(8,128)}, f32[64,512]{1,0:T(8,128)}, /*in...) custom-call(f32[16,512]{1,0:T(8,128)} %pad.121.refs_0_, ...), custom_call_target="tpu_custom_call" | custom-call | flops 12884901888 | bytes 57253888 | tf_op jit(solution)/shard_map/pallas_call | solution.py:595
  311.3 45.9 %shard_map.596 = (f32[64,512]{1,0:T(8,128)}, f32[64,512]{1,0:T(8,128)}, f32[576,512]{1,0:T(8,128)}, bf16[1024,512]{1,0:T(8,128)(2,1)}, bf16[1024,512]{1,0:T(8,12...) custom-call(bf16[1024,64]{1,0:T(8,128)(2,1)} %get-tuple-element.995., ...), custom_call_target="tpu_custom_call" | custom-call | flops 12884901888 | bytes 59625472 | tf_op jit(solution)/shard_map/pallas_call | solution.py:595
  357.2 31.8 %shard_map.597 = (f32[32,128,128]{2,1,0:T(8,128)}, f32[32,128,128]{2,1,0:T(8,128)}, f32[32,128,128]{2,1,0:T(8,128)}, f32[32,128,128]{2,1,0:T(8,128)}, f32[32,128...) custom-call(f32[1,1024]{1,0:T(1,128)} %bitcast.2048, ...), custom_call_target="tpu_custom_call" | custom-call | flops 19327352832 | bytes 41953280 | tf_op jit(solution)/shard_map/pallas_call | solution.py:595
  390.1 26.1 %shard_map.598 = (f32[2,64,1024]{2,1,0:T(8,128)}, f32[16,1024]{1,0:T(8,128)}, f32[3,64,64]{2,1,0:T(8,128)}, f32[2,64,1024]{2,1,0:T(8,128)}, f32[1024,1024]{1,0:T(8,128)}) custom-call(f32[16,512]{1,0:T(8,128)} %pad.121.refs_0_, f32[16,512]{1,0:T(8,128)} %pad_maximum_fusion.20.refs_2_.refs_1_, bf16[1024,512]{1,0:T(8,128)(2,1)} %get-tuple-element.409.refs_2_, ...), custom_call_target="tpu_custom_call" | custom-call | flops 6442450944 | bytes 40288256 | tf_op jit(solution)/shard_map/pallas_call | solution.py:595
  439.3 7.2 %collective-permute-done.49 = f32[2,4,128,128]{3,2,1,0:T(8,128)} collective-permute-done((f32[2,4,128,128]{3,2,1,0:T(8,128)}, f32[2,4,128,128]{3,2,1,0:T(8,128)}, u32[]{:S(2)}, u32[]{:S(2)}) %collective-permute-start.49) | collective-permute-done | bytes 524320 | tf_op jit(solution)/shard_map/ppermute | solution.py:140
  446.5 4.5 collective-permute-done.50
  455.4 8.5 %collective-permute-done.57 = f32[2,4,128,128]{3,2,1,0:T(8,128)S(1)} collective-permute-done((f32[2,4,128,128]{3,2,1,0:T(8,128)S(1)}, f32[2,4,128,128]{3,2,1,0:T(8,128)S(1)}, u32[]{:S(2)}, u32[]{:S(2)}) %collective-permute-start.57) | collective-permute-done | bytes 524320 | tf_op jit(solution)/shard_map/ppermute | solution.py:140
  468.3 3.5 collective-permute-done.64
  472.3 12.0 %collective-permute-done.65 = f32[4,128,128]{2,1,0:T(8,128)S(1)} collective-permute-done((f32[4,128,128]{2,1,0:T(8,128)S(1)}, f32[4,128,128]{2,1,0:T(8,128)S(1)}, u32[]{:S(2)}, u32[]{:S(2)}) %collective-permute-start.65) | collective-permute-done | bytes 262176 | tf_op jit(solution)/shard_map/ppermute | solution.py:140
  486.4 3.6 collective-permute-done.69
  493.8 7.5 %collective-permute-done.59 = f32[2,4,128,128]{3,2,1,0:T(8,128)S(1)} collective-permute-done((f32[2,4,128,128]{3,2,1,0:T(8,128)S(1)}, f32[2,4,128,128]{3,2,1,0:T(8,128)S(1)}, u32[]{:S(2)}, u32[]{:S(2)}) %collective-permute-start.59) | collective-permute-done | bytes 524320 | tf_op jit(solution)/shard_map/ppermute | solution.py:140
  506.7 8.9 %collective-permute-done.70 = f32[8,128,128]{2,1,0:T(8,128)S(1)} collective-permute-done((f32[8,128,128]{2,1,0:T(8,128)S(1)}, f32[8,128,128]{2,1,0:T(8,128)S(1)}, u32[]{:S(2)}, u32[]{:S(2)}) %collective-permute-start.70) | collective-permute-done | bytes 524320 | tf_op jit(solution)/shard_map/ppermute | solution.py:140
  519.1 21.7 %collective-permute-start.63 = (f32[8,128,128]{2,1,0:T(8,128)}, f32[8,128,128]{2,1,0:T(8,128)}, u32[]{:S(2)}, u32[]{:S(2)}) collective-permute-start(f32[8,128,128]{2,1,0:T(8,128)} %get-tuple-element.972), channel_id=1, source_target_pairs={{0,2},{1,3},{8,10},{9,11},{16,18},{17,19},{24,26},{25,27},{6,4},{7... | collective-permute-start | bytes 1572872 | tf_op jit(solution)/shard_map/ppermute | solution.py:140
  544.8 4.6 collective-permute-done.54
  551.9 4.3 collective-permute-done.72
  557.9 15.9 %shard_map.599 = (f32[8,128,128]{2,1,0:T(8,128)}, f32[8,128,128]{2,1,0:T(8,128)}, f32[8,128,128]{2,1,0:T(8,128)}, f32[8,128,128]{2,1,0:T(8,128)}, f32[8,128,128]...) custom-call(f32[8,128,128]{2,1,0:T(8,128)S(1)} %fusion.956.refs_0_, ...), custom_call_target="tpu_custom_call" | custom-call | tf_op jit(solution)/shard_map/pallas_call | solution.py:1573
  573.8 15.2 %all-reduce.39.cloned.1.call-done = (f32[32,1024]{1,0:T(8,128)}, f32[1024,1024]{1,0:T(8,128)}, f32[128,1024]{1,0:T(8,128)}, f32[128,1024]{1,0:T(8,128)}) async-done(((f32[32,1024]{1,0:T(8,128)}, f32[1024,1024]{1,0:T(8,128)}, f32[128,1024]{1,0:T(8,128)}, f32[128,1024]{1,0:T(8,128)}), (f32[32,1024]{1,0:T(8,128)}, f32[1024,1024]{1,0:T(8,128)}, f32[128,1024]{1,0:T(8,128)}, ...) | async-done | bytes 5373968 | tf_op jit(solution)/shard_map/psum | solution.py:2187
  598.4 9.1 %multiply_subtract_fusion.1 = (f32[1024,1024]{1,0:T(8,128)}, f32[1024,1024]{1,0:T(8,128)}, f32[1024,1024]{1,0:T(8,128)}) fusion(f32[1024,1024]{1,0:T(8,128)S(1)} %copy-done.73, f32[1024,1024]{1,0:T(8,128)} %get-tuple-element.470, f32[1024,1024]{1,0:T(8,128)S(1)} %copy-done.187, pred[]{:T(512)S(6)} %le.37, f32[1024,1024]{1,0:T(8,128)} %param.60, ...), kind=kLoop, calls=%fused_computation.1245 | loop fusion | flops 16777216 | bytes 33554432 | tf_op jit(solution)/shard_map/sub | solution.py:1591
  (418 shorter events, 152.4 us)
Async XLA Ops:
  7.2 125.3 %all-gather.2.cloned.1.call-start = ((), (), s32[]{:S(2)}) async-start(), calls=%async_computation | async-start | bytes 17301504 | tf_op jit(solution)/shard_map/all_gather | solution.py:2106
  12.1 34.0 %collective-permute-start.33 = (f32[7,512]{1,0:T(8,128)S(1)}, f32[7,512]{1,0:T(8,128)S(1)}, u32[]{:S(2)}, u32[]{:S(2)}) collective-permute-start(f32[7,512]{1,0:T(8,128)S(1)} %concatenate.86), channel_id=1, source_target_pairs={{0,8},{1,9},{2,10},{3,11},{4,12},{5,13},{6,14},{7,15},{8,0},{9,1},... | collective-permute-start | bytes 43016 | tf_op jit(solution)/shard_map/ppermute | solution.py:140
  15.1 31.0 %collective-permute-start.34 = (f32[7,512]{1,0:T(8,128)S(1)}, f32[7,512]{1,0:T(8,128)S(1)}, u32[]{:S(2)}, u32[]{:S(2)}) collective-permute-start(f32[7,512]{1,0:T(8,128)S(1)} %concatenate.86), channel_id=1, source_target_pairs={{0,16},{1,17},{2,18},{3,19},{4,20},{5,21},{6,22},{7,23},{8,24},{9,... | collective-permute-start | bytes 43016 | tf_op jit(solution)/shard_map/ppermute | solution.py:140
  16.7 29.5 %collective-permute-start.35 = (f32[7,512]{1,0:T(8,128)S(1)}, f32[7,512]{1,0:T(8,128)S(1)}, u32[]{:S(2)}, u32[]{:S(2)}) collective-permute-start(f32[7,512]{1,0:T(8,128)S(1)} %concatenate.86), channel_id=1, source_target_pairs={{0,24},{1,25},{2,26},{3,27},{4,28},{5,29},{6,30},{7,31},{8,16},{9,... | collective-permute-start | bytes 43016 | tf_op jit(solution)/shard_map/ppermute | solution.py:140
  46.2 9.3 %collective-permute-start.36 = (f32[4,7,512]{2,1,0:T(8,128)S(1)}, f32[4,7,512]{2,1,0:T(8,128)S(1)}, u32[]{:S(2)}, u32[]{:S(2)}) collective-permute-start(f32[4,7,512]{2,1,0:T(8,128)S(1)} %get-tuple-element.1018), channel_id=1, source_target_pairs={{0,2},{1,3},{8,10},{9,11},{16,18},{17,19},{24,26},{25,27},{2,0},{3... | collective-permute-start | bytes 172040 | tf_op jit(solution)/shard_map/ppermute | solution.py:140
  48.3 11.8 %collective-permute-start.37 = (f32[4,7,512]{2,1,0:T(8,128)S(1)}, f32[4,7,512]{2,1,0:T(8,128)S(1)}, u32[]{:S(2)}, u32[]{:S(2)}) collective-permute-start(f32[4,7,512]{2,1,0:T(8,128)S(1)} %get-tuple-element.1018), channel_id=1, source_target_pairs={{0,4},{1,5},{8,12},{9,13},{16,20},{17,21},{24,28},{25,29},{2,6},{3... | collective-permute-start | bytes 172040 | tf_op jit(solution)/shard_map/ppermute | solution.py:140
  50.9 9.3 %collective-permute-start.38 = (f32[4,7,512]{2,1,0:T(8,128)S(1)}, f32[4,7,512]{2,1,0:T(8,128)S(1)}, u32[]{:S(2)}, u32[]{:S(2)}) collective-permute-start(f32[4,7,512]{2,1,0:T(8,128)S(1)} %get-tuple-element.1018), channel_id=1, source_target_pairs={{0,6},{1,7},{8,14},{9,15},{16,22},{17,23},{24,30},{25,31},{2,4},{3... | collective-permute-start | bytes 172040 | tf_op jit(solution)/shard_map/ppermute | solution.py:140
  146.6 442.4 %all-reduce.39.cloned.1.call-start = ((), (), s32[]{:S(2)}) async-start(), calls=%async_computation.1 | async-start | bytes 10747904 | tf_op jit(solution)/shard_map/psum | solution.py:2187
  389.0 33.0 %collective-permute-start.48 = (f32[32,128,128]{2,1,0:T(8,128)}, f32[32,128,128]{2,1,0:T(8,128)S(1)}, u32[]{:S(2)}, u32[]{:S(2)}) collective-permute-start(f32[32,128,128]{2,1,0:T(8,128)} %get-tuple-element.445), channel_id=1, source_target_pairs={{0,1},{1,0},{2,3},{3,2},{4,5},{5,4},{6,7},{7,6},{8,9},{9,8},{10,11... | collective-permute-start | bytes 6291464 | tf_op jit(solution)/shard_map/ppermute | solution.py:140
  389.1 45.0 %collective-permute-start.47 = (f32[32,128,128]{2,1,0:T(8,128)}, f32[32,128,128]{2,1,0:T(8,128)}, u32[]{:S(2)}, u32[]{:S(2)}) collective-permute-start(f32[32,128,128]{2,1,0:T(8,128)} %get-tuple-element.443), channel_id=1, source_target_pairs={{0,1},{1,0},{2,3},{3,2},{4,5},{5,4},{6,7},{7,6},{8,9},{9,8},{10,11... | collective-permute-start | bytes 6291464 | tf_op jit(solution)/shard_map/ppermute | solution.py:140
  389.6 40.6 %collective-permute-start.56 = (f32[32,128,128]{2,1,0:T(8,128)}, f32[32,128,128]{2,1,0:T(8,128)}, u32[]{:S(2)}, u32[]{:S(2)}) collective-permute-start(f32[32,128,128]{2,1,0:T(8,128)} %get-tuple-element.449), channel_id=1, source_target_pairs={{0,1},{1,0},{2,3},{3,2},{4,5},{5,4},{6,7},{7,6},{8,9},{9,8},{10,11... | collective-permute-start | bytes 6291464 | tf_op jit(solution)/shard_map/ppermute | solution.py:140
  389.7 47.7 %collective-permute-start.55 = (f32[32,128,128]{2,1,0:T(8,128)}, f32[32,128,128]{2,1,0:T(8,128)}, u32[]{:S(2)}, u32[]{:S(2)}) collective-permute-start(f32[32,128,128]{2,1,0:T(8,128)} %get-tuple-element.448), channel_id=1, source_target_pairs={{0,1},{1,0},{2,3},{3,2},{4,5},{5,4},{6,7},{7,6},{8,9},{9,8},{10,11... | collective-permute-start | bytes 6291464 | tf_op jit(solution)/shard_map/ppermute | solution.py:140
  426.7 19.8 %collective-permute-start.49 = (f32[2,4,128,128]{3,2,1,0:T(8,128)}, f32[2,4,128,128]{3,2,1,0:T(8,128)}, u32[]{:S(2)}, u32[]{:S(2)}) collective-permute-start(f32[2,4,128,128]{3,2,1,0:T(8,128)} %slice_bitcast_fusion.116), channel_id=1, source_target_pairs={{0,8},{1,9},{2,10},{3,11},{4,12},{5,13},{6,14},{7,15},{8,0},{9,1},... | collective-permute-start | bytes 1572872 | tf_op jit(solution)/shard_map/ppermute | solution.py:140
  429.0 22.0 %collective-permute-start.50 = (f32[2,4,128,128]{3,2,1,0:T(8,128)}, f32[2,4,128,128]{3,2,1,0:T(8,128)}, u32[]{:S(2)}, u32[]{:S(2)}) collective-permute-start(f32[2,4,128,128]{3,2,1,0:T(8,128)} %slice_bitcast_fusion.114), channel_id=1, source_target_pairs={{0,16},{1,17},{2,18},{3,19},{4,20},{5,21},{6,22},{7,23},{8,24},{9,... | collective-permute-start | bytes 1572872 | tf_op jit(solution)/shard_map/ppermute | solution.py:140
  432.7 31.1 %collective-permute-start.57 = (f32[2,4,128,128]{3,2,1,0:T(8,128)S(1)}, f32[2,4,128,128]{3,2,1,0:T(8,128)S(1)}, u32[]{:S(2)}, u32[]{:S(2)}) collective-permute-start(f32[2,4,128,128]{3,2,1,0:T(8,128)S(1)} %slice_bitcast_fusion.110), channel_id=1, source_target_pairs={{0,8},{1,9},{2,10},{3,11},{4,12},{5,13},{6,14},{7,15},{8,0},{9,1},... | collective-permute-start | bytes 1572872 | tf_op jit(solution)/shard_map/ppermute | solution.py:140
  434.1 32.1 %collective-permute-start.58 = (f32[2,4,128,128]{3,2,1,0:T(8,128)S(1)}, f32[2,4,128,128]{3,2,1,0:T(8,128)S(1)}, u32[]{:S(2)}, u32[]{:S(2)}) collective-permute-start(f32[2,4,128,128]{3,2,1,0:T(8,128)S(1)} %slice_bitcast_fusion.108), channel_id=1, source_target_pairs={{0,16},{1,17},{2,18},{3,19},{4,20},{5,21},{6,22},{7,23},{8,24},{9,... | collective-permute-start | bytes 1572872 | tf_op jit(solution)/shard_map/ppermute | solution.py:140
  452.5 39.2 %collective-permute-start.51 = (f32[2,4,128,128]{3,2,1,0:T(8,128)S(1)}, f32[2,4,128,128]{3,2,1,0:T(8,128)S(1)}, u32[]{:S(2)}, u32[]{:S(2)}) collective-permute-start(f32[2,4,128,128]{3,2,1,0:T(8,128)S(1)} %slice_bitcast_fusion.119), channel_id=1, source_target_pairs={{0,8},{1,9},{2,10},{3,11},{4,12},{5,13},{6,14},{7,15},{8,0},{9,1},... | collective-permute-start | bytes 1572872 | tf_op jit(solution)/shard_map/ppermute | solution.py:140
  452.6 19.2 %collective-permute-start.64 = (f32[4,128,128]{2,1,0:T(8,128)S(1)}, f32[4,128,128]{2,1,0:T(8,128)S(1)}, u32[]{:S(2)}, u32[]{:S(2)}) collective-permute-start(f32[4,128,128]{2,1,0:T(8,128)S(1)} %get-tuple-element.452), channel_id=1, source_target_pairs={{0,16},{1,17},{2,18},{3,19},{4,20},{5,21},{6,22},{7,23},{8,24},{9,... | collective-permute-start | bytes 786440 | tf_op jit(solution)/shard_map/ppermute | solution.py:140
  454.1 30.3 %collective-permute-start.65 = (f32[4,128,128]{2,1,0:T(8,128)S(1)}, f32[4,128,128]{2,1,0:T(8,128)S(1)}, u32[]{:S(2)}, u32[]{:S(2)}) collective-permute-start(f32[4,128,128]{2,1,0:T(8,128)S(1)} %get-tuple-element.454), channel_id=1, source_target_pairs={{0,8},{1,9},{2,10},{3,11},{4,12},{5,13},{6,14},{7,15},{8,0},{9,1},... | collective-permute-start | bytes 786440 | tf_op jit(solution)/shard_map/ppermute | solution.py:140
  466.4 19.3 %collective-permute-start.68 = (f32[4,128,128]{2,1,0:T(8,128)S(1)}, f32[4,128,128]{2,1,0:T(8,128)S(1)}, u32[]{:S(2)}, u32[]{:S(2)}) collective-permute-start(f32[4,128,128]{2,1,0:T(8,128)S(1)} %get-tuple-element.456), channel_id=1, source_target_pairs={{0,16},{1,17},{2,18},{3,19},{4,20},{5,21},{6,22},{7,23},{8,24},{9,... | collective-permute-start | bytes 786440 | tf_op jit(solution)/shard_map/ppermute | solution.py:140
  467.0 23.0 %collective-permute-start.69 = (f32[4,128,128]{2,1,0:T(8,128)S(1)}, f32[4,128,128]{2,1,0:T(8,128)S(1)}, u32[]{:S(2)}, u32[]{:S(2)}) collective-permute-start(f32[4,128,128]{2,1,0:T(8,128)S(1)} %get-tuple-element.458), channel_id=1, source_target_pairs={{0,8},{1,9},{2,10},{3,11},{4,12},{5,13},{6,14},{7,15},{8,0},{9,1},... | collective-permute-start | bytes 786440 | tf_op jit(solution)/shard_map/ppermute | solution.py:140
  471.8 33.8 %collective-permute-start.53 = (f32[2,4,128,128]{3,2,1,0:T(8,128)S(1)}, f32[2,4,128,128]{3,2,1,0:T(8,128)S(1)}, u32[]{:S(2)}, u32[]{:S(2)}) collective-permute-start(f32[2,4,128,128]{3,2,1,0:T(8,128)S(1)} %slice_bitcast_fusion.112), channel_id=1, source_target_pairs={{0,16},{1,17},{2,18},{3,19},{4,20},{5,21},{6,22},{7,23},{8,24},{9,... | collective-permute-start | bytes 1572872 | tf_op jit(solution)/shard_map/ppermute | solution.py:140
  484.4 17.0 %collective-permute-start.59 = (f32[2,4,128,128]{3,2,1,0:T(8,128)S(1)}, f32[2,4,128,128]{3,2,1,0:T(8,128)S(1)}, u32[]{:S(2)}, u32[]{:S(2)}) collective-permute-start(f32[2,4,128,128]{3,2,1,0:T(8,128)S(1)} %slice_bitcast_fusion.118), channel_id=1, source_target_pairs={{0,8},{1,9},{2,10},{3,11},{4,12},{5,13},{6,14},{7,15},{8,0},{9,1},... | collective-permute-start | bytes 1572872 | tf_op jit(solution)/shard_map/ppermute | solution.py:140
  485.7 19.8 %collective-permute-start.61 = (f32[2,4,128,128]{3,2,1,0:T(8,128)S(1)}, f32[2,4,128,128]{3,2,1,0:T(8,128)S(1)}, u32[]{:S(2)}, u32[]{:S(2)}) collective-permute-start(f32[2,4,128,128]{3,2,1,0:T(8,128)S(1)} %slice_bitcast_fusion.106), channel_id=1, source_target_pairs={{0,16},{1,17},{2,18},{3,19},{4,20},{5,21},{6,22},{7,23},{8,24},{9,... | collective-permute-start | bytes 1572872 | tf_op jit(solution)/shard_map/ppermute | solution.py:140
  490.0 26.3 %collective-permute-start.66 = (f32[8,128,128]{2,1,0:T(8,128)S(1)}, f32[8,128,128]{2,1,0:T(8,128)S(1)}, u32[]{:S(2)}, u32[]{:S(2)}) collective-permute-start(f32[8,128,128]{2,1,0:T(8,128)S(1)} %pad_maximum_fusion.15), channel_id=1, source_target_pairs={{0,2},{1,3},{8,10},{9,11},{16,18},{17,19},{24,26},{25,27},{6,4},{7... | collective-permute-start | bytes 1572872 | tf_op jit(solution)/shard_map/ppermute | solution.py:140
  491.7 23.8 %collective-permute-start.70 = (f32[8,128,128]{2,1,0:T(8,128)S(1)}, f32[8,128,128]{2,1,0:T(8,128)S(1)}, u32[]{:S(2)}, u32[]{:S(2)}) collective-permute-start(f32[8,128,128]{2,1,0:T(8,128)S(1)} %pad_maximum_fusion.16), channel_id=1, source_target_pairs={{0,2},{1,3},{8,10},{9,11},{16,18},{17,19},{24,26},{25,27},{6,4},{7... | collective-permute-start | bytes 1572872 | tf_op jit(solution)/shard_map/ppermute | solution.py:140
  501.4 43.3 %collective-permute-start.52 = (f32[4,128,128]{2,1,0:T(8,128)}, f32[4,128,128]{2,1,0:T(8,128)S(1)}, u32[]{:S(2)}, u32[]{:S(2)}) collective-permute-start(f32[4,128,128]{2,1,0:T(8,128)} %slice_bitcast_fusion.130), channel_id=1, source_target_pairs={{0,16},{1,17},{2,18},{3,19},{4,20},{5,21},{6,22},{7,23},{8,24},{9,... | collective-permute-start | bytes 786440 | tf_op jit(solution)/shard_map/ppermute | solution.py:140
  505.5 12.4 %collective-permute-start.60 = (f32[4,128,128]{2,1,0:T(8,128)S(1)}, f32[4,128,128]{2,1,0:T(8,128)S(1)}, u32[]{:S(2)}, u32[]{:S(2)}) collective-permute-start(f32[4,128,128]{2,1,0:T(8,128)S(1)} %slice_bitcast_fusion.122), channel_id=1, source_target_pairs={{0,16},{1,17},{2,18},{3,19},{4,20},{5,21},{6,22},{7,23},{8,24},{9,... | collective-permute-start | bytes 786440 | tf_op jit(solution)/shard_map/ppermute | solution.py:140
  505.6 12.3 %collective-permute-start.62 = (f32[4,128,128]{2,1,0:T(8,128)S(1)}, f32[4,128,128]{2,1,0:T(8,128)S(1)}, u32[]{:S(2)}, u32[]{:S(2)}) collective-permute-start(f32[4,128,128]{2,1,0:T(8,128)S(1)} %slice_bitcast_fusion.120), channel_id=1, source_target_pairs={{0,8},{1,9},{2,10},{3,11},{4,12},{5,13},{6,14},{7,15},{8,0},{9,1},... | collective-permute-start | bytes 786440 | tf_op jit(solution)/shard_map/ppermute | solution.py:140
  516.4 34.0 %collective-permute-start.67 = (f32[8,128,128]{2,1,0:T(8,128)S(1)}, f32[8,128,128]{2,1,0:T(8,128)}, u32[]{:S(2)}, u32[]{:S(2)}) collective-permute-start(f32[8,128,128]{2,1,0:T(8,128)S(1)} %fusion.1018), channel_id=1, source_target_pairs={{2,4},{3,5},{10,12},{11,13},{18,20},{19,21},{26,28},{27,29},{4,2},... | collective-permute-start | bytes 1572872 | tf_op jit(solution)/shard_map/ppermute | solution.py:140
  519.1 32.8 %collective-permute-start.63 = (f32[8,128,128]{2,1,0:T(8,128)}, f32[8,128,128]{2,1,0:T(8,128)}, u32[]{:S(2)}, u32[]{:S(2)}) collective-permute-start(f32[8,128,128]{2,1,0:T(8,128)} %get-tuple-element.972), channel_id=1, source_target_pairs={{0,2},{1,3},{8,10},{9,11},{16,18},{17,19},{24,26},{25,27},{6,4},{7... | collective-permute-start | bytes 1572872 | tf_op jit(solution)/shard_map/ppermute | solution.py:140
  540.7 15.5 %collective-permute-start.72 = (f32[8,128,128]{2,1,0:T(8,128)}, f32[8,128,128]{2,1,0:T(8,128)}, u32[]{:S(2)}, u32[]{:S(2)}) collective-permute-start(f32[8,128,128]{2,1,0:T(8,128)} %get-tuple-element.973), channel_id=1, source_target_pairs={{2,0},{3,1},{10,8},{11,9},{18,16},{19,17},{26,24},{27,25},{4,6},{5... | collective-permute-start | bytes 1572872 | tf_op jit(solution)/shard_map/ppermute | solution.py:140
  (82 other events, 1313.1 us)
Sparse Core Ops, SparseCore 0:
  11.0 121.4 all-gather.1
  430.3 158.6 all-reduce.38

commit v3 on v2

--- a/solution.py
+++ b/solution.py
@@ -248,11 +248,11 @@
     )
 
 
-def harmonics_dot(unit, dunit):
+def harmonics_dot_rows(unit, dunit):
     x, y, z = unit
     dx, dy, dz = dunit
     h = HARMONIC
-    return jnp.stack(
+    return (
         [
             jnp.zeros_like(x),
             ROOT_THREE * dx,
@@ -267,16 +267,24 @@
     )
 
 
-def harmonics_back(unit, bar):
+def harmonics_back_rows(unit, bar):
     x, y, z = unit
     a, b = HARMONIC * ROOT_TWO, 2.0 * HARMONIC / ROOT_SIX
-    return jnp.stack(
+    return (
         [
             ROOT_THREE * bar[1] + a * (y * bar[4] + z * bar[6] + x * bar[7]) - b * x * bar[8],
             ROOT_THREE * bar[2] + a * (x * bar[4] + z * bar[5] - y * bar[7]) - b * y * bar[8],
             ROOT_THREE * bar[3] + a * (y * bar[5] + x * bar[6]) + 2.0 * b * z * bar[8],
         ]
     )
+
+
+def harmonics_dot(unit, dunit):
+    return jnp.stack(harmonics_dot_rows(unit, dunit))
+
+
+def harmonics_back(unit, bar):
+    return jnp.stack(harmonics_back_rows(unit, bar))
 
 
 def silu(v):
@@ -514,6 +522,16 @@
 NT = ((1,), (1,))
 
 
+def exact(left, ends, dims=((1,), (0,))):
+    high, low = split(left)
+    rest = left - high.astype(jnp.float32) - low.astype(jnp.float32)
+    return (
+        one_pass(high, ends, dims)
+        + one_pass(low, ends, dims)
+        + one_pass(rest.astype(jnp.bfloat16), ends, dims)
+    )
+
+
 def kernel_call(
     body,
     ins,
@@ -643,12 +661,16 @@
         for part, ref in enumerate(refs):
             view = ref.at[rows, :] if index is None else ref.at[index, rows, :]
             copy = pltpu.make_async_copy(
-                view, self.r.held.at[step % 2, part], self.r.arrived.at[step % 2, part]
+                view, self.r.held.at[step % 2, part, pl.ds(0, HALF)], self.r.arrived.at[step % 2, part]
             )
             copy.start() if start else copy.wait()
 
-    def product(self, right, store, extra=None):
+    def product(self, right, store, extra=None, beside=None):
         held = self.r.held
+        if beside is not None:
+            (weight, target), tail = beside, HALF + beside[0][0].shape[0]
+            for part in range(2):
+                held[1, part, HALF:tail, :] = weight[part][...]
         for half in range(2):
             step = self.step
             self.step += 1
@@ -656,15 +678,25 @@
                 self.copies(step + 1, True)
             self.copies(step, False)
             rows = pl.ds(half * HALF, HALF)
-            acc = three_pass((held[half, 0], held[half, 1]), pair(right))
+            end = tail if half and beside is not None else HALF
+            acc = three_pass((held[half, 0, 0:end, :], held[half, 1, 0:end, :]), pair(right))
+            if end > HALF:
+                target[...] = acc[HALF:, :]
+                acc = acc[:HALF, :]
             if extra is not None:
                 acc = acc + three_pass(pair(extra[0], rows), extra[1])
             store[rows, :] = acc
 
 
+def add_small(store, weight, right):
+    for half in range(2):
+        rows = pl.ds(half * HALF, HALF)
+        store[rows, :] += three_pass(pair(weight, rows), right)
+
+
 def stream_scratch():
     return dict(
-        held=pltpu.VMEM((2, 2, HALF, D), jnp.bfloat16),
+        held=pltpu.VMEM((2, 2, HALF + BS, D), jnp.bfloat16),
         arrived=pltpu.SemaphoreType.DMA((2, 2)),
     )
 
@@ -856,7 +888,7 @@
     r.need(r.out0)
     (per1,) = each(lat1, (nothing,))
     r.send(r.lat1)
-    r.w1[...] = three_pass(pair(r.env1w), pair(r.lat1))
+    stream.product(r.lat1, r.pre2, beside=(r.env1w, r.w1))
 
     def embed(base, lane):
         w = r.w1[pl.ds(base, 16), lane]
@@ -879,7 +911,7 @@
         r.res1[pl.ds(base, 16), lane] = sum(a * b for a, b in zip(f, e)) * (1.0 / 3.0)
 
     planes(channels, edges, scalar)
-    stream.product(r.lat1, r.pre2, (r.sc1_t, split(r.res1[...])))
+    add_small(r.pre2, r.sc1_t, split(r.res1[...]))
 
     def act2(rows, per):
         act, slope = silu_parts(r.pre2[rows, :])
@@ -904,10 +936,9 @@
     r.fetch(r.feat1, r.env1)
     clear_tail(r, rows9)
     nothing = jnp.zeros((8, edges), jnp.float32)
-    stream.product(r.pre2_bar, r.lat1_bar)
+    stream.product(r.pre2_bar, r.lat1_bar, beside=(r.sc1, r.res1_bar))
     r.fetch(r.out1, r.mix_t, r.pre1)
     r.need(r.feat1, r.env1)
-    r.res1_bar[...] = three_pass(pair(r.sc1), pair(r.pre2_bar))
 
     def back1(base, lane):
         g = r.res1_bar[pl.ds(base, 16), lane] * (1.0 / 3.0)
@@ -965,8 +996,8 @@
     r.need(r.pre1)
     each(pre1_bar)
     r.send(r.pre1_bar)
-    stream.product(r.pre1_bar, r.lat0_bar)
-    r.res0_bar[0:channels, :] += three_pass(pair(r.sc0), pair(r.pre1_bar))
+    stream.product(r.pre1_bar, r.lat0_bar, beside=(r.sc0, r.w0_bar))
+    r.res0_bar[0:channels, :] += r.w0_bar[...]
     r.send(r.res0_bar)
     r.fetch(r.pre0)
 
@@ -1018,12 +1049,20 @@
     r.send(r.pre0_bar)
     r.bessel_bar[...] = three_pass(pair(r.in_w), pair(r.pre0_bar))
     down = lambda v: jnp.sum(v, axis=0, keepdims=True)
-    r.env_bar[...] = jnp.zeros_like(r.env_bar)
-    r.env_bar[0:1, :] = (
+    env_bar = (
         RES * factor() * (r.per[0:1, :] + 2.0 * env() * r.per[1:2, :])
         + RES * down(env_bar1)
         + down(env_bar0)
     )
+    row = lambda ref, k: ref[k : k + 1, :]
+    unit = [row(r.geo, k) for k in range(3)]
+    dist_bar = env_bar * row(r.geo, 4) + down(r.bessel_bar[0:NB, :] * r.dbessel[0:NB, :])
+    unit_bar = harmonics_back_rows(unit, [row(r.shape_bar, k) for k in range(9)])
+    along = sum(u * b for u, b in zip(unit, unit_bar))
+    r.vec_bar[...] = jnp.zeros_like(r.vec_bar)
+    for k in range(3):
+        r.vec_bar[k : k + 1, :] = dist_bar * unit[k] + (unit_bar[k] - unit[k] * along) * row(r.geo, 3)
+    r.force_part[...] = exact(r.vec_bar[...], r.ends[...])
 
 
 def tangent_up(r, channels, edges, scale):
@@ -1031,7 +1070,7 @@
     env, factor, env_dot = (
         lambda: r.rows[0:1, :],
         lambda: r.rows[1:2, :],
-        lambda: r.rows[2:3, :],
+        lambda: r.env_row[0:1, :],
     )
     lead = lambda: RES * env() * env() * factor()
     lead_dot = lambda: 2.0 * RES * env() * factor() * env_dot()
@@ -1047,6 +1086,22 @@
     r.fetch(r.pre0, r.out0)
     clear_tail(r, rows9)
     nothing = jnp.zeros((8, edges), jnp.float32)
+    row = lambda ref, k: ref[k : k + 1, :]
+    residual = [row(r.force, k) - row(r.label, k) for k in range(3)]
+    r.loss_part[...] = row(r.label, 3) * sum(v * v for v in residual)
+    r.cot[...] = jnp.zeros_like(r.cot)
+    for k in range(3):
+        r.cot[k : k + 1, :] = row(r.label, 4) * residual[k]
+    vec_dot = exact(r.cot[...], r.ends[...], NT)
+    vec_dot = [vec_dot[k : k + 1, :] for k in range(3)]
+    unit = [row(r.geo, k) for k in range(3)]
+    dist_dot = sum(u * v for u, v in zip(unit, vec_dot))
+    unit_dot = [(v - u * dist_dot) * row(r.geo, 3) for u, v in zip(unit, vec_dot)]
+    r.env_row[...] = jnp.broadcast_to(row(r.geo, 4) * dist_dot, r.env_row.shape)
+    r.bessel_dot[...] = r.dbessel[...] * dist_dot
+    r.shape_dot[...] = jnp.zeros_like(r.shape_dot)
+    for k, value in enumerate(harmonics_dot_rows(unit, unit_dot)):
+        r.shape_dot[k : k + 1, :] = value
     bessel = split(r.bessel_dot[...])
 
     @pl.loop(0, 2)
@@ -1075,7 +1130,7 @@
     each(lat0)
     r.send(r.lat0_dot)
     r.fetch(r.pre1, r.out1)
-    r.w0_dot[...] = three_pass(pair(r.env0w), pair(r.lat0_dot))
+    stream.product(r.lat0_dot, r.pre1_dot, beside=(r.env0w, r.w0_dot))
 
     def embed_dot(w_ref, w_dot_ref, base, lane):
         w, wd = w_ref[pl.ds(base, 16), lane], w_dot_ref[pl.ds(base, 16), lane]
@@ -1107,7 +1162,7 @@
     planes(channels, edges, multiply)
     r.send(r.res0_dot)
     r.fetch(r.lat1, r.mix)
-    stream.product(r.lat0_dot, r.pre1_dot, (r.sc0_t, split(r.res0_dot[0:channels, :])))
+    add_small(r.pre1_dot, r.sc0_t, split(r.res0_dot[0:channels, :]))
 
     def act1(rows):
         put(r.act1_dot, rows, r.pre1_dot[rows, :] * silu_parts(r.pre1[rows, :])[1])
@@ -1133,7 +1188,7 @@
     r.need(r.out1, r.lat1)
     (per1,) = each(lat1, (nothing,))
     r.send(r.lat1_dot)
-    r.w1_dot[...] = three_pass(pair(r.env1w), pair(r.lat1_dot))
+    stream.product(r.lat1_dot, r.tmp, beside=(r.env1w, r.w1_dot))
 
     def embed1(base, lane):
         put9_split(r, channels, base, lane, embed_dot(r.w1, r.w1_dot, base, lane))
@@ -1158,7 +1213,7 @@
         r.res1_dot[pl.ds(base, 16), lane] = total * (1.0 / 3.0)
 
     planes(channels, edges, scalar)
-    stream.product(r.lat1_dot, r.tmp, (r.sc1_t, split(r.res1_dot[...])))
+    add_small(r.tmp, r.sc1_t, split(r.res1_dot[...]))
 
     def act2(rows, per):
         v, vd, top = r.pre2[rows, :], r.tmp[rows, :], r.top[rows, :]
@@ -1184,7 +1239,7 @@
     env, factor, env_dot = (
         lambda: r.rows[0:1, :],
         lambda: r.rows[1:2, :],
-        lambda: r.rows[2:3, :],
+        lambda: r.env_row[0:1, :],
     )
     stream = Stream(
         r,
@@ -1197,10 +1252,9 @@
     )
     r.fetch(r.feat1, r.feat1_dot, r.env1, r.env1_dot)
     clear_tail(r, rows9)
-    stream.product(r.pre2_hat, r.hat1)
+    stream.product(r.pre2_hat, r.hat1, beside=(r.sc1, r.small))
     r.fetch(r.emb1_bar, r.lat1_bar)
     r.need(r.feat1, r.feat1_dot, r.env1, r.env1_dot)
-    r.small[...] = three_pass(pair(r.sc1), pair(r.pre2_hat))
 
     def back1(base, lane):
         gh = r.small[pl.ds(base, 16), lane] * (1.0 / 3.0)
@@ -1267,8 +1321,8 @@
     each(pre1)
     r.send(r.pre1_hat)
     r.fetch(r.emb0_bar, r.lat0_bar)
-    stream.product(r.pre1_hat, r.tmp)
-    r.res0_hat[0:channels, :] += three_pass(pair(r.sc0), pair(r.pre1_hat))
+    stream.product(r.pre1_hat, r.tmp, beside=(r.sc0, r.small))
+    r.res0_hat[0:channels, :] += r.small[...]
 
     def embed_pair(base, lane):
         w, wd = r.w0[pl.ds(base, 16), lane], r.w0_dot[pl.ds(base, 16), lane]
@@ -1427,7 +1481,7 @@
             r.flat[slot, 0, :, part] = high
             r.flat[slot, 1, :, part] = low
             r.turned[slot, 0, part, :] = one_pass(eye, high, NT).astype(jnp.bfloat16)
-            r.turned[slot, 1, part, :] = one_pass(eye, low, NT).astype(jnp.bfloat16)
+            r.turned[slot, 1, part, :] = low.T
         for copy in outgoing(step):
             copy.start()
 
@@ -1568,7 +1622,7 @@
 
 def soap_update(arrays):
     slots = arrays[0].shape[0]
-    count = 2 if slots % 2 == 0 else 1
+    count = 4 if slots % 4 == 0 else 1
     spec = pl.BlockSpec((count, BS, BS), lambda s: (s, 0, 0))
     return pl.pallas_call(
         partial(soap_kernel, count),
@@ -1642,7 +1696,7 @@
     return jnp.concatenate(rows, axis=0)
 
 
-def fast_chain(weights, every, inverse, targets, which, where, scale, force_to_tangent, vec, live, src, ss, st):
+def fast_chain(weights, every, inverse, targets, which, where, scale, add_up, label, ends, vec, live, src, ss, st):
     pair_in, pair_out, env_weight, scalar_weight, mix_weight, energy_head = weights
     channels, edges = env_weight.shape[1], vec.shape[1]
     rows9 = 9 * channels
@@ -1654,6 +1708,8 @@
     shape = pad_rows(harmonics(unit), 16)
     feat = jnp.concatenate([bessel, ss, st], axis=0)
     rows = pad_rows(jnp.stack([env, factor]), 8)
+    geo = pad_rows(jnp.concatenate([unit, inv[None], denv[None]], axis=0), 8)
+    dbessel_rows = pad_rows(dbessel, 2 * NB)
     same = (src[:, None] == src[None]).astype(jnp.bfloat16)
     cut = split_outside
     in_t, in_w, out_t, out_w = cut(pair_in.T), cut(pair_in), cut(pair_out.T), cut(pair_out)
@@ -1737,6 +1793,9 @@
             rows=rows,
             same=same,
             head=head_col,
+            geo=geo,
+            dbessel=dbessel_rows,
+            ends=ends,
             w0=one.w0,
             w1=up.w1,
             per=up.per,
@@ -1752,10 +1811,10 @@
             w1_bar=f32(*narrow),
             w0_bar=f32(*narrow),
             shape_bar=f32(16, edges),
-            env_bar=f32(8, edges),
+            force_part=f32(8, ends.shape[1]),
             bessel_bar=f32(16, edges),
         ),
-        temps,
+        dict(**temps, vec_bar=pltpu.VMEM((8, edges), jnp.float32)),
         late=dict(
             pre0=one.pre0,
             out0=one.out0,
@@ -1783,25 +1842,18 @@
         hbm=dict(m=loaded.m, out=out_w),
         flops=4 * unit_flops,
     )
-    dist_bar = down.env_bar[0] * denv + jnp.sum(down.bessel_bar[:NB] * dbessel, axis=0)
-    unit_bar = harmonics_back(unit, down.shape_bar)
-    along = jnp.sum(unit * unit_bar, axis=0)
-    vec_bar = dist_bar[None] * unit + (unit_bar - unit * along[None]) * inv[None]
-    vec_dot, loss = force_to_tangent(vec_bar)
-    dist_dot = jnp.sum(unit * vec_dot, axis=0)
-    unit_dot = (vec_dot - unit * dist_dot[None]) * inv[None]
-    env_dot = denv * dist_dot
-    bessel_dot = pad_rows(dbessel * dist_dot[None], 2 * NB)
-    shape_dot = pad_rows(harmonics_dot(unit, unit_dot), 16)
-    rows = pad_rows(jnp.stack([env, factor, env_dot]), 8)
+    force = add_up(down.force_part)
     tan = kernel_call(
         lambda r: tangent_up(r, *args),
         dict(
             shape=shape,
             rows=rows,
             same=same,
-            shape_dot=shape_dot,
-            bessel_dot=bessel_dot,
+            geo=geo,
+            dbessel=dbessel_rows,
+            ends=ends,
+            force=force,
+            label=label,
             head=head_col,
             top=loaded.top,
             w0=one.w0,
@@ -1819,9 +1871,14 @@
             head_part=f32(D, 128),
             last_part=f32(D, 128),
             per_dot=f32(8, edges),
+            env_row=f32(8, edges),
+            shape_dot=f32(16, edges),
+            bessel_dot=f32(2 * NB, edges),
+            loss_part=f32(1, ends.shape[1]),
         ),
         dict(
             **temps,
+            cot=pltpu.VMEM((8, ends.shape[1]), jnp.float32),
             tmp=pltpu.VMEM(wide, jnp.float32),
             keep=pltpu.VMEM(wide, jnp.float32),
         ),
@@ -1859,7 +1916,8 @@
             shape=shape,
             rows=rows,
             same=same,
-            shape_dot=shape_dot,
+            shape_dot=tan.shape_dot,
+            env_row=tan.env_row,
             head=head_col,
             pre2_hat=tan.pre2_hat,
             w0=one.w0,
@@ -1909,6 +1967,8 @@
         hbm=dict(m=loaded.m, out=out_w),
         flops=4 * unit_flops,
     )
+    env_dot = tan.env_row[0]
+    loss = jnp.sum(tan.loss_part)
     lead_sum = jnp.sum(tan.last_part, axis=1)
     head_grad = RES * jnp.sum(tan.head_part, axis=1) + jnp.sum(
         lead_sum[:, None] * loaded.last, axis=0
@@ -1955,7 +2015,7 @@
         lambda r: small_gradients(r, channels, edges),
         dict(
             feat=feat,
-            bessel_dot=bessel_dot,
+            bessel_dot=tan.bessel_dot,
             hid_dot=tan.hid_dot,
             out0_bar=down.out0_bar,
             w0_bar=down.w0_bar,
@@ -2176,9 +2236,14 @@
         ),
     )
     every_block, general_loss = lax.optimization_barrier((every_block, general_loss))
-    _, my_ss, my_st, my_force = views(my_source, my_target)
+    _, my_ss, my_st, _ = views(my_source, my_target)
+    my_ends = (my_source[:, None] == atom_ids[None]).astype(jnp.bfloat16)
+    my_ends = my_ends - (my_target[:, None] == atom_ids[None]).astype(jnp.bfloat16)
+    labels_all = jnp.concatenate([label_all, 2.0 * label_mask[None] / label_total], axis=0)
+    labels_all = jnp.pad(labels_all, ((0, 8 - labels_all.shape[0]), (0, 0)))
+    add_up = lambda part: sum_small(part, sizes)
     fast = fast_chain(
-        weights, every_block, inverse, targets, which, where, scale, my_force, my_vec, my_live, my_source, my_ss, my_st
+        weights, every_block, inverse, targets, which, where, scale, add_up, labels_all, my_ends, my_vec, my_live, my_source, my_ss, my_st
     )
 
     small, head_part, fast_loss, made = fast

time: 627 us -> 618 us (0.986)
  transfers between devices with their start and end apart: 42 -> 42, of which waited for: 23 -> 21; matrix products, arithmetic and copies ran while one was open for 15% -> 16% of each run, Pallas kernels for 9% -> 8%
where the time goes in v3:
time: 618 us; the launch traced here: 606 us
  Pallas kernels  265 us (43%)
  waiting for transfers between devices  125 us (20%)
  other arithmetic  76.7 us (12%)
  starting transfers between devices  62.2 us (10%)
  local copies, waits for them, and re-layouts  47.2 us (8%)
  between operations  18.7 us (3%)
  loops' own time  8.11 us (1%)
    pallas_call x8, Pallas kernels, kernel_call(): pl.pallas_call(kernel, out_shape=out_leaves, in_specs=in_specs, out_specs...  253 us
    ppermute x40, waiting for transfers between devices, hop(): return lax.ppermute(value, AX, pairs)  85.7 us
    ppermute x40, starting transfers between devices, hop(): return lax.ppermute(value, AX, pairs)  62.1 us
    all_gather x1, waiting for transfers between devices, local(): every_block = lax.all_gather(soap_weight, AX, axis=0, tiled=True)  19.5 us
    psum x1, waiting for transfers between devices, local(): summed = lax.psum(local_sums, AX)  19.2 us
    sub x6, other arithmetic, adamw(): return (weight - 0.01 * (normal + 0.01 * weight), first_new, second_new)  15.7 us
  transfers between devices with their start and end apart: 42, of which 21 were waited for; matrix products, arithmetic and copies ran while one was open for 16% of the time, Pallas kernels for 8%

profile of v3, /device:TPU:0, one launch (start us, length us, event | category | flops | bytes accessed | tf_op | source)
XLA Modules:
  0.0 606.4 jit_solution(1083916874026130434)
XLA Ops:
  12.1 3.0 collective-permute-start.33
  16.7 5.4 copy.249
  40.1 3.0 fusion.927
  51.0 4.5 collective-permute-done.36
  55.5 4.8 collective-permute-done.37
  73.9 5.4 copy.245
  80.3 4.2 convert_reduce_fusion
  84.5 4.7 gather_fusion.3
  100.3 13.0 %shard_map.591 = (f32[64,512]{1,0:T(8,128)}, f32[576,512]{1,0:T(8,128)}, bf16[1024,512]{1,0:T(8,128)(2,1)}, bf16[1024,512]{1,0:T(8,128)(2,1)}, bf16[1024,512]{1,...) custom-call(bf16[64,1024]{1,0:T(8,128)(2,1)} %get-tuple-element.1003, ...), custom_call_target="tpu_custom_call" | custom-call | flops 3221225472 | bytes 16007168 | tf_op jit(solution)/shard_map/pallas_call | solution.py:613
  113.3 19.5 %all-gather.2.cloned.1.call-done.refs_2_ = f32[256,128,128]{2,1,0:T(8,128)} async-done(((f32[8,128,128]{2,1,0:T(8,128)}), f32[256,128,128]{2,1,0:T(8,128)}) %all-gather.2.cloned.1.call-update) | async-done | bytes 16777232 | tf_op jit(solution)/shard_map/all_gather | solution.py:2166
  138.5 8.1 %while.24 = (pred[]{:T(512)}, f32[8,128,128]{2,1,0:T(8,128)}, f32[32,1024]{1,0:T(8,128)}, f32[1024,1024]{1,0:T(8,128)}, f32[128,1024]{1,0:T(8,128)}, /*index=5*/...) while((pred[]{:T(512)}, f32[8,128,128]{2,1,0:T(8,128)}, ...), condition=%region_51.52_spmd.clone.clone, body=%region_13.51_spmd.clone.clone | while | flops 97740455936 | bytes 1994839040 | solution.py:2228
  146.6 22.7 %shard_map.592 = (f32[1024,1024]{1,0:T(8,128)}, f32[1024,1]{1,0:T(8,128)}, bf16[3,1024,1024]{2,1,0:T(8,128)(2,1)}, bf16[3,1024,1024]{2,1,0:T(8,128)(2,1)}, bf16[...) custom-call(f32[1,1024]{1,0:T(1,128)} %bitcast.2042, s32[256]{0:T(256)} %select_reduce_fusion.refs_1_, ...), custom_call_target="tpu_custom_call" | custom-call | bytes 46146560 | tf_op jit(solution)/shard_map/pallas_call | solution.py:613
  169.4 27.6 %shard_map.593 = (f32[8,512]{1,0:T(8,128)}, f32[64,512]{1,0:T(8,128)}, f32[64,512]{1,0:T(8,128)}, bf16[1024,512]{1,0:T(8,128)(2,1)}, bf16[1024,512]{1,0:T(8,128)...) custom-call(bf16[64,1024]{1,0:T(8,128)(2,1)} %get-tuple-element.1002, ...), custom_call_target="tpu_custom_call" | custom-call | flops 9663676416 | bytes 36020224 | tf_op jit(solution)/shard_map/pallas_call | solution.py:613
  197.0 40.9 %shard_map.594 = (f32[16,512]{1,0:T(8,128)}, f32[8,512]{1,0:T(8,128)}, f32[64,512]{1,0:T(8,128)}, f32[16,512]{1,0:T(8,128)}, f32[64,512]{1,0:T(8,128)}, /*index=...) custom-call(f32[16,512]{1,0:T(8,128)} %pad.101.refs_0_, ...), custom_call_target="tpu_custom_call" | custom-call | flops 12884901888 | bytes 56791040 | tf_op jit(solution)/shard_map/pallas_call | solution.py:613
  255.0 45.5 %shard_map.595 = (f32[16,512]{1,0:T(8,128)}, f32[8,512]{1,0:T(8,128)}, f32[1024,128]{1,0:T(8,128)}, f32[1024,128]{1,0:T(8,128)}, f32[1,512]{1,0:T(1,128)}, /*ind...) custom-call(f32[16,512]{1,0:T(8,128)} %pad.101.refs_0_, ...), custom_call_target="tpu_custom_call" | custom-call | flops 12884901888 | bytes 57878528 | tf_op jit(solution)/shard_map/pallas_call | solution.py:613
  302.7 45.0 %shard_map.596 = (f32[64,512]{1,0:T(8,128)}, f32[64,512]{1,0:T(8,128)}, f32[576,512]{1,0:T(8,128)}, bf16[1024,512]{1,0:T(8,128)(2,1)}, bf16[1024,512]{1,0:T(8,12...) custom-call(bf16[1024,64]{1,0:T(8,128)(2,1)} %get-tuple-element.993., ...), custom_call_target="tpu_custom_call" | custom-call | flops 12884901888 | bytes 59641856 | tf_op jit(solution)/shard_map/pallas_call | solution.py:613
  347.8 32.0 %shard_map.597 = (f32[32,128,128]{2,1,0:T(8,128)}, f32[32,128,128]{2,1,0:T(8,128)}, f32[32,128,128]{2,1,0:T(8,128)}, f32[32,128,128]{2,1,0:T(8,128)}, f32[32,128...) custom-call(f32[1,1024]{1,0:T(1,128)} %bitcast.2043, ...), custom_call_target="tpu_custom_call" | custom-call | flops 19327352832 | bytes 41953280 | tf_op jit(solution)/shard_map/pallas_call | solution.py:613
  380.9 26.1 %shard_map.598 = (f32[2,64,1024]{2,1,0:T(8,128)}, f32[16,1024]{1,0:T(8,128)}, f32[3,64,64]{2,1,0:T(8,128)}, f32[2,64,1024]{2,1,0:T(8,128)}, f32[1024,1024]{1,0:T(8,128)}) custom-call(f32[16,512]{1,0:T(8,128)} %get-tuple-element.375.refs_0_, f32[16,512]{1,0:T(8,128)} %pad_maximum_fusion.20.refs_2_.refs_1_, bf16[1024,512]{1,0:T(8,128)(2,1)} %get-tuple-element.413.refs_2_, ...), custom_call_target="tpu_custom_call" | custom-call | flops 6442450944 | bytes 40288256 | tf_op jit(solution)/shard_map/pallas_call | solution.py:613
  430.0 7.3 %collective-permute-done.49 = f32[2,4,128,128]{3,2,1,0:T(8,128)} collective-permute-done((f32[2,4,128,128]{3,2,1,0:T(8,128)}, f32[2,4,128,128]{3,2,1,0:T(8,128)}, u32[]{:S(2)}, u32[]{:S(2)}) %collective-permute-start.49) | collective-permute-done | bytes 524320 | tf_op jit(solution)/shard_map/ppermute | solution.py:140
  437.3 4.5 collective-permute-done.50
  446.2 8.4 %collective-permute-done.57 = f32[2,4,128,128]{3,2,1,0:T(8,128)S(1)} collective-permute-done((f32[2,4,128,128]{3,2,1,0:T(8,128)S(1)}, f32[2,4,128,128]{3,2,1,0:T(8,128)S(1)}, u32[]{:S(2)}, u32[]{:S(2)}) %collective-permute-start.57) | collective-permute-done | bytes 524320 | tf_op jit(solution)/shard_map/ppermute | solution.py:140
  459.1 3.4 collective-permute-done.64
  463.1 12.0 %collective-permute-done.65 = f32[4,128,128]{2,1,0:T(8,128)S(1)} collective-permute-done((f32[4,128,128]{2,1,0:T(8,128)S(1)}, f32[4,128,128]{2,1,0:T(8,128)S(1)}, u32[]{:S(2)}, u32[]{:S(2)}) %collective-permute-start.65) | collective-permute-done | bytes 262176 | tf_op jit(solution)/shard_map/ppermute | solution.py:140
  477.2 3.5 collective-permute-done.69
  484.5 7.6 %collective-permute-done.59 = f32[2,4,128,128]{3,2,1,0:T(8,128)S(1)} collective-permute-done((f32[2,4,128,128]{3,2,1,0:T(8,128)S(1)}, f32[2,4,128,128]{3,2,1,0:T(8,128)S(1)}, u32[]{:S(2)}, u32[]{:S(2)}) %collective-permute-start.59) | collective-permute-done | bytes 524320 | tf_op jit(solution)/shard_map/ppermute | solution.py:140
  497.5 8.7 %collective-permute-done.70 = f32[8,128,128]{2,1,0:T(8,128)S(1)} collective-permute-done((f32[8,128,128]{2,1,0:T(8,128)S(1)}, f32[8,128,128]{2,1,0:T(8,128)S(1)}, u32[]{:S(2)}, u32[]{:S(2)}) %collective-permute-start.70) | collective-permute-done | bytes 524320 | tf_op jit(solution)/shard_map/ppermute | solution.py:140
  509.7 21.6 %collective-permute-start.63 = (f32[8,128,128]{2,1,0:T(8,128)}, f32[8,128,128]{2,1,0:T(8,128)}, u32[]{:S(2)}, u32[]{:S(2)}) collective-permute-start(f32[8,128,128]{2,1,0:T(8,128)} %get-tuple-element.972), channel_id=1, source_target_pairs={{0,2},{1,3},{8,10},{9,11},{16,18},{17,19},{24,26},{25,27},{6,4},{7... | collective-permute-start | bytes 1572872 | tf_op jit(solution)/shard_map/ppermute | solution.py:140
  536.2 3.9 collective-permute-done.54
  542.7 4.2 collective-permute-done.72
  548.7 11.8 %shard_map.599 = (f32[8,128,128]{2,1,0:T(8,128)}, f32[8,128,128]{2,1,0:T(8,128)}, f32[8,128,128]{2,1,0:T(8,128)}, f32[8,128,128]{2,1,0:T(8,128)}, f32[8,128,128]...) custom-call(f32[8,128,128]{2,1,0:T(8,128)S(1)} %fusion.957.refs_0_, ...), custom_call_target="tpu_custom_call" | custom-call | tf_op jit(solution)/shard_map/pallas_call | solution.py:1627
  560.5 19.2 %all-reduce.39.cloned.1.call-done = (f32[32,1024]{1,0:T(8,128)}, f32[1024,1024]{1,0:T(8,128)}, f32[128,1024]{1,0:T(8,128)}, f32[128,1024]{1,0:T(8,128)}) async-done(((f32[32,1024]{1,0:T(8,128)}, f32[1024,1024]{1,0:T(8,128)}, f32[128,1024]{1,0:T(8,128)}, f32[128,1024]{1,0:T(8,128)}), (f32[32,1024]{1,0:T(8,128)}, f32[1024,1024]{1,0:T(8,128)}, f32[128,1024]{1,0:T(8,128)}, ...) | async-done | bytes 5373968 | tf_op jit(solution)/shard_map/psum | solution.py:2252
  589.1 9.1 %multiply_subtract_fusion.1 = (f32[1024,1024]{1,0:T(8,128)}, f32[1024,1024]{1,0:T(8,128)}, f32[1024,1024]{1,0:T(8,128)}) fusion(f32[1024,1024]{1,0:T(8,128)S(1)} %copy-done.73, f32[1024,1024]{1,0:T(8,128)} %get-tuple-element.474, f32[1024,1024]{1,0:T(8,128)S(1)} %copy-done.187, pred[]{:T(512)S(6)} %le.37, f32[1024,1024]{1,0:T(8,128)} %param.60, ...), kind=kLoop, calls=%fused_computation.1245 | loop fusion | flops 16777216 | bytes 33554432 | tf_op jit(solution)/shard_map/sub | solution.py:1645
  (352 shorter events, 147.1 us)
Async XLA Ops:
  7.2 125.6 %all-gather.2.cloned.1.call-start = ((), (), s32[]{:S(2)}) async-start(), calls=%async_computation | async-start | bytes 17301504 | tf_op jit(solution)/shard_map/all_gather | solution.py:2166
  12.1 33.9 %collective-permute-start.33 = (f32[7,512]{1,0:T(8,128)S(1)}, f32[7,512]{1,0:T(8,128)S(1)}, u32[]{:S(2)}, u32[]{:S(2)}) collective-permute-start(f32[7,512]{1,0:T(8,128)S(1)} %concatenate.92), channel_id=1, source_target_pairs={{0,8},{1,9},{2,10},{3,11},{4,12},{5,13},{6,14},{7,15},{8,0},{9,1},... | collective-permute-start | bytes 43016 | tf_op jit(solution)/shard_map/ppermute | solution.py:140
  15.1 30.9 %collective-permute-start.34 = (f32[7,512]{1,0:T(8,128)S(1)}, f32[7,512]{1,0:T(8,128)S(1)}, u32[]{:S(2)}, u32[]{:S(2)}) collective-permute-start(f32[7,512]{1,0:T(8,128)S(1)} %concatenate.92), channel_id=1, source_target_pairs={{0,16},{1,17},{2,18},{3,19},{4,20},{5,21},{6,22},{7,23},{8,24},{9,... | collective-permute-start | bytes 43016 | tf_op jit(solution)/shard_map/ppermute | solution.py:140
  16.7 29.4 %collective-permute-start.35 = (f32[7,512]{1,0:T(8,128)S(1)}, f32[7,512]{1,0:T(8,128)S(1)}, u32[]{:S(2)}, u32[]{:S(2)}) collective-permute-start(f32[7,512]{1,0:T(8,128)S(1)} %concatenate.92), channel_id=1, source_target_pairs={{0,24},{1,25},{2,26},{3,27},{4,28},{5,29},{6,30},{7,31},{8,16},{9,... | collective-permute-start | bytes 43016 | tf_op jit(solution)/shard_map/ppermute | solution.py:140
  46.1 9.4 %collective-permute-start.36 = (f32[4,7,512]{2,1,0:T(8,128)S(1)}, f32[4,7,512]{2,1,0:T(8,128)S(1)}, u32[]{:S(2)}, u32[]{:S(2)}) collective-permute-start(f32[4,7,512]{2,1,0:T(8,128)S(1)} %get-tuple-element.1018), channel_id=1, source_target_pairs={{0,2},{1,3},{8,10},{9,11},{16,18},{17,19},{24,26},{25,27},{2,0},{3... | collective-permute-start | bytes 172040 | tf_op jit(solution)/shard_map/ppermute | solution.py:140
  48.4 11.9 %collective-permute-start.37 = (f32[4,7,512]{2,1,0:T(8,128)S(1)}, f32[4,7,512]{2,1,0:T(8,128)S(1)}, u32[]{:S(2)}, u32[]{:S(2)}) collective-permute-start(f32[4,7,512]{2,1,0:T(8,128)S(1)} %get-tuple-element.1018), channel_id=1, source_target_pairs={{0,4},{1,5},{8,12},{9,13},{16,20},{17,21},{24,28},{25,29},{2,6},{3... | collective-permute-start | bytes 172040 | tf_op jit(solution)/shard_map/ppermute | solution.py:140
  51.0 9.3 %collective-permute-start.38 = (f32[4,7,512]{2,1,0:T(8,128)S(1)}, f32[4,7,512]{2,1,0:T(8,128)S(1)}, u32[]{:S(2)}, u32[]{:S(2)}) collective-permute-start(f32[4,7,512]{2,1,0:T(8,128)S(1)} %get-tuple-element.1018), channel_id=1, source_target_pairs={{0,6},{1,7},{8,14},{9,15},{16,22},{17,23},{24,30},{25,31},{2,4},{3... | collective-permute-start | bytes 172040 | tf_op jit(solution)/shard_map/ppermute | solution.py:140
  146.6 433.1 %all-reduce.39.cloned.1.call-start = ((), (), s32[]{:S(2)}) async-start(), calls=%async_computation.1 | async-start | bytes 10747904 | tf_op jit(solution)/shard_map/psum | solution.py:2252
  379.8 33.0 %collective-permute-start.48 = (f32[32,128,128]{2,1,0:T(8,128)}, f32[32,128,128]{2,1,0:T(8,128)S(1)}, u32[]{:S(2)}, u32[]{:S(2)}) collective-permute-start(f32[32,128,128]{2,1,0:T(8,128)} %get-tuple-element.449), channel_id=1, source_target_pairs={{0,1},{1,0},{2,3},{3,2},{4,5},{5,4},{6,7},{7,6},{8,9},{9,8},{10,11... | collective-permute-start | bytes 6291464 | tf_op jit(solution)/shard_map/ppermute | solution.py:140
  379.8 45.0 %collective-permute-start.47 = (f32[32,128,128]{2,1,0:T(8,128)}, f32[32,128,128]{2,1,0:T(8,128)}, u32[]{:S(2)}, u32[]{:S(2)}) collective-permute-start(f32[32,128,128]{2,1,0:T(8,128)} %get-tuple-element.447), channel_id=1, source_target_pairs={{0,1},{1,0},{2,3},{3,2},{4,5},{5,4},{6,7},{7,6},{8,9},{9,8},{10,11... | collective-permute-start | bytes 6291464 | tf_op jit(solution)/shard_map/ppermute | solution.py:140
  380.3 40.6 %collective-permute-start.56 = (f32[32,128,128]{2,1,0:T(8,128)}, f32[32,128,128]{2,1,0:T(8,128)}, u32[]{:S(2)}, u32[]{:S(2)}) collective-permute-start(f32[32,128,128]{2,1,0:T(8,128)} %get-tuple-element.453), channel_id=1, source_target_pairs={{0,1},{1,0},{2,3},{3,2},{4,5},{5,4},{6,7},{7,6},{8,9},{9,8},{10,11... | collective-permute-start | bytes 6291464 | tf_op jit(solution)/shard_map/ppermute | solution.py:140
  380.4 47.6 %collective-permute-start.55 = (f32[32,128,128]{2,1,0:T(8,128)}, f32[32,128,128]{2,1,0:T(8,128)}, u32[]{:S(2)}, u32[]{:S(2)}) collective-permute-start(f32[32,128,128]{2,1,0:T(8,128)} %get-tuple-element.452), channel_id=1, source_target_pairs={{0,1},{1,0},{2,3},{3,2},{4,5},{5,4},{6,7},{7,6},{8,9},{9,8},{10,11... | collective-permute-start | bytes 6291464 | tf_op jit(solution)/shard_map/ppermute | solution.py:140
  417.4 19.9 %collective-permute-start.49 = (f32[2,4,128,128]{3,2,1,0:T(8,128)}, f32[2,4,128,128]{3,2,1,0:T(8,128)}, u32[]{:S(2)}, u32[]{:S(2)}) collective-permute-start(f32[2,4,128,128]{3,2,1,0:T(8,128)} %slice_bitcast_fusion.116), channel_id=1, source_target_pairs={{0,8},{1,9},{2,10},{3,11},{4,12},{5,13},{6,14},{7,15},{8,0},{9,1},... | collective-permute-start | bytes 1572872 | tf_op jit(solution)/shard_map/ppermute | solution.py:140
  419.7 22.0 %collective-permute-start.50 = (f32[2,4,128,128]{3,2,1,0:T(8,128)}, f32[2,4,128,128]{3,2,1,0:T(8,128)}, u32[]{:S(2)}, u32[]{:S(2)}) collective-permute-start(f32[2,4,128,128]{3,2,1,0:T(8,128)} %slice_bitcast_fusion.114), channel_id=1, source_target_pairs={{0,16},{1,17},{2,18},{3,19},{4,20},{5,21},{6,22},{7,23},{8,24},{9,... | collective-permute-start | bytes 1572872 | tf_op jit(solution)/shard_map/ppermute | solution.py:140
  423.5 31.0 %collective-permute-start.57 = (f32[2,4,128,128]{3,2,1,0:T(8,128)S(1)}, f32[2,4,128,128]{3,2,1,0:T(8,128)S(1)}, u32[]{:S(2)}, u32[]{:S(2)}) collective-permute-start(f32[2,4,128,128]{3,2,1,0:T(8,128)S(1)} %slice_bitcast_fusion.110), channel_id=1, source_target_pairs={{0,8},{1,9},{2,10},{3,11},{4,12},{5,13},{6,14},{7,15},{8,0},{9,1},... | collective-permute-start | bytes 1572872 | tf_op jit(solution)/shard_map/ppermute | solution.py:140
  424.9 32.0 %collective-permute-start.58 = (f32[2,4,128,128]{3,2,1,0:T(8,128)S(1)}, f32[2,4,128,128]{3,2,1,0:T(8,128)S(1)}, u32[]{:S(2)}, u32[]{:S(2)}) collective-permute-start(f32[2,4,128,128]{3,2,1,0:T(8,128)S(1)} %slice_bitcast_fusion.108), channel_id=1, source_target_pairs={{0,16},{1,17},{2,18},{3,19},{4,20},{5,21},{6,22},{7,23},{8,24},{9,... | collective-permute-start | bytes 1572872 | tf_op jit(solution)/shard_map/ppermute | solution.py:140
  443.2 39.1 %collective-permute-start.51 = (f32[2,4,128,128]{3,2,1,0:T(8,128)S(1)}, f32[2,4,128,128]{3,2,1,0:T(8,128)S(1)}, u32[]{:S(2)}, u32[]{:S(2)}) collective-permute-start(f32[2,4,128,128]{3,2,1,0:T(8,128)S(1)} %slice_bitcast_fusion.119), channel_id=1, source_target_pairs={{0,8},{1,9},{2,10},{3,11},{4,12},{5,13},{6,14},{7,15},{8,0},{9,1},... | collective-permute-start | bytes 1572872 | tf_op jit(solution)/shard_map/ppermute | solution.py:140
  443.3 19.2 %collective-permute-start.64 = (f32[4,128,128]{2,1,0:T(8,128)S(1)}, f32[4,128,128]{2,1,0:T(8,128)S(1)}, u32[]{:S(2)}, u32[]{:S(2)}) collective-permute-start(f32[4,128,128]{2,1,0:T(8,128)S(1)} %get-tuple-element.456), channel_id=1, source_target_pairs={{0,16},{1,17},{2,18},{3,19},{4,20},{5,21},{6,22},{7,23},{8,24},{9,... | collective-permute-start | bytes 786440 | tf_op jit(solution)/shard_map/ppermute | solution.py:140
  444.9 30.2 %collective-permute-start.65 = (f32[4,128,128]{2,1,0:T(8,128)S(1)}, f32[4,128,128]{2,1,0:T(8,128)S(1)}, u32[]{:S(2)}, u32[]{:S(2)}) collective-permute-start(f32[4,128,128]{2,1,0:T(8,128)S(1)} %get-tuple-element.458), channel_id=1, source_target_pairs={{0,8},{1,9},{2,10},{3,11},{4,12},{5,13},{6,14},{7,15},{8,0},{9,1},... | collective-permute-start | bytes 786440 | tf_op jit(solution)/shard_map/ppermute | solution.py:140
  457.1 19.3 %collective-permute-start.68 = (f32[4,128,128]{2,1,0:T(8,128)S(1)}, f32[4,128,128]{2,1,0:T(8,128)S(1)}, u32[]{:S(2)}, u32[]{:S(2)}) collective-permute-start(f32[4,128,128]{2,1,0:T(8,128)S(1)} %get-tuple-element.460), channel_id=1, source_target_pairs={{0,16},{1,17},{2,18},{3,19},{4,20},{5,21},{6,22},{7,23},{8,24},{9,... | collective-permute-start | bytes 786440 | tf_op jit(solution)/shard_map/ppermute | solution.py:140
  457.8 23.0 %collective-permute-start.69 = (f32[4,128,128]{2,1,0:T(8,128)S(1)}, f32[4,128,128]{2,1,0:T(8,128)S(1)}, u32[]{:S(2)}, u32[]{:S(2)}) collective-permute-start(f32[4,128,128]{2,1,0:T(8,128)S(1)} %get-tuple-element.462), channel_id=1, source_target_pairs={{0,8},{1,9},{2,10},{3,11},{4,12},{5,13},{6,14},{7,15},{8,0},{9,1},... | collective-permute-start | bytes 786440 | tf_op jit(solution)/shard_map/ppermute | solution.py:140
  462.5 33.8 %collective-permute-start.53 = (f32[2,4,128,128]{3,2,1,0:T(8,128)S(1)}, f32[2,4,128,128]{3,2,1,0:T(8,128)S(1)}, u32[]{:S(2)}, u32[]{:S(2)}) collective-permute-start(f32[2,4,128,128]{3,2,1,0:T(8,128)S(1)} %slice_bitcast_fusion.112), channel_id=1, source_target_pairs={{0,16},{1,17},{2,18},{3,19},{4,20},{5,21},{6,22},{7,23},{8,24},{9,... | collective-permute-start | bytes 1572872 | tf_op jit(solution)/shard_map/ppermute | solution.py:140
  475.1 17.0 %collective-permute-start.59 = (f32[2,4,128,128]{3,2,1,0:T(8,128)S(1)}, f32[2,4,128,128]{3,2,1,0:T(8,128)S(1)}, u32[]{:S(2)}, u32[]{:S(2)}) collective-permute-start(f32[2,4,128,128]{3,2,1,0:T(8,128)S(1)} %slice_bitcast_fusion.118), channel_id=1, source_target_pairs={{0,8},{1,9},{2,10},{3,11},{4,12},{5,13},{6,14},{7,15},{8,0},{9,1},... | collective-permute-start | bytes 1572872 | tf_op jit(solution)/shard_map/ppermute | solution.py:140
  476.4 19.8 %collective-permute-start.61 = (f32[2,4,128,128]{3,2,1,0:T(8,128)S(1)}, f32[2,4,128,128]{3,2,1,0:T(8,128)S(1)}, u32[]{:S(2)}, u32[]{:S(2)}) collective-permute-start(f32[2,4,128,128]{3,2,1,0:T(8,128)S(1)} %slice_bitcast_fusion.106), channel_id=1, source_target_pairs={{0,16},{1,17},{2,18},{3,19},{4,20},{5,21},{6,22},{7,23},{8,24},{9,... | collective-permute-start | bytes 1572872 | tf_op jit(solution)/shard_map/ppermute | solution.py:140
  480.7 26.3 %collective-permute-start.66 = (f32[8,128,128]{2,1,0:T(8,128)S(1)}, f32[8,128,128]{2,1,0:T(8,128)S(1)}, u32[]{:S(2)}, u32[]{:S(2)}) collective-permute-start(f32[8,128,128]{2,1,0:T(8,128)S(1)} %pad_maximum_fusion.15), channel_id=1, source_target_pairs={{0,2},{1,3},{8,10},{9,11},{16,18},{17,19},{24,26},{25,27},{6,4},{7... | collective-permute-start | bytes 1572872 | tf_op jit(solution)/shard_map/ppermute | solution.py:140
  482.4 23.8 %collective-permute-start.70 = (f32[8,128,128]{2,1,0:T(8,128)S(1)}, f32[8,128,128]{2,1,0:T(8,128)S(1)}, u32[]{:S(2)}, u32[]{:S(2)}) collective-permute-start(f32[8,128,128]{2,1,0:T(8,128)S(1)} %pad_maximum_fusion.16), channel_id=1, source_target_pairs={{0,2},{1,3},{8,10},{9,11},{16,18},{17,19},{24,26},{25,27},{6,4},{7... | collective-permute-start | bytes 1572872 | tf_op jit(solution)/shard_map/ppermute | solution.py:140
  492.1 43.9 %collective-permute-start.52 = (f32[4,128,128]{2,1,0:T(8,128)}, f32[4,128,128]{2,1,0:T(8,128)S(1)}, u32[]{:S(2)}, u32[]{:S(2)}) collective-permute-start(f32[4,128,128]{2,1,0:T(8,128)} %slice_bitcast_fusion.130), channel_id=1, source_target_pairs={{0,16},{1,17},{2,18},{3,19},{4,20},{5,21},{6,22},{7,23},{8,24},{9,... | collective-permute-start | bytes 786440 | tf_op jit(solution)/shard_map/ppermute | solution.py:140
  496.2 12.3 %collective-permute-start.60 = (f32[4,128,128]{2,1,0:T(8,128)S(1)}, f32[4,128,128]{2,1,0:T(8,128)S(1)}, u32[]{:S(2)}, u32[]{:S(2)}) collective-permute-start(f32[4,128,128]{2,1,0:T(8,128)S(1)} %slice_bitcast_fusion.122), channel_id=1, source_target_pairs={{0,16},{1,17},{2,18},{3,19},{4,20},{5,21},{6,22},{7,23},{8,24},{9,... | collective-permute-start | bytes 786440 | tf_op jit(solution)/shard_map/ppermute | solution.py:140
  496.3 12.3 %collective-permute-start.62 = (f32[4,128,128]{2,1,0:T(8,128)S(1)}, f32[4,128,128]{2,1,0:T(8,128)S(1)}, u32[]{:S(2)}, u32[]{:S(2)}) collective-permute-start(f32[4,128,128]{2,1,0:T(8,128)S(1)} %slice_bitcast_fusion.120), channel_id=1, source_target_pairs={{0,8},{1,9},{2,10},{3,11},{4,12},{5,13},{6,14},{7,15},{8,0},{9,1},... | collective-permute-start | bytes 786440 | tf_op jit(solution)/shard_map/ppermute | solution.py:140
  507.1 33.9 %collective-permute-start.67 = (f32[8,128,128]{2,1,0:T(8,128)S(1)}, f32[8,128,128]{2,1,0:T(8,128)}, u32[]{:S(2)}, u32[]{:S(2)}) collective-permute-start(f32[8,128,128]{2,1,0:T(8,128)S(1)} %fusion.994), channel_id=1, source_target_pairs={{2,4},{3,5},{10,12},{11,13},{18,20},{19,21},{26,28},{27,29},{4,2},... | collective-permute-start | bytes 1572872 | tf_op jit(solution)/shard_map/ppermute | solution.py:140
  509.7 33.0 %collective-permute-start.63 = (f32[8,128,128]{2,1,0:T(8,128)}, f32[8,128,128]{2,1,0:T(8,128)}, u32[]{:S(2)}, u32[]{:S(2)}) collective-permute-start(f32[8,128,128]{2,1,0:T(8,128)} %get-tuple-element.972), channel_id=1, source_target_pairs={{0,2},{1,3},{8,10},{9,11},{16,18},{17,19},{24,26},{25,27},{6,4},{7... | collective-permute-start | bytes 1572872 | tf_op jit(solution)/shard_map/ppermute | solution.py:140
  531.3 15.6 %collective-permute-start.72 = (f32[8,128,128]{2,1,0:T(8,128)}, f32[8,128,128]{2,1,0:T(8,128)}, u32[]{:S(2)}, u32[]{:S(2)}) collective-permute-start(f32[8,128,128]{2,1,0:T(8,128)} %get-tuple-element.973), channel_id=1, source_target_pairs={{2,0},{3,1},{10,8},{11,9},{18,16},{19,17},{26,24},{27,25},{4,6},{5... | collective-permute-start | bytes 1572872 | tf_op jit(solution)/shard_map/ppermute | solution.py:140
  (57 other events, 603.6 us)
Sparse Core Ops, SparseCore 0:
  11.0 121.6 all-gather.1
  421.1 158.5 all-reduce.38

commit v4 on v3

--- a/solution.py
+++ b/solution.py
@@ -810,6 +810,9 @@
 def first_layer(r, channels, edges, scale):
     rows9 = 9 * channels
     stream = Stream(r, [(r.out_t, None)])
+    for ref in r.blank:
+        ref[...] = jnp.zeros_like(ref)
+    r.send(r.blank)
     feat = split(r.feat[...])
 
     @pl.loop(0, 2)
@@ -1696,7 +1699,7 @@
     return jnp.concatenate(rows, axis=0)
 
 
-def fast_chain(weights, every, inverse, targets, which, where, scale, add_up, label, ends, vec, live, src, ss, st):
+def fast_chain(weights, every, inverse, targets, which, where, scale, add_up, after_first, blank, label, ends, vec, live, src, ss, st):
     pair_in, pair_out, env_weight, scalar_weight, mix_weight, energy_head = weights
     channels, edges = env_weight.shape[1], vec.shape[1]
     rows9 = 9 * channels
@@ -1735,10 +1738,12 @@
             lat0=pair_of(*wide),
             env0=f32(*plane),
             res0=f32(*plane),
+            blank=tuple(f32(*shape) for shape in blank),
         ),
         hbm=dict(out_t=out_t),
         flops=unit_flops,
     )
+    every = after_first(one.blank, every)
     loaded = kernel_call(
         load_blocks,
         dict(head=head[None]),
@@ -2223,19 +2228,17 @@
         return (jnp.asarray(False), own, lax.psum(parts, AX), out[7])
 
     rest_rows = 8 * (-(-(mix_weight.size + energy_head.shape[0]) // (8 * D))) + 2 * NB
-    zeros = lambda n: jnp.zeros((n, D), jnp.float32)
     wide_rows = env_weight.shape[0] * env_weight.shape[1]
-    _, general_own, general_shared, general_loss = lax.while_loop(
-        lambda state: state[0],
-        replace,
-        (
-            jnp.logical_not(fits),
-            jnp.zeros_like(soap_weight),
-            (zeros(rest_rows), zeros(D), zeros(wide_rows), zeros(wide_rows)),
-            jnp.zeros((), jnp.float32),
-        ),
-    )
-    every_block, general_loss = lax.optimization_barrier((every_block, general_loss))
+    blank = (soap_weight.shape, (rest_rows, D), (D, D), (wide_rows, D), (wide_rows, D))
+    general_out = []
+
+    def after_first(empty, every):
+        state = (jnp.logical_not(fits), empty[0], tuple(empty[1:]), jnp.zeros((), jnp.float32))
+        _, own, shared, loss = lax.while_loop(lambda state: state[0], replace, state)
+        every, loss = lax.optimization_barrier((every, loss))
+        general_out.extend((own, shared, loss))
+        return every
+
     _, my_ss, my_st, _ = views(my_source, my_target)
     my_ends = (my_source[:, None] == atom_ids[None]).astype(jnp.bfloat16)
     my_ends = my_ends - (my_target[:, None] == atom_ids[None]).astype(jnp.bfloat16)
@@ -2243,10 +2246,11 @@
     labels_all = jnp.pad(labels_all, ((0, 8 - labels_all.shape[0]), (0, 0)))
     add_up = lambda part: sum_small(part, sizes)
     fast = fast_chain(
-        weights, every_block, inverse, targets, which, where, scale, add_up, labels_all, my_ends, my_vec, my_live, my_source, my_ss, my_st
+        weights, every_block, inverse, targets, which, where, scale, add_up, after_first, blank, labels_all, my_ends, my_vec, my_live, my_source, my_ss, my_st
     )
 
     small, head_part, fast_loss, made = fast
+    general_own, general_shared, general_loss = general_out
     local_sums = pack_first(small.in_grad, small.out_grad, small.mix_grad, head_part)
     local_sums = local_sums + flat_rows(small.env_grad, small.sc_grad)
     summed = lax.psum(local_sums, AX)

time: 618 us -> 612 us (level)
  transfers between devices with their start and end apart: 42 -> 42, of which waited for: 21 -> 21; matrix products, arithmetic and copies ran while one was open for 16% -> 16% of each run, Pallas kernels for 8% -> 9%
where the time goes in v4:
time: 612 us; the launch traced here: 600 us
  Pallas kernels  266 us (43%)
  waiting for transfers between devices  124 us (20%)
  other arithmetic  76.6 us (13%)
  starting transfers between devices  61.9 us (10%)
  local copies, waits for them, and re-layouts  41.3 us (7%)
  between operations  18.7 us (3%)
  loops' own time  8.11 us (1%)
    pallas_call x8, Pallas kernels, kernel_call(): pl.pallas_call(kernel, out_shape=out_leaves, in_specs=in_specs, out_specs...  254 us
    ppermute x40, waiting for transfers between devices, hop(): return lax.ppermute(value, AX, pairs)  85.8 us
    ppermute x40, starting transfers between devices, hop(): return lax.ppermute(value, AX, pairs)  61.8 us
    psum x1, waiting for transfers between devices, local(): summed = lax.psum(local_sums, AX)  19.5 us
    all_gather x1, waiting for transfers between devices, local(): every_block = lax.all_gather(soap_weight, AX, axis=0, tiled=True)  18.3 us
    sub x6, other arithmetic, adamw(): return (weight - 0.01 * (normal + 0.01 * weight), first_new, second_new)  15.7 us
  transfers between devices with their start and end apart: 42, of which 21 were waited for; matrix products, arithmetic and copies ran while one was open for 16% of the time, Pallas kernels for 9%

profile of v4, /device:TPU:0, one launch (start us, length us, event | category | flops | bytes accessed | tf_op | source)
XLA Modules:
  0.0 600.4 jit_solution(702343794904964744)
XLA Ops:
  12.1 3.0 collective-permute-start.33
  16.7 5.4 copy.249
  40.0 3.1 fusion.927
  50.9 4.6 collective-permute-done.36
  55.4 4.7 collective-permute-done.37
  70.2 5.4 copy.245
  76.6 4.2 convert_reduce_fusion
  80.8 4.6 gather_fusion.3
  100.1 14.2 %shard_map.591 = (f32[64,512]{1,0:T(8,128)}, f32[8,128,128]{2,1,0:T(8,128)}, f32[32,1024]{1,0:T(8,128)}, f32[1024,1024]{1,0:T(8,128)}, f32[128,1024]{1,0:T(8,128...) custom-call(bf16[64,1024]{1,0:T(8,128)(2,1)} %get-tuple-element.1013, ...), custom_call_target="tpu_custom_call" | custom-call | flops 3221225472 | bytes 21905408 | tf_op jit(solution)/shard_map/pallas_call | solution.py:613
  114.3 18.3 %all-gather.2.cloned.1.call-done.refs_2_ = f32[256,128,128]{2,1,0:T(8,128)} async-done(((f32[8,128,128]{2,1,0:T(8,128)}), f32[256,128,128]{2,1,0:T(8,128)}) %all-gather.2.cloned.1.call-update) | async-done | bytes 16777232 | tf_op jit(solution)/shard_map/all_gather | solution.py:2171
  132.6 8.1 %while.24 = (pred[]{:T(512)}, f32[8,128,128]{2,1,0:T(8,128)}, f32[32,1024]{1,0:T(8,128)}, f32[1024,1024]{1,0:T(8,128)}, f32[128,1024]{1,0:T(8,128)}, /*index=5*/...) while((pred[]{:T(512)}, f32[8,128,128]{2,1,0:T(8,128)}, ...), condition=%region_51.52_spmd.clone.clone, body=%region_13.51_spmd.clone.clone | while | flops 97740455936 | bytes 1994839040 | solution.py:2237
  140.7 22.7 %shard_map.592 = (f32[1024,1024]{1,0:T(8,128)}, f32[1024,1]{1,0:T(8,128)}, bf16[3,1024,1024]{2,1,0:T(8,128)(2,1)}, bf16[3,1024,1024]{2,1,0:T(8,128)(2,1)}, bf16[...) custom-call(f32[1,1024]{1,0:T(1,128)} %bitcast.2042, s32[256]{0:T(256)} %select_reduce_fusion.refs_1_, ...), custom_call_target="tpu_custom_call" | custom-call | bytes 46146560 | tf_op jit(solution)/shard_map/pallas_call | solution.py:613
  163.4 27.6 %shard_map.593 = (f32[8,512]{1,0:T(8,128)}, f32[64,512]{1,0:T(8,128)}, f32[64,512]{1,0:T(8,128)}, bf16[1024,512]{1,0:T(8,128)(2,1)}, bf16[1024,512]{1,0:T(8,128)...) custom-call(bf16[64,1024]{1,0:T(8,128)(2,1)} %get-tuple-element.1012, ...), custom_call_target="tpu_custom_call" | custom-call | flops 9663676416 | bytes 36020224 | tf_op jit(solution)/shard_map/pallas_call | solution.py:613
  191.1 40.9 %shard_map.594 = (f32[16,512]{1,0:T(8,128)}, f32[8,512]{1,0:T(8,128)}, f32[64,512]{1,0:T(8,128)}, f32[16,512]{1,0:T(8,128)}, f32[64,512]{1,0:T(8,128)}, /*index=...) custom-call(f32[16,512]{1,0:T(8,128)} %pad.101.refs_0_, ...), custom_call_target="tpu_custom_call" | custom-call | flops 12884901888 | bytes 56791040 | tf_op jit(solution)/shard_map/pallas_call | solution.py:613
  249.0 45.4 %shard_map.595 = (f32[16,512]{1,0:T(8,128)}, f32[8,512]{1,0:T(8,128)}, f32[1024,128]{1,0:T(8,128)}, f32[1024,128]{1,0:T(8,128)}, f32[1,512]{1,0:T(1,128)}, /*ind...) custom-call(f32[16,512]{1,0:T(8,128)} %pad.101.refs_0_, ...), custom_call_target="tpu_custom_call" | custom-call | flops 12884901888 | bytes 57878528 | tf_op jit(solution)/shard_map/pallas_call | solution.py:613
  296.7 45.0 %shard_map.596 = (f32[64,512]{1,0:T(8,128)}, f32[64,512]{1,0:T(8,128)}, f32[576,512]{1,0:T(8,128)}, bf16[1024,512]{1,0:T(8,128)(2,1)}, bf16[1024,512]{1,0:T(8,12...) custom-call(bf16[1024,64]{1,0:T(8,128)(2,1)} %get-tuple-element.1003, ...), custom_call_target="tpu_custom_call" | custom-call | flops 12884901888 | bytes 59641856 | tf_op jit(solution)/shard_map/pallas_call | solution.py:613
  341.8 32.0 %shard_map.597 = (f32[32,128,128]{2,1,0:T(8,128)}, f32[32,128,128]{2,1,0:T(8,128)}, f32[32,128,128]{2,1,0:T(8,128)}, f32[32,128,128]{2,1,0:T(8,128)}, f32[32,128...) custom-call(f32[1,1024]{1,0:T(1,128)} %bitcast.2043, ...), custom_call_target="tpu_custom_call" | custom-call | flops 19327352832 | bytes 41953280 | tf_op jit(solution)/shard_map/pallas_call | solution.py:613
  374.9 26.1 %shard_map.598 = (f32[2,64,1024]{2,1,0:T(8,128)}, f32[16,1024]{1,0:T(8,128)}, f32[3,64,64]{2,1,0:T(8,128)}, f32[2,64,1024]{2,1,0:T(8,128)}, f32[1024,1024]{1,0:T(8,128)}) custom-call(f32[16,512]{1,0:T(8,128)} %get-tuple-element.385.refs_0_, f32[16,512]{1,0:T(8,128)} %pad_maximum_fusion.20.refs_2_.refs_1_, bf16[1024,512]{1,0:T(8,128)(2,1)} %get-tuple-element.423.refs_2_, ...), custom_call_target="tpu_custom_call" | custom-call | flops 6442450944 | bytes 40288256 | tf_op jit(solution)/shard_map/pallas_call | solution.py:613
  424.0 7.2 %collective-permute-done.49 = f32[2,4,128,128]{3,2,1,0:T(8,128)} collective-permute-done((f32[2,4,128,128]{3,2,1,0:T(8,128)}, f32[2,4,128,128]{3,2,1,0:T(8,128)}, u32[]{:S(2)}, u32[]{:S(2)}) %collective-permute-start.49) | collective-permute-done | bytes 524320 | tf_op jit(solution)/shard_map/ppermute | solution.py:140
  431.2 4.5 collective-permute-done.50
  440.1 8.4 %collective-permute-done.57 = f32[2,4,128,128]{3,2,1,0:T(8,128)S(1)} collective-permute-done((f32[2,4,128,128]{3,2,1,0:T(8,128)S(1)}, f32[2,4,128,128]{3,2,1,0:T(8,128)S(1)}, u32[]{:S(2)}, u32[]{:S(2)}) %collective-permute-start.57) | collective-permute-done | bytes 524320 | tf_op jit(solution)/shard_map/ppermute | solution.py:140
  453.1 3.4 collective-permute-done.64
  457.1 12.0 %collective-permute-done.65 = f32[4,128,128]{2,1,0:T(8,128)S(1)} collective-permute-done((f32[4,128,128]{2,1,0:T(8,128)S(1)}, f32[4,128,128]{2,1,0:T(8,128)S(1)}, u32[]{:S(2)}, u32[]{:S(2)}) %collective-permute-start.65) | collective-permute-done | bytes 262176 | tf_op jit(solution)/shard_map/ppermute | solution.py:140
  471.1 3.6 collective-permute-done.69
  478.6 7.5 %collective-permute-done.59 = f32[2,4,128,128]{3,2,1,0:T(8,128)S(1)} collective-permute-done((f32[2,4,128,128]{3,2,1,0:T(8,128)S(1)}, f32[2,4,128,128]{3,2,1,0:T(8,128)S(1)}, u32[]{:S(2)}, u32[]{:S(2)}) %collective-permute-start.59) | collective-permute-done | bytes 524320 | tf_op jit(solution)/shard_map/ppermute | solution.py:140
  491.5 8.8 %collective-permute-done.70 = f32[8,128,128]{2,1,0:T(8,128)S(1)} collective-permute-done((f32[8,128,128]{2,1,0:T(8,128)S(1)}, f32[8,128,128]{2,1,0:T(8,128)S(1)}, u32[]{:S(2)}, u32[]{:S(2)}) %collective-permute-start.70) | collective-permute-done | bytes 524320 | tf_op jit(solution)/shard_map/ppermute | solution.py:140
  503.0 22.5 %collective-permute-start.63 = (f32[8,128,128]{2,1,0:T(8,128)}, f32[8,128,128]{2,1,0:T(8,128)}, u32[]{:S(2)}, u32[]{:S(2)}) collective-permute-start(f32[8,128,128]{2,1,0:T(8,128)} %get-tuple-element.982), channel_id=1, source_target_pairs={{0,2},{1,3},{8,10},{9,11},{16,18},{17,19},{24,26},{25,27},{6,4},{7... | collective-permute-start | bytes 1572872 | tf_op jit(solution)/shard_map/ppermute | solution.py:140
  530.2 4.0 collective-permute-done.54
  536.6 4.3 collective-permute-done.72
  542.5 11.8 %shard_map.599 = (f32[8,128,128]{2,1,0:T(8,128)}, f32[8,128,128]{2,1,0:T(8,128)}, f32[8,128,128]{2,1,0:T(8,128)}, f32[8,128,128]{2,1,0:T(8,128)}, f32[8,128,128]...) custom-call(f32[8,128,128]{2,1,0:T(8,128)S(1)} %fusion.957.refs_0_, ...), custom_call_target="tpu_custom_call" | custom-call | tf_op jit(solution)/shard_map/pallas_call | solution.py:1630
  554.3 19.5 %all-reduce.39.cloned.1.call-done = (f32[32,1024]{1,0:T(8,128)}, f32[1024,1024]{1,0:T(8,128)}, f32[128,1024]{1,0:T(8,128)}, f32[128,1024]{1,0:T(8,128)}) async-done(((f32[32,1024]{1,0:T(8,128)}, f32[1024,1024]{1,0:T(8,128)}, f32[128,1024]{1,0:T(8,128)}, f32[128,1024]{1,0:T(8,128)}), (f32[32,1024]{1,0:T(8,128)}, f32[1024,1024]{1,0:T(8,128)}, f32[128,1024]{1,0:T(8,128)}, ...) | async-done | bytes 5373968 | tf_op jit(solution)/shard_map/psum | solution.py:2256
  583.1 9.1 %multiply_subtract_fusion.1 = (f32[1024,1024]{1,0:T(8,128)}, f32[1024,1024]{1,0:T(8,128)}, f32[1024,1024]{1,0:T(8,128)}) fusion(f32[1024,1024]{1,0:T(8,128)S(1)} %copy-done.73, f32[1024,1024]{1,0:T(8,128)} %get-tuple-element.484, f32[1024,1024]{1,0:T(8,128)} %get-tuple-element.1244, pred[]{:T(512)S(6)} %le.37, f32[1024,1024]{1,0:T(8,128)S(1)} %copy-done.196, ...), kind=kLoop, calls=%fused_computation.1245 | loop fusion | flops 16777216 | bytes 33554432 | tf_op jit(solution)/shard_map/sub | solution.py:1648
  (345 shorter events, 139.8 us)
Async XLA Ops:
  7.2 125.3 %all-gather.2.cloned.1.call-start = ((), (), s32[]{:S(2)}) async-start(), calls=%async_computation | async-start | bytes 17301504 | tf_op jit(solution)/shard_map/all_gather | solution.py:2171
  12.1 34.0 %collective-permute-start.33 = (f32[7,512]{1,0:T(8,128)S(1)}, f32[7,512]{1,0:T(8,128)S(1)}, u32[]{:S(2)}, u32[]{:S(2)}) collective-permute-start(f32[7,512]{1,0:T(8,128)S(1)} %concatenate.92), channel_id=1, source_target_pairs={{0,8},{1,9},{2,10},{3,11},{4,12},{5,13},{6,14},{7,15},{8,0},{9,1},... | collective-permute-start | bytes 43016 | tf_op jit(solution)/shard_map/ppermute | solution.py:140
  15.1 31.0 %collective-permute-start.34 = (f32[7,512]{1,0:T(8,128)S(1)}, f32[7,512]{1,0:T(8,128)S(1)}, u32[]{:S(2)}, u32[]{:S(2)}) collective-permute-start(f32[7,512]{1,0:T(8,128)S(1)} %concatenate.92), channel_id=1, source_target_pairs={{0,16},{1,17},{2,18},{3,19},{4,20},{5,21},{6,22},{7,23},{8,24},{9,... | collective-permute-start | bytes 43016 | tf_op jit(solution)/shard_map/ppermute | solution.py:140
  16.7 29.5 %collective-permute-start.35 = (f32[7,512]{1,0:T(8,128)S(1)}, f32[7,512]{1,0:T(8,128)S(1)}, u32[]{:S(2)}, u32[]{:S(2)}) collective-permute-start(f32[7,512]{1,0:T(8,128)S(1)} %concatenate.92), channel_id=1, source_target_pairs={{0,24},{1,25},{2,26},{3,27},{4,28},{5,29},{6,30},{7,31},{8,16},{9,... | collective-permute-start | bytes 43016 | tf_op jit(solution)/shard_map/ppermute | solution.py:140
  46.2 9.3 %collective-permute-start.36 = (f32[4,7,512]{2,1,0:T(8,128)S(1)}, f32[4,7,512]{2,1,0:T(8,128)S(1)}, u32[]{:S(2)}, u32[]{:S(2)}) collective-permute-start(f32[4,7,512]{2,1,0:T(8,128)S(1)} %get-tuple-element.1028), channel_id=1, source_target_pairs={{0,2},{1,3},{8,10},{9,11},{16,18},{17,19},{24,26},{25,27},{2,0},{3... | collective-permute-start | bytes 172040 | tf_op jit(solution)/shard_map/ppermute | solution.py:140
  48.3 11.8 %collective-permute-start.37 = (f32[4,7,512]{2,1,0:T(8,128)S(1)}, f32[4,7,512]{2,1,0:T(8,128)S(1)}, u32[]{:S(2)}, u32[]{:S(2)}) collective-permute-start(f32[4,7,512]{2,1,0:T(8,128)S(1)} %get-tuple-element.1028), channel_id=1, source_target_pairs={{0,4},{1,5},{8,12},{9,13},{16,20},{17,21},{24,28},{25,29},{2,6},{3... | collective-permute-start | bytes 172040 | tf_op jit(solution)/shard_map/ppermute | solution.py:140
  50.9 9.3 %collective-permute-start.38 = (f32[4,7,512]{2,1,0:T(8,128)S(1)}, f32[4,7,512]{2,1,0:T(8,128)S(1)}, u32[]{:S(2)}, u32[]{:S(2)}) collective-permute-start(f32[4,7,512]{2,1,0:T(8,128)S(1)} %get-tuple-element.1028), channel_id=1, source_target_pairs={{0,6},{1,7},{8,14},{9,15},{16,22},{17,23},{24,30},{25,31},{2,4},{3... | collective-permute-start | bytes 172040 | tf_op jit(solution)/shard_map/ppermute | solution.py:140
  140.7 433.1 %all-reduce.39.cloned.1.call-start = ((), (), s32[]{:S(2)}) async-start(), calls=%async_computation.1 | async-start | bytes 10747904 | tf_op jit(solution)/shard_map/psum | solution.py:2256
  373.8 33.0 %collective-permute-start.48 = (f32[32,128,128]{2,1,0:T(8,128)}, f32[32,128,128]{2,1,0:T(8,128)S(1)}, u32[]{:S(2)}, u32[]{:S(2)}) collective-permute-start(f32[32,128,128]{2,1,0:T(8,128)} %get-tuple-element.459), channel_id=1, source_target_pairs={{0,1},{1,0},{2,3},{3,2},{4,5},{5,4},{6,7},{7,6},{8,9},{9,8},{10,11... | collective-permute-start | bytes 6291464 | tf_op jit(solution)/shard_map/ppermute | solution.py:140
  373.8 45.0 %collective-permute-start.47 = (f32[32,128,128]{2,1,0:T(8,128)}, f32[32,128,128]{2,1,0:T(8,128)}, u32[]{:S(2)}, u32[]{:S(2)}) collective-permute-start(f32[32,128,128]{2,1,0:T(8,128)} %get-tuple-element.457), channel_id=1, source_target_pairs={{0,1},{1,0},{2,3},{3,2},{4,5},{5,4},{6,7},{7,6},{8,9},{9,8},{10,11... | collective-permute-start | bytes 6291464 | tf_op jit(solution)/shard_map/ppermute | solution.py:140
  374.3 40.6 %collective-permute-start.56 = (f32[32,128,128]{2,1,0:T(8,128)}, f32[32,128,128]{2,1,0:T(8,128)}, u32[]{:S(2)}, u32[]{:S(2)}) collective-permute-start(f32[32,128,128]{2,1,0:T(8,128)} %get-tuple-element.463), channel_id=1, source_target_pairs={{0,1},{1,0},{2,3},{3,2},{4,5},{5,4},{6,7},{7,6},{8,9},{9,8},{10,11... | collective-permute-start | bytes 6291464 | tf_op jit(solution)/shard_map/ppermute | solution.py:140
  374.4 47.6 %collective-permute-start.55 = (f32[32,128,128]{2,1,0:T(8,128)}, f32[32,128,128]{2,1,0:T(8,128)}, u32[]{:S(2)}, u32[]{:S(2)}) collective-permute-start(f32[32,128,128]{2,1,0:T(8,128)} %get-tuple-element.462), channel_id=1, source_target_pairs={{0,1},{1,0},{2,3},{3,2},{4,5},{5,4},{6,7},{7,6},{8,9},{9,8},{10,11... | collective-permute-start | bytes 6291464 | tf_op jit(solution)/shard_map/ppermute | solution.py:140
  411.4 19.8 %collective-permute-start.49 = (f32[2,4,128,128]{3,2,1,0:T(8,128)}, f32[2,4,128,128]{3,2,1,0:T(8,128)}, u32[]{:S(2)}, u32[]{:S(2)}) collective-permute-start(f32[2,4,128,128]{3,2,1,0:T(8,128)} %slice_bitcast_fusion.116), channel_id=1, source_target_pairs={{0,8},{1,9},{2,10},{3,11},{4,12},{5,13},{6,14},{7,15},{8,0},{9,1},... | collective-permute-start | bytes 1572872 | tf_op jit(solution)/shard_map/ppermute | solution.py:140
  413.7 22.0 %collective-permute-start.50 = (f32[2,4,128,128]{3,2,1,0:T(8,128)}, f32[2,4,128,128]{3,2,1,0:T(8,128)}, u32[]{:S(2)}, u32[]{:S(2)}) collective-permute-start(f32[2,4,128,128]{3,2,1,0:T(8,128)} %slice_bitcast_fusion.114), channel_id=1, source_target_pairs={{0,16},{1,17},{2,18},{3,19},{4,20},{5,21},{6,22},{7,23},{8,24},{9,... | collective-permute-start | bytes 1572872 | tf_op jit(solution)/shard_map/ppermute | solution.py:140
  417.5 31.0 %collective-permute-start.57 = (f32[2,4,128,128]{3,2,1,0:T(8,128)S(1)}, f32[2,4,128,128]{3,2,1,0:T(8,128)S(1)}, u32[]{:S(2)}, u32[]{:S(2)}) collective-permute-start(f32[2,4,128,128]{3,2,1,0:T(8,128)S(1)} %slice_bitcast_fusion.110), channel_id=1, source_target_pairs={{0,8},{1,9},{2,10},{3,11},{4,12},{5,13},{6,14},{7,15},{8,0},{9,1},... | collective-permute-start | bytes 1572872 | tf_op jit(solution)/shard_map/ppermute | solution.py:140
  418.9 32.0 %collective-permute-start.58 = (f32[2,4,128,128]{3,2,1,0:T(8,128)S(1)}, f32[2,4,128,128]{3,2,1,0:T(8,128)S(1)}, u32[]{:S(2)}, u32[]{:S(2)}) collective-permute-start(f32[2,4,128,128]{3,2,1,0:T(8,128)S(1)} %slice_bitcast_fusion.108), channel_id=1, source_target_pairs={{0,16},{1,17},{2,18},{3,19},{4,20},{5,21},{6,22},{7,23},{8,24},{9,... | collective-permute-start | bytes 1572872 | tf_op jit(solution)/shard_map/ppermute | solution.py:140
  437.2 39.2 %collective-permute-start.51 = (f32[2,4,128,128]{3,2,1,0:T(8,128)S(1)}, f32[2,4,128,128]{3,2,1,0:T(8,128)S(1)}, u32[]{:S(2)}, u32[]{:S(2)}) collective-permute-start(f32[2,4,128,128]{3,2,1,0:T(8,128)S(1)} %slice_bitcast_fusion.119), channel_id=1, source_target_pairs={{0,8},{1,9},{2,10},{3,11},{4,12},{5,13},{6,14},{7,15},{8,0},{9,1},... | collective-permute-start | bytes 1572872 | tf_op jit(solution)/shard_map/ppermute | solution.py:140
  437.3 19.2 %collective-permute-start.64 = (f32[4,128,128]{2,1,0:T(8,128)S(1)}, f32[4,128,128]{2,1,0:T(8,128)S(1)}, u32[]{:S(2)}, u32[]{:S(2)}) collective-permute-start(f32[4,128,128]{2,1,0:T(8,128)S(1)} %get-tuple-element.466), channel_id=1, source_target_pairs={{0,16},{1,17},{2,18},{3,19},{4,20},{5,21},{6,22},{7,23},{8,24},{9,... | collective-permute-start | bytes 786440 | tf_op jit(solution)/shard_map/ppermute | solution.py:140
  438.8 30.2 %collective-permute-start.65 = (f32[4,128,128]{2,1,0:T(8,128)S(1)}, f32[4,128,128]{2,1,0:T(8,128)S(1)}, u32[]{:S(2)}, u32[]{:S(2)}) collective-permute-start(f32[4,128,128]{2,1,0:T(8,128)S(1)} %get-tuple-element.468), channel_id=1, source_target_pairs={{0,8},{1,9},{2,10},{3,11},{4,12},{5,13},{6,14},{7,15},{8,0},{9,1},... | collective-permute-start | bytes 786440 | tf_op jit(solution)/shard_map/ppermute | solution.py:140
  451.1 19.3 %collective-permute-start.68 = (f32[4,128,128]{2,1,0:T(8,128)S(1)}, f32[4,128,128]{2,1,0:T(8,128)S(1)}, u32[]{:S(2)}, u32[]{:S(2)}) collective-permute-start(f32[4,128,128]{2,1,0:T(8,128)S(1)} %get-tuple-element.470), channel_id=1, source_target_pairs={{0,16},{1,17},{2,18},{3,19},{4,20},{5,21},{6,22},{7,23},{8,24},{9,... | collective-permute-start | bytes 786440 | tf_op jit(solution)/shard_map/ppermute | solution.py:140
  451.7 23.0 %collective-permute-start.69 = (f32[4,128,128]{2,1,0:T(8,128)S(1)}, f32[4,128,128]{2,1,0:T(8,128)S(1)}, u32[]{:S(2)}, u32[]{:S(2)}) collective-permute-start(f32[4,128,128]{2,1,0:T(8,128)S(1)} %get-tuple-element.472), channel_id=1, source_target_pairs={{0,8},{1,9},{2,10},{3,11},{4,12},{5,13},{6,14},{7,15},{8,0},{9,1},... | collective-permute-start | bytes 786440 | tf_op jit(solution)/shard_map/ppermute | solution.py:140
  456.5 33.8 %collective-permute-start.53 = (f32[2,4,128,128]{3,2,1,0:T(8,128)S(1)}, f32[2,4,128,128]{3,2,1,0:T(8,128)S(1)}, u32[]{:S(2)}, u32[]{:S(2)}) collective-permute-start(f32[2,4,128,128]{3,2,1,0:T(8,128)S(1)} %slice_bitcast_fusion.112), channel_id=1, source_target_pairs={{0,16},{1,17},{2,18},{3,19},{4,20},{5,21},{6,22},{7,23},{8,24},{9,... | collective-permute-start | bytes 1572872 | tf_op jit(solution)/shard_map/ppermute | solution.py:140
  469.1 17.0 %collective-permute-start.59 = (f32[2,4,128,128]{3,2,1,0:T(8,128)S(1)}, f32[2,4,128,128]{3,2,1,0:T(8,128)S(1)}, u32[]{:S(2)}, u32[]{:S(2)}) collective-permute-start(f32[2,4,128,128]{3,2,1,0:T(8,128)S(1)} %slice_bitcast_fusion.118), channel_id=1, source_target_pairs={{0,8},{1,9},{2,10},{3,11},{4,12},{5,13},{6,14},{7,15},{8,0},{9,1},... | collective-permute-start | bytes 1572872 | tf_op jit(solution)/shard_map/ppermute | solution.py:140
  470.4 19.8 %collective-permute-start.61 = (f32[2,4,128,128]{3,2,1,0:T(8,128)S(1)}, f32[2,4,128,128]{3,2,1,0:T(8,128)S(1)}, u32[]{:S(2)}, u32[]{:S(2)}) collective-permute-start(f32[2,4,128,128]{3,2,1,0:T(8,128)S(1)} %slice_bitcast_fusion.106), channel_id=1, source_target_pairs={{0,16},{1,17},{2,18},{3,19},{4,20},{5,21},{6,22},{7,23},{8,24},{9,... | collective-permute-start | bytes 1572872 | tf_op jit(solution)/shard_map/ppermute | solution.py:140
  474.7 26.3 %collective-permute-start.66 = (f32[8,128,128]{2,1,0:T(8,128)S(1)}, f32[8,128,128]{2,1,0:T(8,128)S(1)}, u32[]{:S(2)}, u32[]{:S(2)}) collective-permute-start(f32[8,128,128]{2,1,0:T(8,128)S(1)} %pad_maximum_fusion.15), channel_id=1, source_target_pairs={{0,2},{1,3},{8,10},{9,11},{16,18},{17,19},{24,26},{25,27},{6,4},{7... | collective-permute-start | bytes 1572872 | tf_op jit(solution)/shard_map/ppermute | solution.py:140
  476.5 23.8 %collective-permute-start.70 = (f32[8,128,128]{2,1,0:T(8,128)S(1)}, f32[8,128,128]{2,1,0:T(8,128)S(1)}, u32[]{:S(2)}, u32[]{:S(2)}) collective-permute-start(f32[8,128,128]{2,1,0:T(8,128)S(1)} %pad_maximum_fusion.16), channel_id=1, source_target_pairs={{0,2},{1,3},{8,10},{9,11},{16,18},{17,19},{24,26},{25,27},{6,4},{7... | collective-permute-start | bytes 1572872 | tf_op jit(solution)/shard_map/ppermute | solution.py:140
  486.1 43.9 %collective-permute-start.52 = (f32[4,128,128]{2,1,0:T(8,128)}, f32[4,128,128]{2,1,0:T(8,128)S(1)}, u32[]{:S(2)}, u32[]{:S(2)}) collective-permute-start(f32[4,128,128]{2,1,0:T(8,128)} %slice_bitcast_fusion.130), channel_id=1, source_target_pairs={{0,16},{1,17},{2,18},{3,19},{4,20},{5,21},{6,22},{7,23},{8,24},{9,... | collective-permute-start | bytes 786440 | tf_op jit(solution)/shard_map/ppermute | solution.py:140
  490.2 11.6 %collective-permute-start.60 = (f32[4,128,128]{2,1,0:T(8,128)S(1)}, f32[4,128,128]{2,1,0:T(8,128)S(1)}, u32[]{:S(2)}, u32[]{:S(2)}) collective-permute-start(f32[4,128,128]{2,1,0:T(8,128)S(1)} %slice_bitcast_fusion.122), channel_id=1, source_target_pairs={{0,16},{1,17},{2,18},{3,19},{4,20},{5,21},{6,22},{7,23},{8,24},{9,... | collective-permute-start | bytes 786440 | tf_op jit(solution)/shard_map/ppermute | solution.py:140
  490.3 11.6 %collective-permute-start.62 = (f32[4,128,128]{2,1,0:T(8,128)S(1)}, f32[4,128,128]{2,1,0:T(8,128)S(1)}, u32[]{:S(2)}, u32[]{:S(2)}) collective-permute-start(f32[4,128,128]{2,1,0:T(8,128)S(1)} %slice_bitcast_fusion.120), channel_id=1, source_target_pairs={{0,8},{1,9},{2,10},{3,11},{4,12},{5,13},{6,14},{7,15},{8,0},{9,1},... | collective-permute-start | bytes 786440 | tf_op jit(solution)/shard_map/ppermute | solution.py:140
  501.1 34.0 %collective-permute-start.67 = (f32[8,128,128]{2,1,0:T(8,128)S(1)}, f32[8,128,128]{2,1,0:T(8,128)S(1)}, u32[]{:S(2)}, u32[]{:S(2)}) collective-permute-start(f32[8,128,128]{2,1,0:T(8,128)S(1)} %fusion.994), channel_id=1, source_target_pairs={{2,4},{3,5},{10,12},{11,13},{18,20},{19,21},{26,28},{27,29},{4,2},... | collective-permute-start | bytes 1572872 | tf_op jit(solution)/shard_map/ppermute | solution.py:140
  503.0 33.6 %collective-permute-start.63 = (f32[8,128,128]{2,1,0:T(8,128)}, f32[8,128,128]{2,1,0:T(8,128)}, u32[]{:S(2)}, u32[]{:S(2)}) collective-permute-start(f32[8,128,128]{2,1,0:T(8,128)} %get-tuple-element.982), channel_id=1, source_target_pairs={{0,2},{1,3},{8,10},{9,11},{16,18},{17,19},{24,26},{25,27},{6,4},{7... | collective-permute-start | bytes 1572872 | tf_op jit(solution)/shard_map/ppermute | solution.py:140
  525.5 15.5 %collective-permute-start.72 = (f32[8,128,128]{2,1,0:T(8,128)}, f32[8,128,128]{2,1,0:T(8,128)}, u32[]{:S(2)}, u32[]{:S(2)}) collective-permute-start(f32[8,128,128]{2,1,0:T(8,128)} %get-tuple-element.983), channel_id=1, source_target_pairs={{2,0},{3,1},{10,8},{11,9},{18,16},{19,17},{26,24},{27,25},{4,6},{5... | collective-permute-start | bytes 1572872 | tf_op jit(solution)/shard_map/ppermute | solution.py:140
  (56 other events, 592.1 us)
Sparse Core Ops, SparseCore 0:
  11.0 121.4 all-gather.1
  415.1 158.6 all-reduce.38
